TPU v7x, 32 devices: a whole 2x2x4 slice. The times are simulated.
32 devices in a mesh: dom: 8 (over y, x, core), blk: 4 (over z).
Axes of the slice: x: 2, y: 2, z: 4, core: 2. Of those that a mesh axis runs over, the one named last changes fastest.
Arguments:
- positions: float32 [3, 65536], P(None, ('dom', 'blk')), may hold values from -0.5 to 0.5
- strength: float32 [3, 65536], P(None, ('dom', 'blk')), may hold values from -0.18 to 0.18
- core_radius: float32 [65536], P(('dom', 'blk')), may hold values from 0.15 to 0.3
- dye_amount: float32 [65536], P(('dom', 'blk')), may hold values from -0.18 to 0.18
- cell_fraction: float32 [3, 65536], P(None, ('dom', 'blk')), may hold values from 0 to 1
- cell_index: int32 [65536], P(('dom', 'blk')), may hold values from 0 to 127
- tile_local: int32 [65536], P(('dom', 'blk')), may hold values from 0 to 15
- owner_dom: int32 [65536, 1], P(('dom', 'blk')), may hold values from 0 to 7; in each aligned block of 2048 rows (0 to 2047, 2048 to 4095, ...) at most 1280 rows name the same one
Outputs:
- velocity: float32 [3, 65536], P(None, ('dom', 'blk'))
- tile_grid: float32 [512, 4, 128], P(('dom', 'blk'))
Inputs may be any that keep to these rules, and one draw needn't show every extreme that they name: `owner_dom`: in every block of 2048 rows of one device no value appears more than 1280 times, and in some block a value appears exactly 1280 times.
All inputs are finite; a program needn't handle non-finite values.
Results may differ from a plain program's by a relative error of at most 0.0003.
Values sent between devices are 32-bit elements; how exact they have to be, the bound alone decides.
No kernel may reach another device: no remote copies, remote signals or barrier semaphores. Data moves between devices by JAX's collectives and lax.ppermute only.
A program may use at most 64 MiB of HBM per device.

v0:
```python
import math

import jax
import jax.numpy as jnp
from jax import lax
from jax.sharding import PartitionSpec as P

time_step = 0.02
move_scale = 2.0
inverse_volume = 32.0
kernel_scale = 1.0 / (4.0 * math.pi)
highest = lax.Precision.HIGHEST


def cross_product(left_vec, right_vec):
    return jnp.stack(
        [
            left_vec[1] * right_vec[2] - left_vec[2] * right_vec[1],
            left_vec[2] * right_vec[0] - left_vec[0] * right_vec[2],
            left_vec[0] * right_vec[1] - left_vec[1] * right_vec[0],
        ]
    )


def pair_sums(partial_value, source_block, target_rows):
    points = source_block[0:3]
    vortex = source_block[3:6]
    radius = source_block[6]
    source_rows = jnp.concatenate(
        [
            -2.0 * points,
            (jnp.sum(points * points, axis=0) + radius * radius)[None],
            jnp.ones_like(radius)[None],
        ],
        axis=0,
    )
    square = lax.dot_general(
        source_rows,
        target_rows,
        (((0,), (0,)), ((), ())),
        precision=highest,
        preferred_element_type=jnp.float32,
    )
    inverse = lax.rsqrt(square)
    kernel_vals = kernel_scale * inverse * inverse * inverse
    slope_vals = -3.0 * kernel_vals * inverse * inverse
    crossed = cross_product(vortex, points)
    moment_one = (points[:, None, :] * vortex[None, :, :]).reshape(9, -1)
    moment_two = (points[:, None, :] * crossed[None, :, :]).reshape(9, -1)
    first_rows = jnp.concatenate([vortex, crossed], axis=0)
    second_rows = jnp.concatenate([vortex, crossed, moment_one, moment_two], axis=0)
    first = partial_value[0] + jnp.dot(
        first_rows, kernel_vals, precision=highest, preferred_element_type=jnp.float32
    )
    second = partial_value[1] + jnp.dot(
        second_rows, slope_vals, precision=highest, preferred_element_type=jnp.float32
    )
    return (first, second)


def block_fold(running, sources, target_rows):
    overall = sources.shape[1]
    block_width = math.gcd(overall, 1024)
    blocks = sources.reshape(7, overall // block_width, block_width).transpose(1, 0, 2)

    def scan_step(partial_value, source_block):
        return (pair_sums(partial_value, source_block, target_rows), None)

    result, ignored = lax.scan(scan_step, running, blocks)
    return result


def combine(points, vortex, first, second):
    sum_kernel = first[0:3]
    velocity = cross_product(sum_kernel, points) - first[3:6]
    term_one = cross_product(sum_kernel, vortex)
    moment_one = second[6:15].reshape(3, 3, -1)
    moment_two = second[15:24].reshape(3, 3, -1)
    dot_self = jnp.sum(vortex * points, axis=0)
    mixed_one = jnp.sum(vortex[:, None, :] * moment_one, axis=0)
    mixed_two = jnp.sum(vortex[:, None, :] * moment_two, axis=0)
    term_two = (
        dot_self * (cross_product(second[0:3], points) - second[3:6])
        - cross_product(mixed_one, points)
        + mixed_two
    )
    return (velocity, term_one + term_two)


def spline_weight(distance):
    return jnp.where(
        distance < 1.0,
        1.0 - 2.5 * distance * distance + 1.5 * distance * distance * distance,
        0.5 * (2.0 - distance) * (2.0 - distance) * (1.0 - distance),
    )


def grid_place(cell_fraction, cell_index, velocity):
    cell_start = jnp.stack([cell_index % 8, cell_index // 8 % 4, cell_index // 32]).astype(
        jnp.float32
    )
    coords = cell_start + cell_fraction + move_scale * velocity
    lowest = jnp.floor(coords)
    fraction = coords - lowest
    lowest_int = lowest.astype(jnp.int32)
    base_code = lowest_int[2] % 4 * 32 + lowest_int[1] % 4 * 8 + lowest_int[0] % 8
    return (fraction, base_code)


def node_weights(fraction):
    per_axis = [
        [
            spline_weight(fraction[axis_id] + 1.0),
            spline_weight(fraction[axis_id]),
            spline_weight(1.0 - fraction[axis_id]),
            spline_weight(2.0 - fraction[axis_id]),
        ]
        for axis_id in range(3)
    ]
    weights = []
    for along_z in range(4):
        for along_y in range(4):
            for along_x in range(4):
                weights.append(per_axis[2][along_z] * per_axis[1][along_y] * per_axis[0][along_x])
    return jnp.stack(weights)


def cells_of(base_code):
    base_x = base_code % 8
    base_y = base_code // 8 % 4
    base_z = base_code // 32
    stencil_cells = []
    for along_z in range(4):
        for along_y in range(4):
            for along_x in range(4):
                stencil_cells.append(
                    (base_z + along_z - 1) % 4 * 32
                    + (base_y + along_y - 1) % 4 * 8
                    + (base_x + along_x - 1) % 8
                )
    return jnp.stack(stencil_cells)


def spread(weights, stencil_cells):
    cell_ids = jnp.arange(128, dtype=jnp.int32)[:, None]
    overall = jnp.zeros((128, weights.shape[1]), jnp.float32)
    for node in range(64):
        overall = overall + jnp.where(
            stencil_cells[node][None, :] == cell_ids, weights[node][None, :], 0.0
        )
    return overall


def on_device(
    positions, strength, core_radius, dye_amount, cell_fraction, cell_index, tile_local, owner_dom
):
    local_count = positions.shape[1]
    tiles_count = local_count // 128
    sources = jnp.concatenate([positions, strength, core_radius[None]], axis=0)
    target_rows = jnp.concatenate(
        [
            positions,
            jnp.ones_like(positions[0])[None],
            jnp.sum(positions * positions, axis=0)[None],
        ],
        axis=0,
    )
    start_sums = (
        jnp.zeros((6, local_count), jnp.float32),
        jnp.zeros((24, local_count), jnp.float32),
    )
    first, second = block_fold(
        start_sums, lax.all_gather(sources, "blk", axis=1, tiled=True), target_rows
    )
    velocity, stretch = combine(positions, strength, first, second)
    new_strength = strength + time_step * stretch
    fraction, base_code = grid_place(cell_fraction, cell_index, velocity)
    values = jnp.concatenate([new_strength, dye_amount[None]], axis=0)
    owner_ids = owner_dom[:, 0]
    spread_w = spread(node_weights(fraction), cells_of(base_code))
    contrib = jnp.einsum("cp,kp->pck", values, spread_w).reshape(local_count, 512)
    group_tile = owner_ids * tiles_count + tile_local
    shifted = group_tile
    shifted = jnp.where(
        (shifted >= 0) & (shifted < tiles_count * lax.axis_size("dom")),
        shifted,
        tiles_count * lax.axis_size("dom"),
    )
    summed = lax.psum_scatter(
        jax.ops.segment_sum(contrib, shifted, num_segments=tiles_count * lax.axis_size("dom")),
        "dom",
        scatter_dimension=0,
        tiled=True,
    )
    tile_grid = (summed * inverse_volume).reshape(tiles_count, 4, 128)
    return (velocity, tile_grid)


def solution(mesh):
    placed = (
        P(None, ("dom", "blk")),
        P(None, ("dom", "blk")),
        P(("dom", "blk")),
        P(("dom", "blk")),
        P(None, ("dom", "blk")),
        P(("dom", "blk")),
        P(("dom", "blk")),
        P(("dom", "blk"), None),
    )
    return jax.shard_map(
        on_device,
        mesh=mesh,
        in_specs=placed,
        out_specs=(P(None, ("dom", "blk")), P(("dom", "blk"), None, None)),
        check_vma=False,
    )
```

profile of v0, /device:TPU:0, one launch (start us, length us, event | category | flops | bytes accessed | tf_op | source)
XLA Modules:
  0.0 340.1 jit_solution(3424060244694692656)
XLA Ops:
  7.2 0.8 multiply_reduce_fusion.3
  8.1 0.8 pad_maximum_fusion.1
  8.9 15.6 %all_gather.3 = f32[7,8192]{1,0:T(8,128)S(1)} all-gather(f32[7,2048]{1,0:T(8,128)S(1)} %pad_maximum_fusion.1), channel_id=1, replica_groups=mesh['dom'=8,'blk'=4] {'blk'}, dimensions={1}, use_global_device_ids=true | all-gather | bytes 286720 | tf_op jit(solution)/shard_map/all_gather | solution.py:173
  25.4 209.1 %while.13 = (s32[]{:T(128)}, f32[6,2048]{1,0:T(8,128)S(1)}, f32[24,2048]{1,0:T(8,128)S(1)}, f32[8,7,1024]{2,1,0:T(8,128)S(1)}, f32[5,2048]{1,0:T(8,128)S(1)}, /*...) while((s32[]{:T(128)}, f32[6,2048]{1,0:T(8,128)S(1)}, ...), condition=%wide.region_3.4_spmd.clone, body=%wide.region_1.3_spmd.clone.sunk | while | flops 899873792 | bytes 26444100 | solution.py:69
  25.6 9.2 %fusion.173 = f32[1024,2048]{1,0:T(8,128)} fusion(f32[5,2048]{1,0:T(8,128)S(1)} %get-tuple-element.467, f32[1,1024]{1,0:T(1,128)S(1)} %fusion.172, f32[3,1024]{1,0:T(4,128)S(1)} %get-tuple-element.429, f32[5]{0:T(128)S(1)} %pad.5.clone.2), kind=kOutput, calls=%fused_computation.19.clone.1 | convolution fusion | flops 125839360 | bytes 8445972 | tf_op jit(solution)/shard_map/while/body/eval_jaxpr/dot_general | solution.py:37
  34.8 7.7 %fusion.174 = f32[6,2048]{1,0:T(8,128)S(1)} fusion(f32[1024,2048]{1,0:T(8,128)} %fusion.173, f32[6,2048]{1,0:T(8,128)S(1)} %get-tuple-element.449, f32[1,1024]{1,0:T(1,128)S(1)} %get-tuple-element.425, f32[1,1024]{1,0:T(1,128)S(1)} %get-tuple-element.426, f32[1,1024]{1,0:T(1,128)S(1)} %get-tuple-element.427, ...), kind=kOutput, calls=%fused_computation.11.clone.1 | convolution fusion | flops 157329408 | bytes 8511489 | tf_op jit(solution)/shard_map/while/body/eval_jaxpr/dot_general | solution.py:52
  42.9 8.6 %fusion.175 = f32[24,2048]{1,0:T(8,128)S(1)} fusion(f32[24,1024]{1,0:T(8,128)S(1)} %concatenate.30, f32[1024,2048]{1,0:T(8,128)} %fusion.173, f32[24,2048]{1,0:T(8,128)S(1)} %get-tuple-element.450, pred[]{:T(512)S(6)} %compare.286), kind=kOutput, calls=%fused_computation.10.clone.1 | convolution fusion | flops 616660992 | bytes 8880129 | tf_op jit(solution)/shard_map/while/body/eval_jaxpr/dot_general | solution.py:55
  51.7 9.2 %fusion.173 = f32[1024,2048]{1,0:T(8,128)} fusion(f32[5,2048]{1,0:T(8,128)S(1)} %get-tuple-element.467, f32[1,1024]{1,0:T(1,128)S(1)} %fusion.172, f32[3,1024]{1,0:T(4,128)S(1)} %get-tuple-element.429, f32[5]{0:T(128)S(1)} %pad.5.clone.2), kind=kOutput, calls=%fused_computation.19.clone.1 | convolution fusion | flops 125839360 | bytes 8445972 | tf_op jit(solution)/shard_map/while/body/eval_jaxpr/dot_general | solution.py:37
  60.9 7.7 %fusion.174 = f32[6,2048]{1,0:T(8,128)S(1)} fusion(f32[1024,2048]{1,0:T(8,128)} %fusion.173, f32[6,2048]{1,0:T(8,128)S(1)} %get-tuple-element.449, f32[1,1024]{1,0:T(1,128)S(1)} %get-tuple-element.425, f32[1,1024]{1,0:T(1,128)S(1)} %get-tuple-element.426, f32[1,1024]{1,0:T(1,128)S(1)} %get-tuple-element.427, ...), kind=kOutput, calls=%fused_computation.11.clone.1 | convolution fusion | flops 157329408 | bytes 8511489 | tf_op jit(solution)/shard_map/while/body/eval_jaxpr/dot_general | solution.py:52
  69.0 8.6 %fusion.175 = f32[24,2048]{1,0:T(8,128)S(1)} fusion(f32[24,1024]{1,0:T(8,128)S(1)} %concatenate.30, f32[1024,2048]{1,0:T(8,128)} %fusion.173, f32[24,2048]{1,0:T(8,128)S(1)} %get-tuple-element.450, pred[]{:T(512)S(6)} %compare.286), kind=kOutput, calls=%fused_computation.10.clone.1 | convolution fusion | flops 616660992 | bytes 8880129 | tf_op jit(solution)/shard_map/while/body/eval_jaxpr/dot_general | solution.py:55
  77.8 9.2 %fusion.173 = f32[1024,2048]{1,0:T(8,128)} fusion(f32[5,2048]{1,0:T(8,128)S(1)} %get-tuple-element.467, f32[1,1024]{1,0:T(1,128)S(1)} %fusion.172, f32[3,1024]{1,0:T(4,128)S(1)} %get-tuple-element.429, f32[5]{0:T(128)S(1)} %pad.5.clone.2), kind=kOutput, calls=%fused_computation.19.clone.1 | convolution fusion | flops 125839360 | bytes 8445972 | tf_op jit(solution)/shard_map/while/body/eval_jaxpr/dot_general | solution.py:37
  87.0 7.7 %fusion.174 = f32[6,2048]{1,0:T(8,128)S(1)} fusion(f32[1024,2048]{1,0:T(8,128)} %fusion.173, f32[6,2048]{1,0:T(8,128)S(1)} %get-tuple-element.449, f32[1,1024]{1,0:T(1,128)S(1)} %get-tuple-element.425, f32[1,1024]{1,0:T(1,128)S(1)} %get-tuple-element.426, f32[1,1024]{1,0:T(1,128)S(1)} %get-tuple-element.427, ...), kind=kOutput, calls=%fused_computation.11.clone.1 | convolution fusion | flops 157329408 | bytes 8511489 | tf_op jit(solution)/shard_map/while/body/eval_jaxpr/dot_general | solution.py:52
  95.1 8.6 %fusion.175 = f32[24,2048]{1,0:T(8,128)S(1)} fusion(f32[24,1024]{1,0:T(8,128)S(1)} %concatenate.30, f32[1024,2048]{1,0:T(8,128)} %fusion.173, f32[24,2048]{1,0:T(8,128)S(1)} %get-tuple-element.450, pred[]{:T(512)S(6)} %compare.286), kind=kOutput, calls=%fused_computation.10.clone.1 | convolution fusion | flops 616660992 | bytes 8880129 | tf_op jit(solution)/shard_map/while/body/eval_jaxpr/dot_general | solution.py:55
  103.9 9.2 %fusion.173 = f32[1024,2048]{1,0:T(8,128)} fusion(f32[5,2048]{1,0:T(8,128)S(1)} %get-tuple-element.467, f32[1,1024]{1,0:T(1,128)S(1)} %fusion.172, f32[3,1024]{1,0:T(4,128)S(1)} %get-tuple-element.429, f32[5]{0:T(128)S(1)} %pad.5.clone.2), kind=kOutput, calls=%fused_computation.19.clone.1 | convolution fusion | flops 125839360 | bytes 8445972 | tf_op jit(solution)/shard_map/while/body/eval_jaxpr/dot_general | solution.py:37
  113.1 7.7 %fusion.174 = f32[6,2048]{1,0:T(8,128)S(1)} fusion(f32[1024,2048]{1,0:T(8,128)} %fusion.173, f32[6,2048]{1,0:T(8,128)S(1)} %get-tuple-element.449, f32[1,1024]{1,0:T(1,128)S(1)} %get-tuple-element.425, f32[1,1024]{1,0:T(1,128)S(1)} %get-tuple-element.426, f32[1,1024]{1,0:T(1,128)S(1)} %get-tuple-element.427, ...), kind=kOutput, calls=%fused_computation.11.clone.1 | convolution fusion | flops 157329408 | bytes 8511489 | tf_op jit(solution)/shard_map/while/body/eval_jaxpr/dot_general | solution.py:52
  121.2 8.6 %fusion.175 = f32[24,2048]{1,0:T(8,128)S(1)} fusion(f32[24,1024]{1,0:T(8,128)S(1)} %concatenate.30, f32[1024,2048]{1,0:T(8,128)} %fusion.173, f32[24,2048]{1,0:T(8,128)S(1)} %get-tuple-element.450, pred[]{:T(512)S(6)} %compare.286), kind=kOutput, calls=%fused_computation.10.clone.1 | convolution fusion | flops 616660992 | bytes 8880129 | tf_op jit(solution)/shard_map/while/body/eval_jaxpr/dot_general | solution.py:55
  130.0 9.2 %fusion.173 = f32[1024,2048]{1,0:T(8,128)} fusion(f32[5,2048]{1,0:T(8,128)S(1)} %get-tuple-element.467, f32[1,1024]{1,0:T(1,128)S(1)} %fusion.172, f32[3,1024]{1,0:T(4,128)S(1)} %get-tuple-element.429, f32[5]{0:T(128)S(1)} %pad.5.clone.2), kind=kOutput, calls=%fused_computation.19.clone.1 | convolution fusion | flops 125839360 | bytes 8445972 | tf_op jit(solution)/shard_map/while/body/eval_jaxpr/dot_general | solution.py:37
  139.2 7.7 %fusion.174 = f32[6,2048]{1,0:T(8,128)S(1)} fusion(f32[1024,2048]{1,0:T(8,128)} %fusion.173, f32[6,2048]{1,0:T(8,128)S(1)} %get-tuple-element.449, f32[1,1024]{1,0:T(1,128)S(1)} %get-tuple-element.425, f32[1,1024]{1,0:T(1,128)S(1)} %get-tuple-element.426, f32[1,1024]{1,0:T(1,128)S(1)} %get-tuple-element.427, ...), kind=kOutput, calls=%fused_computation.11.clone.1 | convolution fusion | flops 157329408 | bytes 8511489 | tf_op jit(solution)/shard_map/while/body/eval_jaxpr/dot_general | solution.py:52
  147.4 8.6 %fusion.175 = f32[24,2048]{1,0:T(8,128)S(1)} fusion(f32[24,1024]{1,0:T(8,128)S(1)} %concatenate.30, f32[1024,2048]{1,0:T(8,128)} %fusion.173, f32[24,2048]{1,0:T(8,128)S(1)} %get-tuple-element.450, pred[]{:T(512)S(6)} %compare.286), kind=kOutput, calls=%fused_computation.10.clone.1 | convolution fusion | flops 616660992 | bytes 8880129 | tf_op jit(solution)/shard_map/while/body/eval_jaxpr/dot_general | solution.py:55
  156.2 9.2 %fusion.173 = f32[1024,2048]{1,0:T(8,128)} fusion(f32[5,2048]{1,0:T(8,128)S(1)} %get-tuple-element.467, f32[1,1024]{1,0:T(1,128)S(1)} %fusion.172, f32[3,1024]{1,0:T(4,128)S(1)} %get-tuple-element.429, f32[5]{0:T(128)S(1)} %pad.5.clone.2), kind=kOutput, calls=%fused_computation.19.clone.1 | convolution fusion | flops 125839360 | bytes 8445972 | tf_op jit(solution)/shard_map/while/body/eval_jaxpr/dot_general | solution.py:37
  165.3 7.7 %fusion.174 = f32[6,2048]{1,0:T(8,128)S(1)} fusion(f32[1024,2048]{1,0:T(8,128)} %fusion.173, f32[6,2048]{1,0:T(8,128)S(1)} %get-tuple-element.449, f32[1,1024]{1,0:T(1,128)S(1)} %get-tuple-element.425, f32[1,1024]{1,0:T(1,128)S(1)} %get-tuple-element.426, f32[1,1024]{1,0:T(1,128)S(1)} %get-tuple-element.427, ...), kind=kOutput, calls=%fused_computation.11.clone.1 | convolution fusion | flops 157329408 | bytes 8511489 | tf_op jit(solution)/shard_map/while/body/eval_jaxpr/dot_general | solution.py:52
  173.5 8.6 %fusion.175 = f32[24,2048]{1,0:T(8,128)S(1)} fusion(f32[24,1024]{1,0:T(8,128)S(1)} %concatenate.30, f32[1024,2048]{1,0:T(8,128)} %fusion.173, f32[24,2048]{1,0:T(8,128)S(1)} %get-tuple-element.450, pred[]{:T(512)S(6)} %compare.286), kind=kOutput, calls=%fused_computation.10.clone.1 | convolution fusion | flops 616660992 | bytes 8880129 | tf_op jit(solution)/shard_map/while/body/eval_jaxpr/dot_general | solution.py:55
  182.3 9.2 %fusion.173 = f32[1024,2048]{1,0:T(8,128)} fusion(f32[5,2048]{1,0:T(8,128)S(1)} %get-tuple-element.467, f32[1,1024]{1,0:T(1,128)S(1)} %fusion.172, f32[3,1024]{1,0:T(4,128)S(1)} %get-tuple-element.429, f32[5]{0:T(128)S(1)} %pad.5.clone.2), kind=kOutput, calls=%fused_computation.19.clone.1 | convolution fusion | flops 125839360 | bytes 8445972 | tf_op jit(solution)/shard_map/while/body/eval_jaxpr/dot_general | solution.py:37
  191.4 7.7 %fusion.174 = f32[6,2048]{1,0:T(8,128)S(1)} fusion(f32[1024,2048]{1,0:T(8,128)} %fusion.173, f32[6,2048]{1,0:T(8,128)S(1)} %get-tuple-element.449, f32[1,1024]{1,0:T(1,128)S(1)} %get-tuple-element.425, f32[1,1024]{1,0:T(1,128)S(1)} %get-tuple-element.426, f32[1,1024]{1,0:T(1,128)S(1)} %get-tuple-element.427, ...), kind=kOutput, calls=%fused_computation.11.clone.1 | convolution fusion | flops 157329408 | bytes 8511489 | tf_op jit(solution)/shard_map/while/body/eval_jaxpr/dot_general | solution.py:52
  199.6 8.6 %fusion.175 = f32[24,2048]{1,0:T(8,128)S(1)} fusion(f32[24,1024]{1,0:T(8,128)S(1)} %concatenate.30, f32[1024,2048]{1,0:T(8,128)} %fusion.173, f32[24,2048]{1,0:T(8,128)S(1)} %get-tuple-element.450, pred[]{:T(512)S(6)} %compare.286), kind=kOutput, calls=%fused_computation.10.clone.1 | convolution fusion | flops 616660992 | bytes 8880129 | tf_op jit(solution)/shard_map/while/body/eval_jaxpr/dot_general | solution.py:55
  208.4 9.2 %fusion.173 = f32[1024,2048]{1,0:T(8,128)} fusion(f32[5,2048]{1,0:T(8,128)S(1)} %get-tuple-element.467, f32[1,1024]{1,0:T(1,128)S(1)} %fusion.172, f32[3,1024]{1,0:T(4,128)S(1)} %get-tuple-element.429, f32[5]{0:T(128)S(1)} %pad.5.clone.2), kind=kOutput, calls=%fused_computation.19.clone.1 | convolution fusion | flops 125839360 | bytes 8445972 | tf_op jit(solution)/shard_map/while/body/eval_jaxpr/dot_general | solution.py:37
  217.5 7.7 %fusion.174 = f32[6,2048]{1,0:T(8,128)S(1)} fusion(f32[1024,2048]{1,0:T(8,128)} %fusion.173, f32[6,2048]{1,0:T(8,128)S(1)} %get-tuple-element.449, f32[1,1024]{1,0:T(1,128)S(1)} %get-tuple-element.425, f32[1,1024]{1,0:T(1,128)S(1)} %get-tuple-element.426, f32[1,1024]{1,0:T(1,128)S(1)} %get-tuple-element.427, ...), kind=kOutput, calls=%fused_computation.11.clone.1 | convolution fusion | flops 157329408 | bytes 8511489 | tf_op jit(solution)/shard_map/while/body/eval_jaxpr/dot_general | solution.py:52
  225.7 8.6 %fusion.175 = f32[24,2048]{1,0:T(8,128)S(1)} fusion(f32[24,1024]{1,0:T(8,128)S(1)} %concatenate.30, f32[1024,2048]{1,0:T(8,128)} %fusion.173, f32[24,2048]{1,0:T(8,128)S(1)} %get-tuple-element.450, pred[]{:T(512)S(6)} %compare.286), kind=kOutput, calls=%fused_computation.10.clone.1 | convolution fusion | flops 616660992 | bytes 8880129 | tf_op jit(solution)/shard_map/while/body/eval_jaxpr/dot_general | solution.py:55
  237.4 35.5 %add_bitcast_fusion = f32[2048,128]{1,0:T(8,128)S(1)} fusion(f32[2048]{0:T(1024)S(1)} %bitcast.230, s32[2048]{0:T(1024)S(1)} %bitcast.275, f32[2048]{0:T(1024)S(1)} %bitcast.231, s32[2048]{0:T(1024)S(1)} %bitcast.276, f32[2048]{0:T(1024)S(1)} %bitcast.232, s32[2048]{0:T(1024)S(1)} %bitcast.277, f32[2048]{0:T(1024)S(1)} %bitcast.296, s32[2048]{0:T(1024)S(1)} %bitcast.314, ...), kind=kLoop, calls=%fused_computation.53 | loop fusion | flops 50069504 | bytes 2097152 | tf_op jit(solution)/shard_map/add | solution.py:148
  272.9 8.7 %broadcast_multiply_fusion.3 = f32[2048,4,128]{2,1,0:T(4,128)} fusion(f32[2048,128]{1,0:T(8,128)S(1)} %add_bitcast_fusion, f32[2048,4]{1,0:T(8,128)S(1)} %copy.10), kind=kLoop, calls=%fused_computation.52 | loop fusion | flops 1048576 | bytes 5275648 | tf_op jit(solution)/shard_map/cp,kp->pck/dot_general | solution.py:181
  281.6 15.0 %scatter_custom_fusion = f32[128,512]{1,0:T(8,128)} fusion(s32[2048]{0:T(1024)S(1)} %and_select_fusion.19, f32[256,8,4,128]{3,2,1,0:T(4,128)} %bitcast.179, f32[]{:T(128)} %constant.741.clone.1), kind=kCustom, calls=%fused_computation.49 | custom fusion | flops 1048576 | bytes 4456452 | tf_op jit(solution)/shard_map/scatter-add | solution.py:190
  296.6 35.3 %reduce-scatter.2.cloned.1.call-done = f32[16,512]{1,0:T(8,128)} async-done(((f32[128,512]{1,0:T(8,128)}), f32[16,512]{1,0:T(8,128)}) %reduce-scatter.2.cloned.1.call-update) | async-done | bytes 32784 | tf_op jit(solution)/shard_map/reduce_scatter | solution.py:189
  (129 shorter events, 9.6 us)
Async XLA Ops:
  7.2 324.7 %reduce-scatter.2.cloned.1.call-start = ((), (), s32[]{:S(2)}) async-start(), calls=%async_computation.1 | async-start | bytes 294912 | tf_op jit(solution)/shard_map/reduce_scatter | solution.py:189
  25.3 209.2 %copy-start = (f32[3,2048]{1,0:T(4,128)S(1)}, f32[3,2048]{1,0:T(4,128)}, u32[]{:S(2)}) copy-start(f32[3,2048]{1,0:T(4,128)} %param.10) | copy-start | bytes 73732
  25.3 209.2 %copy-start.1 = (f32[3,2048]{1,0:T(4,128)S(1)}, f32[3,2048]{1,0:T(4,128)}, u32[]{:S(2)}) copy-start(f32[3,2048]{1,0:T(4,128)} %param.11) | copy-start | bytes 73732
  25.3 209.4 %copy-start.7 = (s32[2048]{0:T(1024)S(1)}, s32[2048]{0:T(1024)}, u32[]{:S(2)}) copy-start(s32[2048]{0:T(1024)} %param.15) | copy-start | bytes 24580
  25.3 209.4 %copy-start.6 = (s32[2048,1]{0,1:T(1,128)S(1)}, s32[2048,1]{0,1:T(1,128)}, u32[]{:S(2)}) copy-start(s32[2048,1]{0,1:T(1,128)} %param.17) | copy-start | bytes 24580
  25.3 209.4 %copy-start.2 = (f32[3,2048]{1,0:T(4,128)S(1)}, f32[3,2048]{1,0:T(4,128)}, u32[]{:S(2)}) copy-start(f32[3,2048]{1,0:T(4,128)} %param.14) | copy-start | bytes 73732
  25.4 210.0 %copy-start.4 = (f32[2048]{0:T(1024)S(1)}, f32[2048]{0:T(1024)}, u32[]{:S(2)}) copy-start(f32[2048]{0:T(1024)} %param.13) | copy-start | bytes 24580
  25.4 210.4 %copy-start.5 = (s32[2048]{0:T(1024)S(1)}, s32[2048]{0:T(1024)}, u32[]{:S(2)}) copy-start(s32[2048]{0:T(1024)} %param.16) | copy-start | bytes 24580
  234.8 61.7 %copy-start.3 = (f32[3,2048]{1,0:T(4,128)}, f32[3,2048]{1,0:T(4,128)S(1)}, u32[]{:S(2)}) copy-start(f32[3,2048]{1,0:T(4,128)S(1)} %get-tuple-element.166) | copy-start | bytes 73732
Sparse Core Ops, SparseCore 0:
  296.7 35.1 reduce-scatter.1
where the time goes:
time: 341 us; the launch traced here: 340 us
  matrix products  204 us (60%)
  other arithmetic  65.4 us (19%)
  waiting for transfers between devices  35.3 us (10%)
  blocking collectives  15.6 us (5%)
  between operations  14.4 us (4%)
  local copies, waits for them, and re-layouts  4.82 us (1%)
    dot_general x8, matrix products, pair_sums(): lax.dot_general(source_rows, target_rows, (((0,), (0,)), ((), ())), preci...  73.3 us
    dot_general x8, matrix products, pair_sums(): jnp.dot(second_rows, slope_vals, precision=highest, preferred_element_typ...  68.6 us
    dot_general x8, matrix products, pair_sums(): jnp.dot(first_rows, kernel_vals, precision=highest, preferred_element_typ...  61.8 us
    add x1, other arithmetic, spread(): overall + jnp.where(stencil_cells[node][None, :] == cell_ids, weights[nod...  35.5 us
    reduce_scatter x1, waiting for transfers between devices, on_device(): lax.psum_scatter(jax.ops.segment_sum(contrib, shifted, num_segments=tiles...  35.3 us
    all_gather x1, blocking collectives, on_device(): lax.all_gather(sources, 'blk', axis=1, tiled=True)  15.6 us
    scatter-add x1, other arithmetic, on_device(): jax.ops.segment_sum(contrib, shifted, num_segments=tiles_count * lax.axis...  15 us
    dot_general x1, other arithmetic, on_device(): jnp.einsum('cp,kp->pck', values, spread_w).reshape(local_count, 512)  8.66 us
  transfers between devices with their start and end apart: 1, of which 1 were waited for; matrix products, arithmetic and copies ran while one was open for 0% of the time, Pallas kernels for 0%

commit v1 on v0

v1 whole, which is shorter than its diff:
```python
import functools
import math

import jax
import jax.numpy as jnp
from jax import lax
from jax.experimental import pallas as pl
from jax.experimental.pallas import tpu as pltpu
from jax.sharding import PartitionSpec as P

time_step = 0.02
move_scale = 2.0
inverse_volume = 32.0
kernel_scale = 1.0 / (4.0 * math.pi)
f32 = jnp.float32
bf16 = jnp.bfloat16
transposed_rhs = (((1,), (1,)), ((), ()))


def split3(x):
    high = x.astype(bf16).astype(f32)
    rest = x - high
    middle = rest.astype(bf16).astype(f32)
    return high, middle, rest - middle


def rows_of(array, first, count):
    return [array[first + d : first + d + 1] for d in range(count)]


def cross_rows(left, right):
    return [
        left[1] * right[2] - left[2] * right[1],
        left[2] * right[0] - left[0] * right[2],
        left[0] * right[1] - left[1] * right[0],
    ]


def square_sum(rows):
    return rows[0] * rows[0] + rows[1] * rows[1] + rows[2] * rows[2]


def target_features(points):
    one = jnp.ones_like(points[0])
    zero = jnp.zeros_like(one)
    stack = jnp.concatenate(points + [one, square_sum(points), zero, zero, zero], axis=0)
    high, middle, low = split3(stack)
    return jnp.concatenate([high, middle, high, low, high, middle], axis=0)


def source_features(src):
    points = rows_of(src, 0, 3)
    vortex = rows_of(src, 3, 3)
    radius = src[6:7]
    offset = square_sum(points) + radius * radius
    one = jnp.ones_like(radius)
    zero = jnp.zeros_like(radius)
    stack = jnp.concatenate([-2.0 * p for p in points] + [offset, one, zero, zero, zero], axis=0)
    high, middle, low = split3(stack)
    features = jnp.concatenate([high, high, middle, high, low, middle], axis=0)
    base = jnp.concatenate(vortex + cross_rows(vortex, points) + [zero, zero], axis=0)
    groups = jnp.concatenate([base] + [base * p for p in points] + [base * offset], axis=0)
    parts = split3(groups)
    moments = jnp.concatenate(list(parts) + [jnp.zeros_like(base)], axis=0)
    return features.astype(bf16), moments.astype(bf16)


def add_pair_sums(count, width, target_ref, feature_ref, moment_ref, sum_ref):
    def step(k, carry):
        start = pl.multiple_of(k * width, width)
        square = jnp.dot(
            target_ref[...], feature_ref[:, pl.ds(start, width)], preferred_element_type=f32
        )
        inverse = lax.rsqrt(square)
        inverse2 = inverse * inverse
        slope = inverse2 * inverse2 * inverse
        high = slope.astype(bf16)
        low = (slope - high.astype(f32)).astype(bf16)
        moments = moment_ref[:, pl.ds(start, width)]
        sum_ref[...] += lax.dot_general(
            high, moments, transposed_rhs, preferred_element_type=f32
        ) + lax.dot_general(low, moments, transposed_rhs, preferred_element_type=f32)
        return carry

    lax.fori_loop(0, count // width, step, 0)


def own_kernel(width, pos_ref, src_ref, sum_ref, target_ref, feature_ref, moment_ref):
    target_ref[...] = target_features(rows_of(pos_ref[...], 0, 3)).T.astype(bf16)
    features, moments = source_features(src_ref[...])
    feature_ref[...] = features
    moment_ref[...] = moments
    sum_ref[...] = jnp.zeros_like(sum_ref)
    add_pair_sums(src_ref.shape[1], width, target_ref, feature_ref, moment_ref, sum_ref)


def combine(points, vortex, sums):
    plain, by_x, by_y, by_z, by_offset = [sums[8 * k : 8 * k + 8] for k in range(5)]
    kernel = (
        square_sum(points) * plain
        + by_offset
        - 2.0 * (points[0] * by_x + points[1] * by_y + points[2] * by_z)
    ) * kernel_scale
    along = points[0] * vortex[0] + points[1] * vortex[1] + points[2] * vortex[2]
    slope = (along * plain - vortex[0] * by_x - vortex[1] * by_y - vortex[2] * by_z) * (
        -3.0 * kernel_scale
    )
    kernel_a = rows_of(kernel, 0, 3)
    velocity = [u - v for u, v in zip(cross_rows(kernel_a, points), rows_of(kernel, 3, 3))]
    term_one = cross_rows(kernel_a, vortex)
    slope_a = rows_of(slope, 0, 3)
    term_two = [u - v for u, v in zip(cross_rows(slope_a, points), rows_of(slope, 3, 3))]
    return velocity, [u + v for u, v in zip(term_one, term_two)]


def axis_weights(node, base, fraction, cells):
    t = fraction
    s = 1.0 - t
    inner = [1.0 - 2.5 * u * u + 1.5 * u * u * u for u in (t, s)]
    weights = [-0.5 * s * s * t, inner[0], inner[1], -0.5 * t * t * s]
    place = (node - base + 1) & (cells - 1)
    out = jnp.zeros(node.shape, f32)
    for k in range(4):
        out = jnp.where(place == k, weights[k], out)
    return out


def tail_kernel(
    width,
    tiles,
    owners,
    pos_ref,
    src_ref,
    before_ref,
    dye_ref,
    frac_ref,
    cell_ref,
    tile_ref,
    owner_ref,
    *refs,
):
    other_refs = refs[:-6]
    velocity_ref, grid_ref, target_ref, feature_ref, moment_ref, sum_ref = refs[-6:]
    count = src_ref.shape[1]
    points = rows_of(pos_ref[...], 0, 3)
    target_ref[...] = target_features(points).T.astype(bf16)
    for k, other_ref in enumerate(other_refs):
        features, moments = source_features(other_ref[...])
        feature_ref[:, k * count : (k + 1) * count] = features
        moment_ref[:, k * count : (k + 1) * count] = moments
    sum_ref[...] = before_ref[...]
    add_pair_sums(
        len(other_refs) * count, width, target_ref, feature_ref, moment_ref, sum_ref
    )
    sums = sum_ref[...].T
    sums = sums[0:40] + sums[40:80] + sums[80:120]
    vortex = rows_of(src_ref[...], 3, 3)
    velocity, stretch = combine(points, vortex, sums)
    velocity_ref[...] = jnp.concatenate(velocity, axis=0)

    values = [inverse_volume * (a + time_step * d) for a, d in zip(vortex, stretch)]
    values.append(inverse_volume * dye_ref[...])
    cell = cell_ref[...]
    starts = [cell & 7, (cell >> 3) & 3, cell >> 5]
    bases, fractions = [], []
    for d in range(3):
        place = starts[d].astype(f32) + frac_ref[d : d + 1, :] + move_scale * velocity[d]
        lowest = jnp.floor(place)
        bases.append(lowest.astype(jnp.int32))
        fractions.append(place - lowest)
    node = lax.broadcasted_iota(jnp.int32, (8, count), 0)
    weight_x = axis_weights(node, bases[0], fractions[0], 8)
    node = lax.broadcasted_iota(jnp.int32, (16, count), 0)
    weight_zy = axis_weights(node & 3, bases[1], fractions[1], 4) * axis_weights(
        node >> 2, bases[2], fractions[2], 4
    )
    spread = jnp.concatenate([weight_zy[k : k + 1] * weight_x for k in range(16)], axis=0)
    spread_high = spread.astype(bf16)
    spread_low = (spread - spread_high.astype(f32)).astype(bf16)
    spread_both = jnp.concatenate([spread_high, spread_low], axis=0)

    me = lax.axis_index("dom")
    slot = owner_ref[...] ^ me
    node = lax.broadcasted_iota(jnp.int32, (16, count), 0)
    mine = slot * tiles + tile_ref[...] - (node >> 2)
    value = jnp.concatenate(values * 4, axis=0)
    value_high = value.astype(bf16).astype(f32)
    value_low = value - value_high
    half = 8
    per_group = tiles // half * half // 4
    for group in range(owners * tiles // (4 * half)):
        masks = [mine == 4 * (group * half + k) for k in range(half)]
        picked_high = jnp.concatenate(
            [jnp.where(m, value_high, 0.0).astype(bf16) for m in masks], axis=0
        )
        picked_low = jnp.concatenate(
            [jnp.where(m, value_low, 0.0).astype(bf16) for m in masks], axis=0
        )
        both = lax.dot_general(
            picked_high, spread_both, transposed_rhs, preferred_element_type=f32
        )
        low = lax.dot_general(
            picked_low, spread_high, transposed_rhs, preferred_element_type=f32
        )
        grid_ref[group * 16 * half : (group + 1) * 16 * half, :] = (
            both[:, 0:128] + both[:, 128:256] + low
        )


def vmem_specs(count):
    return [pl.BlockSpec(memory_space=pltpu.VMEM)] * count


def on_device(
    positions, strength, core_radius, dye_amount, cell_fraction, cell_index, tile_local, owner_dom
):
    count = positions.shape[1]
    tiles = count // 128
    owners = lax.axis_size("dom")
    blocks = lax.axis_size("blk")
    width = math.gcd(count, 512)
    sources = jnp.concatenate([positions, strength, core_radius[None]], axis=0)
    others = [
        lax.ppermute(sources, "blk", [(i, (i + s) % blocks) for i in range(blocks)])
        for s in range(1, blocks)
    ]
    scratch = lambda n: [
        pltpu.VMEM((count, 48), bf16),
        pltpu.VMEM((48, n * count), bf16),
        pltpu.VMEM((128, n * count), bf16),
    ]
    params = pltpu.CompilerParams(vmem_limit_bytes=48 * 2**20)
    cost = lambda n: pl.CostEstimate(
        flops=n * count * count * 256 * 2 * 3,
        bytes_accessed=4 * count * 256,
        transcendentals=n * count * count,
    )
    own_sums = pl.pallas_call(
        functools.partial(own_kernel, width),
        out_shape=jax.ShapeDtypeStruct((count, 128), f32),
        in_specs=vmem_specs(2),
        out_specs=vmem_specs(1)[0],
        scratch_shapes=scratch(1),
        compiler_params=params,
        cost_estimate=cost(1),
        name="own_pairs",
    )(positions, sources)
    velocity, grid = pl.pallas_call(
        functools.partial(tail_kernel, width, tiles, owners),
        out_shape=(
            jax.ShapeDtypeStruct((3, count), f32),
            jax.ShapeDtypeStruct((owners * tiles * 4, 128), f32),
        ),
        in_specs=vmem_specs(8 + len(others)),
        out_specs=tuple(vmem_specs(2)),
        scratch_shapes=scratch(len(others)) + [pltpu.VMEM((count, 128), f32)],
        compiler_params=params,
        cost_estimate=cost(len(others)),
        name="other_pairs_and_deposit",
    )(
        positions,
        sources,
        own_sums,
        dye_amount[None],
        cell_fraction,
        cell_index[None],
        tile_local[None],
        owner_dom.reshape(1, count),
        *others,
    )
    step = owners // 2
    grid = grid.reshape(owners, tiles * 4, 128)
    bit = 1
    while bit < owners:
        pairs = grid.reshape(-1, 2, *grid.shape[1:])
        got = lax.ppermute(pairs[:, 1], "dom", [(i, i ^ bit) for i in range(owners)])
        grid = pairs[:, 0] + got
        bit *= 2
    return velocity, grid.reshape(tiles, 4, 128)


def solution(mesh):
    both = ("dom", "blk")
    placed = (
        P(None, both),
        P(None, both),
        P(both),
        P(both),
        P(None, both),
        P(both),
        P(both),
        P(both, None),
    )
    return jax.shard_map(
        on_device,
        mesh=mesh,
        in_specs=placed,
        out_specs=(P(None, both), P(both, None, None)),
        check_vma=False,
    )
```

time: 341 us -> 53.3 us (0.16)
  matrix products: 204 us -> 0 us
  other arithmetic: 65.4 us -> 1.5 us
  Pallas kernels: 0 us -> 34.9 us
  waiting for transfers between devices: 35.3 us -> 6.51 us
  blocking collectives: 15.6 us -> 0 us
  between operations: 14.4 us -> 0.8 us
  starting transfers between devices: 0.04 us -> 9.32 us
  local copies, waits for them, and re-layouts: 4.82 us -> 0.06 us
    dot_general x24 -> x0, matrix products: 204 us -> none  [the longest x8 73.3 us: pair_sums(): lax.dot_general(source_rows, target_rows, (((0,), (0,)), ((), ())), preci...]
    add x14 -> x2, other arithmetic: 36.6 us -> 0.64 us  [on_device(): grid = pairs[:, 0] + got]
    reduce_scatter x1 -> x0, waiting for transfers between devices: 35.3 us -> none  [on_device(): lax.psum_scatter(jax.ops.segment_sum(contrib, shifted, num_segments=tiles...]
    pallas_call x0 -> x2, Pallas kernels: none -> 34.9 us  [the longest x1 26.7 us: on_device(): pl.pallas_call(functools.partial(tail_kernel, width, tiles, owners), out_...]
    all_gather x1 -> x0, blocking collectives: 15.6 us -> none  [on_device(): lax.all_gather(sources, 'blk', axis=1, tiled=True)]
    scatter-add x1 -> x0, other arithmetic: 15 us -> none  [on_device(): jax.ops.segment_sum(contrib, shifted, num_segments=tiles_count * lax.axis...]
    ppermute x0 -> x6, starting transfers between devices: none -> 9.32 us  [the longest x3 6.11 us: on_device(): lax.ppermute(sources, 'blk', [(i, (i + s) % blocks) for i in range(blocks)])]
    dot_general x1 -> x0, other arithmetic: 8.66 us -> none  [on_device(): jnp.einsum('cp,kp->pck', values, spread_w).reshape(local_count, 512)]
  transfers between devices with their start and end apart: 1 -> 6, of which waited for: 1 -> 3; matrix products, arithmetic and copies ran while one was open for 0% -> 0% of each run, Pallas kernels for 0% -> 16%
where the time goes in v1:
time: 53.3 us; the launch traced here: 53.1 us
  Pallas kernels  34.9 us (65%)
  starting transfers between devices  9.32 us (17%)
  waiting for transfers between devices  6.51 us (12%)
  other arithmetic  1.5 us (3%)
  between operations  0.8 us (2%)
    pallas_call x1, Pallas kernels, on_device(): pl.pallas_call(functools.partial(tail_kernel, width, tiles, owners), out_...  26.7 us
    pallas_call x1, Pallas kernels, on_device(): pl.pallas_call(functools.partial(own_kernel, width), out_shape=jax.ShapeD...  8.25 us
    ppermute x3, waiting for transfers between devices, on_device(): lax.ppermute(pairs[:, 1], 'dom', [(i, i ^ bit) for i in range(owners)])  6.51 us
    ppermute x3, starting transfers between devices, on_device(): lax.ppermute(sources, 'blk', [(i, (i + s) % blocks) for i in range(blocks)])  6.11 us
    ppermute x3, starting transfers between devices, on_device(): lax.ppermute(pairs[:, 1], 'dom', [(i, i ^ bit) for i in range(owners)])  3.21 us
  transfers between devices with their start and end apart: 6, of which 3 were waited for; matrix products, arithmetic and copies ran while one was open for 0% of the time, Pallas kernels for 16%

profile of v1, /device:TPU:0, one launch (start us, length us, event | category | flops | bytes accessed | tf_op | source)
XLA Modules:
  0.0 53.1 jit_solution(2554532970587530470)
XLA Ops:
  0.6 0.0 copy-start
  0.6 0.8 %pad_maximum_fusion.src_ref = f32[7,2048]{1,0:T(8,128)S(1)} fusion(f32[1,2048]{1,0:T(1,128)} %bitcast.45, f32[3,2048]{1,0:T(4,128)} %param.9, f32[3,2048]{1,0:T(4,128)} %pos_ref.3), kind=kLoop, calls=%fused_computation.7 | loop fusion | flops 28672 | bytes 114688 | tf_op jit(solution)/shard_map/concatenate | solution.py:222
  1.5 0.0 copy-start.1
  1.5 0.0 copy-start.2
  1.5 0.0 copy-start.3
  1.5 0.0 copy-start.4
  1.5 0.0 copy-start.5
  1.6 5.1 %collective-permute-start.2 = (f32[7,2048]{1,0:T(8,128)S(1)}, f32[7,2048]{1,0:T(8,128)S(1)}, u32[]{:S(2)}, u32[]{:S(2)}) collective-permute-start(f32[7,2048]{1,0:T(8,128)S(1)} %pad_maximum_fusion.src_ref), channel_id=1, source_target_pairs={{0,3},{1,0},{2,1},{3,2},{4,7},{5,4},{6,5},{7,6},{8,11},{9,8},{10,9... | collective-permute-start | bytes 172040 | tf_op jit(solution)/shard_map/ppermute | solution.py:224
  6.7 0.0 collective-permute-start.1
  6.7 1.0 %collective-permute-start = (f32[7,2048]{1,0:T(8,128)S(1)}, f32[7,2048]{1,0:T(8,128)S(1)}, u32[]{:S(2)}, u32[]{:S(2)}) collective-permute-start(f32[7,2048]{1,0:T(8,128)S(1)} %pad_maximum_fusion.src_ref), channel_id=1, source_target_pairs={{0,1},{1,2},{2,3},{3,0},{4,5},{5,6},{6,7},{7,4},{8,9},{9,10},{10,1... | collective-permute-start | bytes 172040 | tf_op jit(solution)/shard_map/ppermute | solution.py:224
  7.7 0.0 copy-done
  7.7 8.2 %own_pairs.1.before_ref = f32[2048,128]{1,0:T(8,128)S(1)} custom-call(f32[3,2048]{1,0:T(4,128)S(1)} %copy-done, f32[7,2048]{1,0:T(8,128)S(1)} %pad_maximum_fusion.src_ref), custom_call_target="tpu_custom_call" | custom-call | flops 6442450944 | bytes 2097152 | tf_op jit(solution)/shard_map/own_pairs/pallas_call | solution.py:238
  15.9 0.0 collective-permute-done.2.refs_2_
  15.9 0.0 collective-permute-done.1.refs_1_
  15.9 0.0 collective-permute-done.refs_0_
  16.0 0.0 copy-done.1
  16.0 0.0 copy-done.2
  16.0 0.0 copy-done.3
  16.0 0.0 copy-done.4
  16.0 0.0 copy-done.5
  16.0 26.7 %other_pairs_and_deposit.1 = (f32[3,2048]{1,0:T(4,128)}, f32[512,128]{1,0:T(8,128)S(1)}) custom-call(f32[3,2048]{1,0:T(4,128)S(1)} %copy-done, f32[7,2048]{1,0:T(8,128)S(1)} %pad_maximum_fusion.src_ref, f32[2048,128]{1,0:T(8,128)S(1)} %own_pairs.1.before_ref, f32[1,2048]{1,0:T(1,128)S(1)} %bitcast.38, f32[3,2048]{1,0:T(4,128)S(1)} %copy-done.1, ...), custom_call_target="tpu_custom_call" | custom-call | flops 19327352832 | bytes 2097152 | tf_op jit(solution)/shard_map/other_pairs_and_deposit/pallas_call | solution.py:248
  42.7 0.1 collective-permute-start.3
  42.8 1.3 %collective-permute-done.3 = f32[4,64,128]{2,1,0:T(8,128)S(1)} collective-permute-done((f32[4,64,128]{2,1,0:T(8,128)S(1)}, f32[4,64,128]{2,1,0:T(8,128)S(1)}, u32[]{:S(2)}, u32[]{:S(2)}) %collective-permute-start.3) | collective-permute-done | bytes 131104 | tf_op jit(solution)/shard_map/ppermute | solution.py:276
  44.1 1.6 %collective-permute-start.4 = (f32[2,64,128]{2,1,0:T(8,128)S(1)}, f32[2,64,128]{2,1,0:T(8,128)S(1)}, u32[]{:S(2)}, u32[]{:S(2)}) collective-permute-start(f32[2,64,128]{2,1,0:T(8,128)S(1)} %slice_bitcast_fusion.2), channel_id=1, source_target_pairs={{0,8},{4,12},{8,0},{12,4},{16,24},{20,28},{24,16},{28,20},{1,9},{5... | collective-permute-start | bytes 196616 | tf_op jit(solution)/shard_map/ppermute | solution.py:276
  45.7 2.8 %collective-permute-done.4 = f32[2,64,128]{2,1,0:T(8,128)S(1)} collective-permute-done((f32[2,64,128]{2,1,0:T(8,128)S(1)}, f32[2,64,128]{2,1,0:T(8,128)S(1)}, u32[]{:S(2)}, u32[]{:S(2)}) %collective-permute-start.4) | collective-permute-done | bytes 65568 | tf_op jit(solution)/shard_map/ppermute | solution.py:276
  48.5 1.6 %collective-permute-start.5 = (f32[1,64,128]{2,1,0:T(8,128)S(1)}, f32[1,64,128]{2,1,0:T(8,128)S(1)}, u32[]{:S(2)}, u32[]{:S(2)}) collective-permute-start(f32[1,64,128]{2,1,0:T(8,128)S(1)} %slice_bitcast_fusion.4), channel_id=1, source_target_pairs={{0,16},{4,20},{8,24},{12,28},{16,0},{20,4},{24,8},{28,12},{1,17},{... | collective-permute-start | bytes 98312 | tf_op jit(solution)/shard_map/ppermute | solution.py:276
  50.1 2.4 %collective-permute-done.5 = f32[1,64,128]{2,1,0:T(8,128)S(1)} collective-permute-done((f32[1,64,128]{2,1,0:T(8,128)S(1)}, f32[1,64,128]{2,1,0:T(8,128)S(1)}, u32[]{:S(2)}, u32[]{:S(2)}) %collective-permute-start.5) | collective-permute-done | bytes 32800 | tf_op jit(solution)/shard_map/ppermute | solution.py:276
  52.5 0.6 %fusion.3 = f32[1,64,128]{2,1,0:T(8,128)} fusion(f32[1,64,128]{2,1,0:T(8,128)S(1)} %collective-permute-done.5, f32[1,2,64,128]{3,2,1,0:T(8,128)S(1)} %fusion.2), kind=kLoop, calls=%fused_computation.10 | loop fusion | flops 8192 | bytes 98304 | tf_op jit(solution)/shard_map/add | solution.py:277
  (5 shorter events, 0.1 us)
Async XLA Ops:
  0.6 7.0 %copy-start = (f32[3,2048]{1,0:T(4,128)S(1)}, f32[3,2048]{1,0:T(4,128)}, u32[]{:S(2)}) copy-start(f32[3,2048]{1,0:T(4,128)} %pos_ref.3) | copy-start | bytes 73732
  1.5 14.5 %copy-start.1 = (f32[3,2048]{1,0:T(4,128)S(1)}, f32[3,2048]{1,0:T(4,128)}, u32[]{:S(2)}) copy-start(f32[3,2048]{1,0:T(4,128)} %frac_ref.1) | copy-start | bytes 73732
  1.5 14.5 %copy-start.2 = (f32[2048]{0:T(1024)S(1)}, f32[2048]{0:T(1024)}, u32[]{:S(2)}) copy-start(f32[2048]{0:T(1024)} %param.11) | copy-start | bytes 24580
  1.5 14.5 %copy-start.3 = (s32[2048]{0:T(1024)S(1)}, s32[2048]{0:T(1024)}, u32[]{:S(2)}) copy-start(s32[2048]{0:T(1024)} %param.13) | copy-start | bytes 24580
  1.5 14.5 %copy-start.4 = (s32[2048]{0:T(1024)S(1)}, s32[2048]{0:T(1024)}, u32[]{:S(2)}) copy-start(s32[2048]{0:T(1024)} %param.14) | copy-start | bytes 24580
  1.5 14.5 %copy-start.5 = (s32[2048,1]{0,1:T(1,128)S(1)}, s32[2048,1]{0,1:T(1,128)}, u32[]{:S(2)}) copy-start(s32[2048,1]{0,1:T(1,128)} %param.15) | copy-start | bytes 24580
  1.6 14.4 %collective-permute-start.2 = (f32[7,2048]{1,0:T(8,128)S(1)}, f32[7,2048]{1,0:T(8,128)S(1)}, u32[]{:S(2)}, u32[]{:S(2)}) collective-permute-start(f32[7,2048]{1,0:T(8,128)S(1)} %pad_maximum_fusion.src_ref), channel_id=1, source_target_pairs={{0,3},{1,0},{2,1},{3,2},{4,7},{5,4},{6,5},{7,6},{8,11},{9,8},{10,9... | collective-permute-start | bytes 172040 | tf_op jit(solution)/shard_map/ppermute | solution.py:224
  6.7 9.3 %collective-permute-start.1 = (f32[7,2048]{1,0:T(8,128)S(1)}, f32[7,2048]{1,0:T(8,128)S(1)}, u32[]{:S(2)}, u32[]{:S(2)}) collective-permute-start(f32[7,2048]{1,0:T(8,128)S(1)} %pad_maximum_fusion.src_ref), channel_id=1, source_target_pairs={{0,2},{1,3},{2,0},{3,1},{4,6},{5,7},{6,4},{7,5},{8,10},{9,11},{10,... | collective-permute-start | bytes 172040 | tf_op jit(solution)/shard_map/ppermute | solution.py:224
  6.7 9.3 %collective-permute-start = (f32[7,2048]{1,0:T(8,128)S(1)}, f32[7,2048]{1,0:T(8,128)S(1)}, u32[]{:S(2)}, u32[]{:S(2)}) collective-permute-start(f32[7,2048]{1,0:T(8,128)S(1)} %pad_maximum_fusion.src_ref), channel_id=1, source_target_pairs={{0,1},{1,2},{2,3},{3,0},{4,5},{5,6},{6,7},{7,4},{8,9},{9,10},{10,1... | collective-permute-start | bytes 172040 | tf_op jit(solution)/shard_map/ppermute | solution.py:224
  42.7 1.4 %collective-permute-start.3 = (f32[4,64,128]{2,1,0:T(8,128)S(1)}, f32[4,64,128]{2,1,0:T(8,128)S(1)}, u32[]{:S(2)}, u32[]{:S(2)}) collective-permute-start(f32[4,64,128]{2,1,0:T(8,128)S(1)} %slice_bitcast_fusion), channel_id=1, source_target_pairs={{0,4},{4,0},{8,12},{12,8},{16,20},{20,16},{24,28},{28,24},{1,5},{5... | collective-permute-start | bytes 393224 | tf_op jit(solution)/shard_map/ppermute | solution.py:276
  44.1 4.3 %collective-permute-start.4 = (f32[2,64,128]{2,1,0:T(8,128)S(1)}, f32[2,64,128]{2,1,0:T(8,128)S(1)}, u32[]{:S(2)}, u32[]{:S(2)}) collective-permute-start(f32[2,64,128]{2,1,0:T(8,128)S(1)} %slice_bitcast_fusion.2), channel_id=1, source_target_pairs={{0,8},{4,12},{8,0},{12,4},{16,24},{20,28},{24,16},{28,20},{1,9},{5... | collective-permute-start | bytes 196616 | tf_op jit(solution)/shard_map/ppermute | solution.py:276
  48.5 4.0 %collective-permute-start.5 = (f32[1,64,128]{2,1,0:T(8,128)S(1)}, f32[1,64,128]{2,1,0:T(8,128)S(1)}, u32[]{:S(2)}, u32[]{:S(2)}) collective-permute-start(f32[1,64,128]{2,1,0:T(8,128)S(1)} %slice_bitcast_fusion.4), channel_id=1, source_target_pairs={{0,16},{4,20},{8,24},{12,28},{16,0},{20,4},{24,8},{28,12},{1,17},{... | collective-permute-start | bytes 98312 | tf_op jit(solution)/shard_map/ppermute | solution.py:276

commit v2 on v1

--- a/solution.py
+++ b/solution.py
@@ -60,38 +60,75 @@
     features = jnp.concatenate([high, high, middle, high, low, middle], axis=0)
     base = jnp.concatenate(vortex + cross_rows(vortex, points) + [zero, zero], axis=0)
     groups = jnp.concatenate([base] + [base * p for p in points] + [base * offset], axis=0)
-    parts = split3(groups)
-    moments = jnp.concatenate(list(parts) + [jnp.zeros_like(base)], axis=0)
+    moments = jnp.concatenate(list(split3(groups)) + [jnp.zeros_like(base)], axis=0)
     return features.astype(bf16), moments.astype(bf16)
 
 
-def add_pair_sums(count, width, target_ref, feature_ref, moment_ref, sum_ref):
-    def step(k, carry):
-        start = pl.multiple_of(k * width, width)
+def add_pair_sums(count, target_ref, feature_ref, moment_ref, sum_ref, slope_ref):
+    targets = sum_ref.shape[0]
+    width = slope_ref.shape[1]
+    chunk = math.gcd(targets, 256)
+    chunks = targets // chunk
+    lag = min(2, chunks)
+
+    def produce(start, number):
+        rows = slice(number * chunk, (number + 1) * chunk)
         square = jnp.dot(
-            target_ref[...], feature_ref[:, pl.ds(start, width)], preferred_element_type=f32
+            target_ref[rows, :], feature_ref[:, pl.ds(start, width)], preferred_element_type=f32
         )
         inverse = lax.rsqrt(square)
         inverse2 = inverse * inverse
         slope = inverse2 * inverse2 * inverse
         high = slope.astype(bf16)
-        low = (slope - high.astype(f32)).astype(bf16)
-        moments = moment_ref[:, pl.ds(start, width)]
-        sum_ref[...] += lax.dot_general(
-            high, moments, transposed_rhs, preferred_element_type=f32
-        ) + lax.dot_general(low, moments, transposed_rhs, preferred_element_type=f32)
+        first = 2 * number * chunk
+        slope_ref[first : first + chunk, :] = high
+        slope_ref[first + chunk : first + 2 * chunk, :] = (slope - high.astype(f32)).astype(bf16)
+
+    def consume(start, number):
+        both = lax.dot_general(
+            slope_ref[2 * number * chunk : 2 * (number + 1) * chunk, :],
+            moment_ref[:, pl.ds(start, width)],
+            transposed_rhs,
+            preferred_element_type=f32,
+        )
+        sum_ref[number * chunk : (number + 1) * chunk, :] += both[:chunk] + both[chunk:]
+
+    first = 2 * (chunks - lag) * chunk
+    slope_ref[first:, :] = jnp.zeros((2 * lag * chunk, width), bf16)
+    steps = count // width
+    unroll = math.gcd(steps, 4)
+
+    def step(k, carry):
+        for u in range(unroll):
+            start = pl.multiple_of((k * unroll + u) * width, width)
+            before = pl.multiple_of(jnp.maximum(k * unroll + u - 1, 0) * width, width)
+            for number in range(chunks):
+                if number >= lag:
+                    consume(start, number - lag)
+                else:
+                    consume(before, number - lag + chunks)
+                produce(start, number)
         return carry
 
-    lax.fori_loop(0, count // width, step, 0)
-
-
-def own_kernel(width, pos_ref, src_ref, sum_ref, target_ref, feature_ref, moment_ref):
+    lax.fori_loop(0, steps // unroll, step, 0)
+    for number in range(chunks - lag, chunks):
+        consume((steps - 1) * width, number)
+
+
+def own_kernel(
+    pos_ref, src_ref, sum_ref, target_ref, feature_ref, moment_ref, slope_ref
+):
     target_ref[...] = target_features(rows_of(pos_ref[...], 0, 3)).T.astype(bf16)
-    features, moments = source_features(src_ref[...])
-    feature_ref[...] = features
-    moment_ref[...] = moments
+    feature_ref[...], moment_ref[...] = source_features(src_ref[...])
     sum_ref[...] = jnp.zeros_like(sum_ref)
-    add_pair_sums(src_ref.shape[1], width, target_ref, feature_ref, moment_ref, sum_ref)
+    add_pair_sums(
+        src_ref.shape[1],
+        target_ref,
+        feature_ref,
+        moment_ref,
+        sum_ref,
+        slope_ref,
+    )
 
 
 def combine(points, vortex, sums):
@@ -126,7 +163,6 @@
 
 
 def tail_kernel(
-    width,
     tiles,
     owners,
     pos_ref,
@@ -139,18 +175,23 @@
     owner_ref,
     *refs,
 ):
-    other_refs = refs[:-6]
-    velocity_ref, grid_ref, target_ref, feature_ref, moment_ref, sum_ref = refs[-6:]
+    other_refs = refs[:-9]
+    velocity_ref, keep_ref, send_ref, *refs = refs[-9:]
+    target_ref, feature_ref, moment_ref, slope_ref, sum_ref, pick_ref = refs
     count = src_ref.shape[1]
     points = rows_of(pos_ref[...], 0, 3)
     target_ref[...] = target_features(points).T.astype(bf16)
     for k, other_ref in enumerate(other_refs):
-        features, moments = source_features(other_ref[...])
-        feature_ref[:, k * count : (k + 1) * count] = features
-        moment_ref[:, k * count : (k + 1) * count] = moments
+        place = slice(k * count, (k + 1) * count)
+        feature_ref[:, place], moment_ref[:, place] = source_features(other_ref[...])
     sum_ref[...] = before_ref[...]
     add_pair_sums(
-        len(other_refs) * count, width, target_ref, feature_ref, moment_ref, sum_ref
+        len(other_refs) * count,
+        target_ref,
+        feature_ref,
+        moment_ref,
+        sum_ref,
+        slope_ref,
     )
     sums = sum_ref[...].T
     sums = sums[0:40] + sums[40:80] + sums[80:120]
@@ -179,32 +220,27 @@
     spread_low = (spread - spread_high.astype(f32)).astype(bf16)
     spread_both = jnp.concatenate([spread_high, spread_low], axis=0)
 
-    me = lax.axis_index("dom")
-    slot = owner_ref[...] ^ me
+    slot = owner_ref[...] ^ lax.axis_index("dom")
+    slot = (slot & 1) * (owners // 2) + (slot >> 1)
     node = lax.broadcasted_iota(jnp.int32, (16, count), 0)
     mine = slot * tiles + tile_ref[...] - (node >> 2)
     value = jnp.concatenate(values * 4, axis=0)
     value_high = value.astype(bf16).astype(f32)
     value_low = value - value_high
-    half = 8
-    per_group = tiles // half * half // 4
-    for group in range(owners * tiles // (4 * half)):
-        masks = [mine == 4 * (group * half + k) for k in range(half)]
-        picked_high = jnp.concatenate(
-            [jnp.where(m, value_high, 0.0).astype(bf16) for m in masks], axis=0
-        )
-        picked_low = jnp.concatenate(
-            [jnp.where(m, value_low, 0.0).astype(bf16) for m in masks], axis=0
-        )
-        both = lax.dot_general(
-            picked_high, spread_both, transposed_rhs, preferred_element_type=f32
-        )
-        low = lax.dot_general(
-            picked_low, spread_high, transposed_rhs, preferred_element_type=f32
-        )
-        grid_ref[group * 16 * half : (group + 1) * 16 * half, :] = (
-            both[:, 0:128] + both[:, 128:256] + low
-        )
+    total = owners * tiles * 4
+    for group in range(total // 16):
+        mask = mine == 4 * group
+        first = 16 * group
+        pick_ref[first : first + 16, :] = jnp.where(mask, value_high, 0.0).astype(bf16)
+        first = total + 16 * group
+        pick_ref[first : first + 16, :] = jnp.where(mask, value_low, 0.0).astype(bf16)
+    both = lax.dot_general(
+        pick_ref[...], spread_both, transposed_rhs, preferred_element_type=f32
+    )
+    both = both[:, 0:128] + both[:, 128:256]
+    both = both[:total] + both[total:]
+    keep_ref[...] = both[: total // 2]
+    send_ref[...] = both[total // 2 :]
 
 
 def vmem_specs(count):
@@ -228,6 +264,7 @@
         pltpu.VMEM((count, 48), bf16),
         pltpu.VMEM((48, n * count), bf16),
         pltpu.VMEM((128, n * count), bf16),
+        pltpu.VMEM((2 * count, width), bf16),
     ]
     params = pltpu.CompilerParams(vmem_limit_bytes=48 * 2**20)
     cost = lambda n: pl.CostEstimate(
@@ -236,7 +273,7 @@
         transcendentals=n * count * count,
     )
     own_sums = pl.pallas_call(
-        functools.partial(own_kernel, width),
+        own_kernel,
         out_shape=jax.ShapeDtypeStruct((count, 128), f32),
         in_specs=vmem_specs(2),
         out_specs=vmem_specs(1)[0],
@@ -245,15 +282,14 @@
         cost_estimate=cost(1),
         name="own_pairs",
     )(positions, sources)
-    velocity, grid = pl.pallas_call(
-        functools.partial(tail_kernel, width, tiles, owners),
-        out_shape=(
-            jax.ShapeDtypeStruct((3, count), f32),
-            jax.ShapeDtypeStruct((owners * tiles * 4, 128), f32),
-        ),
+    half = jax.ShapeDtypeStruct((owners * tiles * 2, 128), f32)
+    velocity, keep, send = pl.pallas_call(
+        functools.partial(tail_kernel, tiles, owners),
+        out_shape=(jax.ShapeDtypeStruct((3, count), f32), half, half),
         in_specs=vmem_specs(8 + len(others)),
-        out_specs=tuple(vmem_specs(2)),
-        scratch_shapes=scratch(len(others)) + [pltpu.VMEM((count, 128), f32)],
+        out_specs=tuple(vmem_specs(3)),
+        scratch_shapes=scratch(len(others))
+        + [pltpu.VMEM((count, 128), f32), pltpu.VMEM((owners * tiles * 8, count), bf16)],
         compiler_params=params,
         cost_estimate=cost(len(others)),
         name="other_pairs_and_deposit",
@@ -268,15 +304,10 @@
         owner_dom.reshape(1, count),
         *others,
     )
-    step = owners // 2
-    grid = grid.reshape(owners, tiles * 4, 128)
-    bit = 1
-    while bit < owners:
-        pairs = grid.reshape(-1, 2, *grid.shape[1:])
-        got = lax.ppermute(pairs[:, 1], "dom", [(i, i ^ bit) for i in range(owners)])
-        grid = pairs[:, 0] + got
-        bit *= 2
-    return velocity, grid.reshape(tiles, 4, 128)
+    exchange = lambda x, s: lax.ppermute(x, "dom", [(i, i ^ s) for i in range(owners)])
+    grid = (keep + exchange(send, 1)).reshape(owners // 2, tiles, 4, 128)
+    got = [exchange(grid[j], 2 * j) for j in range(owners // 2 - 1, 0, -1)]
+    return velocity, sum(got, grid[0])
 
 
 def solution(mesh):

time: 53.3 us -> 47.4 us (0.89)
  Pallas kernels: 34.9 us -> 30.4 us
  waiting for transfers between devices: 6.51 us -> 4.75 us
    pallas_call x2, Pallas kernels: 34.9 us -> 30.4 us  [the longest x1 23.3 us: on_device(): pl.pallas_call(functools.partial(tail_kernel, tiles, owners), out_shape=(...]
    ppermute x3 -> x4, waiting for transfers between devices: 6.51 us -> 4.74 us  [on_device(): lax.ppermute(x, 'dom', [(i, i ^ s) for i in range(owners)])]
    ppermute x3 -> x4, starting transfers between devices: 3.21 us -> 3.62 us  [on_device(): lax.ppermute(x, 'dom', [(i, i ^ s) for i in range(owners)])]
  transfers between devices with their start and end apart: 6 -> 7, of which waited for: 3 -> 4; matrix products, arithmetic and copies ran while one was open for 0% -> 0% of each run, Pallas kernels for 16% -> 15%
where the time goes in v2:
time: 47.4 us; the launch traced here: 47.2 us
  Pallas kernels  30.4 us (64%)
  starting transfers between devices  9.74 us (21%)
  waiting for transfers between devices  4.75 us (10%)
  other arithmetic  1.49 us (3%)
  between operations  0.78 us (2%)
    pallas_call x1, Pallas kernels, on_device(): pl.pallas_call(functools.partial(tail_kernel, tiles, owners), out_shape=(...  23.3 us
    pallas_call x1, Pallas kernels, on_device(): pl.pallas_call(own_kernel, out_shape=jax.ShapeDtypeStruct((count, 128), f...  7.1 us
    ppermute x3, starting transfers between devices, on_device(): lax.ppermute(sources, 'blk', [(i, (i + s) % blocks) for i in range(blocks)])  6.11 us
    ppermute x4, waiting for transfers between devices, on_device(): lax.ppermute(x, 'dom', [(i, i ^ s) for i in range(owners)])  4.74 us
    ppermute x4, starting transfers between devices, on_device(): lax.ppermute(x, 'dom', [(i, i ^ s) for i in range(owners)])  3.62 us
  transfers between devices with their start and end apart: 7, of which 4 were waited for; matrix products, arithmetic and copies ran while one was open for 0% of the time, Pallas kernels for 15%

profile of v2, /device:TPU:0, one launch (start us, length us, event | category | flops | bytes accessed | tf_op | source)
XLA Modules:
  0.0 47.2 jit_solution(386163305228708044)
XLA Ops:
  0.6 0.0 copy-start
  0.6 0.8 %pad_maximum_fusion.src_ref = f32[7,2048]{1,0:T(8,128)S(1)} fusion(f32[1,2048]{1,0:T(1,128)} %bitcast.26, f32[3,2048]{1,0:T(4,128)} %param.9, f32[3,2048]{1,0:T(4,128)} %pos_ref.3), kind=kLoop, calls=%fused_computation | loop fusion | flops 28672 | bytes 114688 | tf_op jit(solution)/shard_map/concatenate | solution.py:258
  1.5 0.0 copy-start.1
  1.5 0.0 copy-start.2
  1.5 0.0 copy-start.3
  1.5 0.0 copy-start.4
  1.5 0.0 copy-start.5
  1.6 5.1 %collective-permute-start.2 = (f32[7,2048]{1,0:T(8,128)S(1)}, f32[7,2048]{1,0:T(8,128)S(1)}, u32[]{:S(2)}, u32[]{:S(2)}) collective-permute-start(f32[7,2048]{1,0:T(8,128)S(1)} %pad_maximum_fusion.src_ref), channel_id=1, source_target_pairs={{0,3},{1,0},{2,1},{3,2},{4,7},{5,4},{6,5},{7,6},{8,11},{9,8},{10,9... | collective-permute-start | bytes 172040 | tf_op jit(solution)/shard_map/ppermute | solution.py:260
  6.7 0.0 collective-permute-start.1
  6.7 1.0 %collective-permute-start = (f32[7,2048]{1,0:T(8,128)S(1)}, f32[7,2048]{1,0:T(8,128)S(1)}, u32[]{:S(2)}, u32[]{:S(2)}) collective-permute-start(f32[7,2048]{1,0:T(8,128)S(1)} %pad_maximum_fusion.src_ref), channel_id=1, source_target_pairs={{0,1},{1,2},{2,3},{3,0},{4,5},{5,6},{6,7},{7,4},{8,9},{9,10},{10,1... | collective-permute-start | bytes 172040 | tf_op jit(solution)/shard_map/ppermute | solution.py:260
  7.7 0.0 copy-done
  7.7 7.1 %own_pairs.1.before_ref = f32[2048,128]{1,0:T(8,128)S(1)} custom-call(f32[3,2048]{1,0:T(4,128)S(1)} %copy-done, f32[7,2048]{1,0:T(8,128)S(1)} %pad_maximum_fusion.src_ref), custom_call_target="tpu_custom_call" | custom-call | flops 6442450944 | bytes 2097152 | tf_op jit(solution)/shard_map/own_pairs/pallas_call | solution.py:275
  14.8 0.0 collective-permute-done.2.refs_2_
  14.8 0.0 collective-permute-done.1.refs_1_
  14.8 0.0 collective-permute-done.refs_0_
  14.8 0.0 copy-done.1
  14.8 0.0 copy-done.2
  14.8 0.0 copy-done.3
  14.8 0.0 copy-done.4
  14.8 0.0 copy-done.5
  14.9 23.3 %other_pairs_and_deposit.1 = (f32[3,2048]{1,0:T(4,128)}, f32[256,128]{1,0:T(8,128)S(1)}, f32[256,128]{1,0:T(8,128)S(1)}) custom-call(f32[3,2048]{1,0:T(4,128)S(1)} %copy-done, f32[7,2048]{1,0:T(8,128)S(1)} %pad_maximum_fusion.src_ref, f32[2048,128]{1,0:T(8,128)S(1)} %own_pairs.1.before_ref, f32[1,2048]{1,0:T(1,128)S(1)} %bitcast.14, ...), custom_call_target="tpu_custom_call" | custom-call | flops 19327352832 | bytes 2097152 | tf_op jit(solution)/shard_map/other_pairs_and_deposit/pallas_call | solution.py:286
  38.2 0.1 collective-permute-start.3
  38.3 1.3 %collective-permute-done.3 = f32[256,128]{1,0:T(8,128)S(1)} collective-permute-done((f32[256,128]{1,0:T(8,128)S(1)}, f32[256,128]{1,0:T(8,128)S(1)}, u32[]{:S(2)}, u32[]{:S(2)}) %collective-permute-start.3) | collective-permute-done | bytes 131104 | tf_op jit(solution)/shard_map/ppermute | solution.py:307
  39.7 1.6 %collective-permute-start.6 = (f32[16,4,128]{2,1,0:T(4,128)S(1)}, f32[16,4,128]{2,1,0:T(4,128)S(1)}, u32[]{:S(2)}, u32[]{:S(2)}) collective-permute-start(f32[16,4,128]{2,1,0:T(4,128)S(1)} %bitcast.25), channel_id=1, source_target_pairs={{0,8},{4,12},{8,0},{12,4},{16,24},{20,28},{24,16},{28,20},{1,9},{5... | collective-permute-start | bytes 98312 | tf_op jit(solution)/shard_map/ppermute | solution.py:307
  41.2 1.5 %collective-permute-start.4 = (f32[16,4,128]{2,1,0:T(4,128)S(1)}, f32[16,4,128]{2,1,0:T(4,128)S(1)}, u32[]{:S(2)}, u32[]{:S(2)}) collective-permute-start(f32[16,4,128]{2,1,0:T(4,128)S(1)} %bitcast.24), channel_id=1, source_target_pairs={{0,24},{4,28},{8,16},{12,20},{16,8},{20,12},{24,0},{28,4},{1,25},{... | collective-permute-start | bytes 98312 | tf_op jit(solution)/shard_map/ppermute | solution.py:307
  42.7 0.5 %collective-permute-start.5 = (f32[16,4,128]{2,1,0:T(4,128)S(1)}, f32[16,4,128]{2,1,0:T(4,128)S(1)}, u32[]{:S(2)}, u32[]{:S(2)}) collective-permute-start(f32[16,4,128]{2,1,0:T(4,128)S(1)} %bitcast.23), channel_id=1, source_target_pairs={{0,16},{4,20},{8,24},{12,28},{16,0},{20,4},{24,8},{28,12},{1,17},{... | collective-permute-start | bytes 98312 | tf_op jit(solution)/shard_map/ppermute | solution.py:307
  43.2 0.4 collective-permute-done.6
  43.6 2.4 %collective-permute-done.4 = f32[16,4,128]{2,1,0:T(4,128)S(1)} collective-permute-done((f32[16,4,128]{2,1,0:T(4,128)S(1)}, f32[16,4,128]{2,1,0:T(4,128)S(1)}, u32[]{:S(2)}, u32[]{:S(2)}) %collective-permute-start.4) | collective-permute-done | bytes 32800 | tf_op jit(solution)/shard_map/ppermute | solution.py:307
  46.0 0.6 %collective-permute-done.5 = f32[16,4,128]{2,1,0:T(4,128)S(1)} collective-permute-done((f32[16,4,128]{2,1,0:T(4,128)S(1)}, f32[16,4,128]{2,1,0:T(4,128)S(1)}, u32[]{:S(2)}, u32[]{:S(2)}) %collective-permute-start.5) | collective-permute-done | bytes 32800 | tf_op jit(solution)/shard_map/ppermute | solution.py:307
  46.6 0.6 %add_add_fusion = f32[8,8,128]{2,1,0:T(8,128)} fusion(f32[8,8,128]{2,1,0:T(8,128)S(1)} %bitcast.19, f32[8,8,128]{2,1,0:T(8,128)S(1)} %bitcast.21, f32[8,8,128]{2,1,0:T(8,128)S(1)} %bitcast.18, f32[8,8,128]{2,1,0:T(8,128)S(1)} %bitcast.20), kind=kLoop, calls=%fused_computation.1 | loop fusion | flops 24576 | bytes 163840 | tf_op jit(solution)/shard_map/add | solution.py:310
  (2 shorter events, 0.0 us)
Async XLA Ops:
  0.6 7.0 %copy-start = (f32[3,2048]{1,0:T(4,128)S(1)}, f32[3,2048]{1,0:T(4,128)}, u32[]{:S(2)}) copy-start(f32[3,2048]{1,0:T(4,128)} %pos_ref.3) | copy-start | bytes 73732
  1.5 13.3 %copy-start.1 = (f32[3,2048]{1,0:T(4,128)S(1)}, f32[3,2048]{1,0:T(4,128)}, u32[]{:S(2)}) copy-start(f32[3,2048]{1,0:T(4,128)} %frac_ref.1) | copy-start | bytes 73732
  1.5 13.3 %copy-start.2 = (f32[2048]{0:T(1024)S(1)}, f32[2048]{0:T(1024)}, u32[]{:S(2)}) copy-start(f32[2048]{0:T(1024)} %param.11) | copy-start | bytes 24580
  1.5 13.3 %copy-start.3 = (s32[2048]{0:T(1024)S(1)}, s32[2048]{0:T(1024)}, u32[]{:S(2)}) copy-start(s32[2048]{0:T(1024)} %param.13) | copy-start | bytes 24580
  1.5 13.3 %copy-start.4 = (s32[2048]{0:T(1024)S(1)}, s32[2048]{0:T(1024)}, u32[]{:S(2)}) copy-start(s32[2048]{0:T(1024)} %param.14) | copy-start | bytes 24580
  1.5 13.3 %copy-start.5 = (s32[2048,1]{0,1:T(1,128)S(1)}, s32[2048,1]{0,1:T(1,128)}, u32[]{:S(2)}) copy-start(s32[2048,1]{0,1:T(1,128)} %param.15) | copy-start | bytes 24580
  1.6 13.2 %collective-permute-start.2 = (f32[7,2048]{1,0:T(8,128)S(1)}, f32[7,2048]{1,0:T(8,128)S(1)}, u32[]{:S(2)}, u32[]{:S(2)}) collective-permute-start(f32[7,2048]{1,0:T(8,128)S(1)} %pad_maximum_fusion.src_ref), channel_id=1, source_target_pairs={{0,3},{1,0},{2,1},{3,2},{4,7},{5,4},{6,5},{7,6},{8,11},{9,8},{10,9... | collective-permute-start | bytes 172040 | tf_op jit(solution)/shard_map/ppermute | solution.py:260
  6.7 8.1 %collective-permute-start.1 = (f32[7,2048]{1,0:T(8,128)S(1)}, f32[7,2048]{1,0:T(8,128)S(1)}, u32[]{:S(2)}, u32[]{:S(2)}) collective-permute-start(f32[7,2048]{1,0:T(8,128)S(1)} %pad_maximum_fusion.src_ref), channel_id=1, source_target_pairs={{0,2},{1,3},{2,0},{3,1},{4,6},{5,7},{6,4},{7,5},{8,10},{9,11},{10,... | collective-permute-start | bytes 172040 | tf_op jit(solution)/shard_map/ppermute | solution.py:260
  6.7 8.1 %collective-permute-start = (f32[7,2048]{1,0:T(8,128)S(1)}, f32[7,2048]{1,0:T(8,128)S(1)}, u32[]{:S(2)}, u32[]{:S(2)}) collective-permute-start(f32[7,2048]{1,0:T(8,128)S(1)} %pad_maximum_fusion.src_ref), channel_id=1, source_target_pairs={{0,1},{1,2},{2,3},{3,0},{4,5},{5,6},{6,7},{7,4},{8,9},{9,10},{10,1... | collective-permute-start | bytes 172040 | tf_op jit(solution)/shard_map/ppermute | solution.py:260
  38.2 1.4 %collective-permute-start.3 = (f32[256,128]{1,0:T(8,128)S(1)}, f32[256,128]{1,0:T(8,128)S(1)}, u32[]{:S(2)}, u32[]{:S(2)}) collective-permute-start(f32[256,128]{1,0:T(8,128)S(1)} %get-tuple-element.7), channel_id=1, source_target_pairs={{0,4},{4,0},{8,12},{12,8},{16,20},{20,16},{24,28},{28,24},{1,5},{5... | collective-permute-start | bytes 393224 | tf_op jit(solution)/shard_map/ppermute | solution.py:307
  39.7 4.0 %collective-permute-start.6 = (f32[16,4,128]{2,1,0:T(4,128)S(1)}, f32[16,4,128]{2,1,0:T(4,128)S(1)}, u32[]{:S(2)}, u32[]{:S(2)}) collective-permute-start(f32[16,4,128]{2,1,0:T(4,128)S(1)} %bitcast.25), channel_id=1, source_target_pairs={{0,8},{4,12},{8,0},{12,4},{16,24},{20,28},{24,16},{28,20},{1,9},{5... | collective-permute-start | bytes 98312 | tf_op jit(solution)/shard_map/ppermute | solution.py:307
  41.2 4.8 %collective-permute-start.4 = (f32[16,4,128]{2,1,0:T(4,128)S(1)}, f32[16,4,128]{2,1,0:T(4,128)S(1)}, u32[]{:S(2)}, u32[]{:S(2)}) collective-permute-start(f32[16,4,128]{2,1,0:T(4,128)S(1)} %bitcast.24), channel_id=1, source_target_pairs={{0,24},{4,28},{8,16},{12,20},{16,8},{20,12},{24,0},{28,4},{1,25},{... | collective-permute-start | bytes 98312 | tf_op jit(solution)/shard_map/ppermute | solution.py:307
  42.7 3.9 %collective-permute-start.5 = (f32[16,4,128]{2,1,0:T(4,128)S(1)}, f32[16,4,128]{2,1,0:T(4,128)S(1)}, u32[]{:S(2)}, u32[]{:S(2)}) collective-permute-start(f32[16,4,128]{2,1,0:T(4,128)S(1)} %bitcast.23), channel_id=1, source_target_pairs={{0,16},{4,20},{8,24},{12,28},{16,0},{20,4},{24,8},{28,12},{1,17},{... | collective-permute-start | bytes 98312 | tf_op jit(solution)/shard_map/ppermute | solution.py:307

commit v3 on v2

--- a/solution.py
+++ b/solution.py
@@ -58,18 +58,18 @@
     stack = jnp.concatenate([-2.0 * p for p in points] + [offset, one, zero, zero, zero], axis=0)
     high, middle, low = split3(stack)
     features = jnp.concatenate([high, high, middle, high, low, middle], axis=0)
-    base = jnp.concatenate(vortex + cross_rows(vortex, points) + [zero, zero], axis=0)
+    base = jnp.concatenate(vortex + cross_rows(vortex, points), axis=0)
     groups = jnp.concatenate([base] + [base * p for p in points] + [base * offset], axis=0)
     moments = jnp.concatenate(list(split3(groups)) + [jnp.zeros_like(base)], axis=0)
     return features.astype(bf16), moments.astype(bf16)
 
 
 def add_pair_sums(count, target_ref, feature_ref, moment_ref, sum_ref, slope_ref):
-    targets = sum_ref.shape[0]
+    targets = sum_ref.shape[1]
     width = slope_ref.shape[1]
     chunk = math.gcd(targets, 256)
     chunks = targets // chunk
-    lag = min(2, chunks)
+    lag = min(4, chunks)
 
     def produce(start, number):
         rows = slice(number * chunk, (number + 1) * chunk)
@@ -86,17 +86,17 @@
 
     def consume(start, number):
         both = lax.dot_general(
+            moment_ref[:, pl.ds(start, width)],
             slope_ref[2 * number * chunk : 2 * (number + 1) * chunk, :],
-            moment_ref[:, pl.ds(start, width)],
             transposed_rhs,
             preferred_element_type=f32,
         )
-        sum_ref[number * chunk : (number + 1) * chunk, :] += both[:chunk] + both[chunk:]
+        sum_ref[:, number * chunk : (number + 1) * chunk] += both[:, :chunk] + both[:, chunk:]
 
     first = 2 * (chunks - lag) * chunk
     slope_ref[first:, :] = jnp.zeros((2 * lag * chunk, width), bf16)
     steps = count // width
-    unroll = math.gcd(steps, 4)
+    unroll = math.gcd(steps, 8)
 
     def step(k, carry):
         for u in range(unroll):
@@ -132,7 +132,7 @@
 
 
 def combine(points, vortex, sums):
-    plain, by_x, by_y, by_z, by_offset = [sums[8 * k : 8 * k + 8] for k in range(5)]
+    plain, by_x, by_y, by_z, by_offset = [sums[6 * k : 6 * k + 6] for k in range(5)]
     kernel = (
         square_sum(points) * plain
         + by_offset
@@ -193,8 +193,7 @@
         sum_ref,
         slope_ref,
     )
-    sums = sum_ref[...].T
-    sums = sums[0:40] + sums[40:80] + sums[80:120]
+    sums = sum_ref[0:30, :] + sum_ref[30:60, :] + sum_ref[60:90, :]
     vortex = rows_of(src_ref[...], 3, 3)
     velocity, stretch = combine(points, vortex, sums)
     velocity_ref[...] = jnp.concatenate(velocity, axis=0)
@@ -254,7 +253,7 @@
     tiles = count // 128
     owners = lax.axis_size("dom")
     blocks = lax.axis_size("blk")
-    width = math.gcd(count, 512)
+    width = math.gcd(count, 256)
     sources = jnp.concatenate([positions, strength, core_radius[None]], axis=0)
     others = [
         lax.ppermute(sources, "blk", [(i, (i + s) % blocks) for i in range(blocks)])
@@ -263,7 +262,7 @@
     scratch = lambda n: [
         pltpu.VMEM((count, 48), bf16),
         pltpu.VMEM((48, n * count), bf16),
-        pltpu.VMEM((128, n * count), bf16),
+        pltpu.VMEM((96, n * count), bf16),
         pltpu.VMEM((2 * count, width), bf16),
     ]
     params = pltpu.CompilerParams(vmem_limit_bytes=48 * 2**20)
@@ -274,7 +273,7 @@
     )
     own_sums = pl.pallas_call(
         own_kernel,
-        out_shape=jax.ShapeDtypeStruct((count, 128), f32),
+        out_shape=jax.ShapeDtypeStruct((96, count), f32),
         in_specs=vmem_specs(2),
         out_specs=vmem_specs(1)[0],
         scratch_shapes=scratch(1),
@@ -289,7 +288,7 @@
         in_specs=vmem_specs(8 + len(others)),
         out_specs=tuple(vmem_specs(3)),
         scratch_shapes=scratch(len(others))
-        + [pltpu.VMEM((count, 128), f32), pltpu.VMEM((owners * tiles * 8, count), bf16)],
+        + [pltpu.VMEM((96, count), f32), pltpu.VMEM((owners * tiles * 8, count), bf16)],
         compiler_params=params,
         cost_estimate=cost(len(others)),
         name="other_pairs_and_deposit",

time: 47.4 us -> 45.5 us (0.960)
  Pallas kernels: 30.4 us -> 28.5 us
    pallas_call x1, Pallas kernels: 23.3 us -> 21.9 us  [on_device(): pl.pallas_call(functools.partial(tail_kernel, tiles, owners), out_shape=(...]
where the time goes in v3:
time: 45.5 us; the launch traced here: 45.3 us
  Pallas kernels  28.5 us (63%)
  starting transfers between devices  9.67 us (21%)
  waiting for transfers between devices  4.76 us (10%)
  other arithmetic  1.49 us (3%)
  between operations  0.77 us (2%)
    pallas_call x1, Pallas kernels, on_device(): pl.pallas_call(functools.partial(tail_kernel, tiles, owners), out_shape=(...  21.9 us
    pallas_call x1, Pallas kernels, on_device(): pl.pallas_call(own_kernel, out_shape=jax.ShapeDtypeStruct((96, count), f3...  6.66 us
    ppermute x3, starting transfers between devices, on_device(): lax.ppermute(sources, 'blk', [(i, (i + s) % blocks) for i in range(blocks)])  6.11 us
    ppermute x4, waiting for transfers between devices, on_device(): lax.ppermute(x, 'dom', [(i, i ^ s) for i in range(owners)])  4.75 us
    ppermute x4, starting transfers between devices, on_device(): lax.ppermute(x, 'dom', [(i, i ^ s) for i in range(owners)])  3.56 us
  transfers between devices with their start and end apart: 7, of which 4 were waited for; matrix products, arithmetic and copies ran while one was open for 0% of the time, Pallas kernels for 15%

profile of v3, /device:TPU:0, one launch (start us, length us, event | category | flops | bytes accessed | tf_op | source)
XLA Modules:
  0.0 45.3 jit_solution(5503695545308575450)
XLA Ops:
  0.6 0.0 copy-start
  0.6 0.8 %pad_maximum_fusion.src_ref = f32[7,2048]{1,0:T(8,128)S(1)} fusion(f32[1,2048]{1,0:T(1,128)} %bitcast.26, f32[3,2048]{1,0:T(4,128)} %param.9, f32[3,2048]{1,0:T(4,128)} %pos_ref.3), kind=kLoop, calls=%fused_computation | loop fusion | flops 28672 | bytes 114688 | tf_op jit(solution)/shard_map/concatenate | solution.py:257
  1.5 0.0 copy-start.1
  1.5 0.0 copy-start.2
  1.5 0.0 copy-start.3
  1.5 0.0 copy-start.4
  1.5 0.0 copy-start.5
  1.6 5.1 %collective-permute-start.2 = (f32[7,2048]{1,0:T(8,128)S(1)}, f32[7,2048]{1,0:T(8,128)S(1)}, u32[]{:S(2)}, u32[]{:S(2)}) collective-permute-start(f32[7,2048]{1,0:T(8,128)S(1)} %pad_maximum_fusion.src_ref), channel_id=1, source_target_pairs={{0,3},{1,0},{2,1},{3,2},{4,7},{5,4},{6,5},{7,6},{8,11},{9,8},{10,9... | collective-permute-start | bytes 172040 | tf_op jit(solution)/shard_map/ppermute | solution.py:259
  6.7 0.0 collective-permute-start.1
  6.7 1.0 %collective-permute-start = (f32[7,2048]{1,0:T(8,128)S(1)}, f32[7,2048]{1,0:T(8,128)S(1)}, u32[]{:S(2)}, u32[]{:S(2)}) collective-permute-start(f32[7,2048]{1,0:T(8,128)S(1)} %pad_maximum_fusion.src_ref), channel_id=1, source_target_pairs={{0,1},{1,2},{2,3},{3,0},{4,5},{5,6},{6,7},{7,4},{8,9},{9,10},{10,1... | collective-permute-start | bytes 172040 | tf_op jit(solution)/shard_map/ppermute | solution.py:259
  7.7 0.0 copy-done
  7.7 6.7 %own_pairs.1.before_ref = f32[96,2048]{1,0:T(8,128)S(1)} custom-call(f32[3,2048]{1,0:T(4,128)S(1)} %copy-done, f32[7,2048]{1,0:T(8,128)S(1)} %pad_maximum_fusion.src_ref), custom_call_target="tpu_custom_call" | custom-call | flops 6442450944 | bytes 2097152 | tf_op jit(solution)/shard_map/own_pairs/pallas_call | solution.py:274
  14.3 0.0 collective-permute-done.2.refs_2_
  14.3 0.0 collective-permute-done.1.refs_1_
  14.4 0.0 collective-permute-done.refs_0_
  14.4 0.0 copy-done.1
  14.4 0.0 copy-done.2
  14.4 0.0 copy-done.3
  14.4 0.0 copy-done.4
  14.4 0.0 copy-done.5
  14.4 21.9 %other_pairs_and_deposit.1 = (f32[3,2048]{1,0:T(4,128)}, f32[256,128]{1,0:T(8,128)S(1)}, f32[256,128]{1,0:T(8,128)S(1)}) custom-call(f32[3,2048]{1,0:T(4,128)S(1)} %copy-done, f32[7,2048]{1,0:T(8,128)S(1)} %pad_maximum_fusion.src_ref, f32[96,2048]{1,0:T(8,128)S(1)} %own_pairs.1.before_ref, f32[1,2048]{1,0:T(1,128)S(1)} %bitcast.14, f32[3,2048]{1,0:T(4,128)S(1)} %copy-done.1, ...), custom_call_target="tpu_custom_call" | custom-call | flops 19327352832 | bytes 2097152 | tf_op jit(solution)/shard_map/other_pairs_and_deposit/pallas_call | solution.py:285
  36.3 0.0 collective-permute-start.3
  36.3 1.3 %collective-permute-done.3 = f32[256,128]{1,0:T(8,128)S(1)} collective-permute-done((f32[256,128]{1,0:T(8,128)S(1)}, f32[256,128]{1,0:T(8,128)S(1)}, u32[]{:S(2)}, u32[]{:S(2)}) %collective-permute-start.3) | collective-permute-done | bytes 131104 | tf_op jit(solution)/shard_map/ppermute | solution.py:306
  37.7 1.6 %collective-permute-start.6 = (f32[16,4,128]{2,1,0:T(4,128)S(1)}, f32[16,4,128]{2,1,0:T(4,128)S(1)}, u32[]{:S(2)}, u32[]{:S(2)}) collective-permute-start(f32[16,4,128]{2,1,0:T(4,128)S(1)} %bitcast.25), channel_id=1, source_target_pairs={{0,8},{4,12},{8,0},{12,4},{16,24},{20,28},{24,16},{28,20},{1,9},{5... | collective-permute-start | bytes 98312 | tf_op jit(solution)/shard_map/ppermute | solution.py:306
  39.3 1.5 %collective-permute-start.4 = (f32[16,4,128]{2,1,0:T(4,128)S(1)}, f32[16,4,128]{2,1,0:T(4,128)S(1)}, u32[]{:S(2)}, u32[]{:S(2)}) collective-permute-start(f32[16,4,128]{2,1,0:T(4,128)S(1)} %bitcast.24), channel_id=1, source_target_pairs={{0,24},{4,28},{8,16},{12,20},{16,8},{20,12},{24,0},{28,4},{1,25},{... | collective-permute-start | bytes 98312 | tf_op jit(solution)/shard_map/ppermute | solution.py:306
  40.7 0.5 %collective-permute-start.5 = (f32[16,4,128]{2,1,0:T(4,128)S(1)}, f32[16,4,128]{2,1,0:T(4,128)S(1)}, u32[]{:S(2)}, u32[]{:S(2)}) collective-permute-start(f32[16,4,128]{2,1,0:T(4,128)S(1)} %bitcast.23), channel_id=1, source_target_pairs={{0,16},{4,20},{8,24},{12,28},{16,0},{20,4},{24,8},{28,12},{1,17},{... | collective-permute-start | bytes 98312 | tf_op jit(solution)/shard_map/ppermute | solution.py:306
  41.3 0.4 collective-permute-done.6
  41.7 2.4 %collective-permute-done.4 = f32[16,4,128]{2,1,0:T(4,128)S(1)} collective-permute-done((f32[16,4,128]{2,1,0:T(4,128)S(1)}, f32[16,4,128]{2,1,0:T(4,128)S(1)}, u32[]{:S(2)}, u32[]{:S(2)}) %collective-permute-start.4) | collective-permute-done | bytes 32800 | tf_op jit(solution)/shard_map/ppermute | solution.py:306
  44.1 0.6 %collective-permute-done.5 = f32[16,4,128]{2,1,0:T(4,128)S(1)} collective-permute-done((f32[16,4,128]{2,1,0:T(4,128)S(1)}, f32[16,4,128]{2,1,0:T(4,128)S(1)}, u32[]{:S(2)}, u32[]{:S(2)}) %collective-permute-start.5) | collective-permute-done | bytes 32800 | tf_op jit(solution)/shard_map/ppermute | solution.py:306
  44.7 0.6 %add_add_fusion = f32[8,8,128]{2,1,0:T(8,128)} fusion(f32[8,8,128]{2,1,0:T(8,128)S(1)} %bitcast.19, f32[8,8,128]{2,1,0:T(8,128)S(1)} %bitcast.21, f32[8,8,128]{2,1,0:T(8,128)S(1)} %bitcast.18, f32[8,8,128]{2,1,0:T(8,128)S(1)} %bitcast.20), kind=kLoop, calls=%fused_computation.1 | loop fusion | flops 24576 | bytes 163840 | tf_op jit(solution)/shard_map/add | solution.py:309
  (2 shorter events, 0.0 us)
Async XLA Ops:
  0.6 7.0 %copy-start = (f32[3,2048]{1,0:T(4,128)S(1)}, f32[3,2048]{1,0:T(4,128)}, u32[]{:S(2)}) copy-start(f32[3,2048]{1,0:T(4,128)} %pos_ref.3) | copy-start | bytes 73732
  1.5 12.9 %copy-start.1 = (f32[3,2048]{1,0:T(4,128)S(1)}, f32[3,2048]{1,0:T(4,128)}, u32[]{:S(2)}) copy-start(f32[3,2048]{1,0:T(4,128)} %frac_ref.1) | copy-start | bytes 73732
  1.5 12.9 %copy-start.2 = (f32[2048]{0:T(1024)S(1)}, f32[2048]{0:T(1024)}, u32[]{:S(2)}) copy-start(f32[2048]{0:T(1024)} %param.11) | copy-start | bytes 24580
  1.5 12.9 %copy-start.3 = (s32[2048]{0:T(1024)S(1)}, s32[2048]{0:T(1024)}, u32[]{:S(2)}) copy-start(s32[2048]{0:T(1024)} %param.13) | copy-start | bytes 24580
  1.5 12.9 %copy-start.4 = (s32[2048]{0:T(1024)S(1)}, s32[2048]{0:T(1024)}, u32[]{:S(2)}) copy-start(s32[2048]{0:T(1024)} %param.14) | copy-start | bytes 24580
  1.5 12.9 %copy-start.5 = (s32[2048,1]{0,1:T(1,128)S(1)}, s32[2048,1]{0,1:T(1,128)}, u32[]{:S(2)}) copy-start(s32[2048,1]{0,1:T(1,128)} %param.15) | copy-start | bytes 24580
  1.6 12.8 %collective-permute-start.2 = (f32[7,2048]{1,0:T(8,128)S(1)}, f32[7,2048]{1,0:T(8,128)S(1)}, u32[]{:S(2)}, u32[]{:S(2)}) collective-permute-start(f32[7,2048]{1,0:T(8,128)S(1)} %pad_maximum_fusion.src_ref), channel_id=1, source_target_pairs={{0,3},{1,0},{2,1},{3,2},{4,7},{5,4},{6,5},{7,6},{8,11},{9,8},{10,9... | collective-permute-start | bytes 172040 | tf_op jit(solution)/shard_map/ppermute | solution.py:259
  6.7 7.7 %collective-permute-start.1 = (f32[7,2048]{1,0:T(8,128)S(1)}, f32[7,2048]{1,0:T(8,128)S(1)}, u32[]{:S(2)}, u32[]{:S(2)}) collective-permute-start(f32[7,2048]{1,0:T(8,128)S(1)} %pad_maximum_fusion.src_ref), channel_id=1, source_target_pairs={{0,2},{1,3},{2,0},{3,1},{4,6},{5,7},{6,4},{7,5},{8,10},{9,11},{10,... | collective-permute-start | bytes 172040 | tf_op jit(solution)/shard_map/ppermute | solution.py:259
  6.7 7.7 %collective-permute-start = (f32[7,2048]{1,0:T(8,128)S(1)}, f32[7,2048]{1,0:T(8,128)S(1)}, u32[]{:S(2)}, u32[]{:S(2)}) collective-permute-start(f32[7,2048]{1,0:T(8,128)S(1)} %pad_maximum_fusion.src_ref), channel_id=1, source_target_pairs={{0,1},{1,2},{2,3},{3,0},{4,5},{5,6},{6,7},{7,4},{8,9},{9,10},{10,1... | collective-permute-start | bytes 172040 | tf_op jit(solution)/shard_map/ppermute | solution.py:259
  36.3 1.3 %collective-permute-start.3 = (f32[256,128]{1,0:T(8,128)S(1)}, f32[256,128]{1,0:T(8,128)S(1)}, u32[]{:S(2)}, u32[]{:S(2)}) collective-permute-start(f32[256,128]{1,0:T(8,128)S(1)} %get-tuple-element.7), channel_id=1, source_target_pairs={{0,4},{4,0},{8,12},{12,8},{16,20},{20,16},{24,28},{28,24},{1,5},{5... | collective-permute-start | bytes 393224 | tf_op jit(solution)/shard_map/ppermute | solution.py:306
  37.7 4.0 %collective-permute-start.6 = (f32[16,4,128]{2,1,0:T(4,128)S(1)}, f32[16,4,128]{2,1,0:T(4,128)S(1)}, u32[]{:S(2)}, u32[]{:S(2)}) collective-permute-start(f32[16,4,128]{2,1,0:T(4,128)S(1)} %bitcast.25), channel_id=1, source_target_pairs={{0,8},{4,12},{8,0},{12,4},{16,24},{20,28},{24,16},{28,20},{1,9},{5... | collective-permute-start | bytes 98312 | tf_op jit(solution)/shard_map/ppermute | solution.py:306
  39.3 4.8 %collective-permute-start.4 = (f32[16,4,128]{2,1,0:T(4,128)S(1)}, f32[16,4,128]{2,1,0:T(4,128)S(1)}, u32[]{:S(2)}, u32[]{:S(2)}) collective-permute-start(f32[16,4,128]{2,1,0:T(4,128)S(1)} %bitcast.24), channel_id=1, source_target_pairs={{0,24},{4,28},{8,16},{12,20},{16,8},{20,12},{24,0},{28,4},{1,25},{... | collective-permute-start | bytes 98312 | tf_op jit(solution)/shard_map/ppermute | solution.py:306
  40.7 3.9 %collective-permute-start.5 = (f32[16,4,128]{2,1,0:T(4,128)S(1)}, f32[16,4,128]{2,1,0:T(4,128)S(1)}, u32[]{:S(2)}, u32[]{:S(2)}) collective-permute-start(f32[16,4,128]{2,1,0:T(4,128)S(1)} %bitcast.23), channel_id=1, source_target_pairs={{0,16},{4,20},{8,24},{12,28},{16,0},{20,4},{24,8},{28,12},{1,17},{... | collective-permute-start | bytes 98312 | tf_op jit(solution)/shard_map/ppermute | solution.py:306

commit v4 on v3

--- a/solution.py
+++ b/solution.py
@@ -61,42 +61,38 @@
     base = jnp.concatenate(vortex + cross_rows(vortex, points), axis=0)
     groups = jnp.concatenate([base] + [base * p for p in points] + [base * offset], axis=0)
     moments = jnp.concatenate(list(split3(groups)) + [jnp.zeros_like(base)], axis=0)
-    return features.astype(bf16), moments.astype(bf16)
-
-
-def add_pair_sums(count, target_ref, feature_ref, moment_ref, sum_ref, slope_ref):
+    return features.T.astype(bf16), moments.astype(bf16)
+
+
+def add_pair_sums(lag, unroll, target_ref, feature_ref, moment_ref, sum_ref, slope_ref):
     targets = sum_ref.shape[1]
-    width = slope_ref.shape[1]
-    chunk = math.gcd(targets, 256)
-    chunks = targets // chunk
-    lag = min(4, chunks)
+    slots, chunk, width = slope_ref.shape
+    chunk = chunk // 2
+    chunks = feature_ref.shape[0] // chunk
+    tiles = targets // width
+    lag = min(lag, chunks)
 
     def produce(start, number):
-        rows = slice(number * chunk, (number + 1) * chunk)
         square = jnp.dot(
-            target_ref[rows, :], feature_ref[:, pl.ds(start, width)], preferred_element_type=f32
+            feature_ref[number * chunk : (number + 1) * chunk, :],
+            target_ref[:, pl.ds(start, width)],
+            preferred_element_type=f32,
         )
         inverse = lax.rsqrt(square)
         inverse2 = inverse * inverse
         slope = inverse2 * inverse2 * inverse
         high = slope.astype(bf16)
-        first = 2 * number * chunk
-        slope_ref[first : first + chunk, :] = high
-        slope_ref[first + chunk : first + 2 * chunk, :] = (slope - high.astype(f32)).astype(bf16)
+        slope_ref[number % slots, :chunk] = high
+        slope_ref[number % slots, chunk:] = (slope - high.astype(f32)).astype(bf16)
 
     def consume(start, number):
-        both = lax.dot_general(
-            moment_ref[:, pl.ds(start, width)],
-            slope_ref[2 * number * chunk : 2 * (number + 1) * chunk, :],
-            transposed_rhs,
-            preferred_element_type=f32,
-        )
-        sum_ref[:, number * chunk : (number + 1) * chunk] += both[:, :chunk] + both[:, chunk:]
-
-    first = 2 * (chunks - lag) * chunk
-    slope_ref[first:, :] = jnp.zeros((2 * lag * chunk, width), bf16)
-    steps = count // width
-    unroll = math.gcd(steps, 8)
+        moments = moment_ref[:, number * chunk : (number + 1) * chunk]
+        sum_ref[:, pl.ds(start, width)] += jnp.dot(
+            moments, slope_ref[number % slots, :chunk], preferred_element_type=f32
+        ) + jnp.dot(moments, slope_ref[number % slots, chunk:], preferred_element_type=f32)
+
+    for number in range(chunks - lag, chunks):
+        slope_ref[number % slots] = jnp.zeros(slope_ref.shape[1:], bf16)
 
     def step(k, carry):
         for u in range(unroll):
@@ -110,24 +106,20 @@
                 produce(start, number)
         return carry
 
-    lax.fori_loop(0, steps // unroll, step, 0)
+    lax.fori_loop(0, tiles // unroll, step, 0)
     for number in range(chunks - lag, chunks):
-        consume((steps - 1) * width, number)
+        consume((tiles - 1) * width, number)
 
 
 def own_kernel(
     pos_ref, src_ref, sum_ref, target_ref, feature_ref, moment_ref, slope_ref
 ):
-    target_ref[...] = target_features(rows_of(pos_ref[...], 0, 3)).T.astype(bf16)
+    target_ref[...] = target_features(rows_of(pos_ref[...], 0, 3)).astype(bf16)
     feature_ref[...], moment_ref[...] = source_features(src_ref[...])
     sum_ref[...] = jnp.zeros_like(sum_ref)
+    tiles = sum_ref.shape[1] // slope_ref.shape[2]
     add_pair_sums(
-        src_ref.shape[1],
-        target_ref,
-        feature_ref,
-        moment_ref,
-        sum_ref,
-        slope_ref,
+        4, math.gcd(tiles, 8), target_ref, feature_ref, moment_ref, sum_ref, slope_ref
     )
 
 
@@ -180,13 +172,14 @@
     target_ref, feature_ref, moment_ref, slope_ref, sum_ref, pick_ref = refs
     count = src_ref.shape[1]
     points = rows_of(pos_ref[...], 0, 3)
-    target_ref[...] = target_features(points).T.astype(bf16)
+    target_ref[...] = target_features(points).astype(bf16)
     for k, other_ref in enumerate(other_refs):
         place = slice(k * count, (k + 1) * count)
-        feature_ref[:, place], moment_ref[:, place] = source_features(other_ref[...])
+        feature_ref[place], moment_ref[:, place] = source_features(other_ref[...])
     sum_ref[...] = before_ref[...]
     add_pair_sums(
-        len(other_refs) * count,
+        8,
+        math.gcd(count // slope_ref.shape[2], 2),
         target_ref,
         feature_ref,
         moment_ref,
@@ -260,10 +253,10 @@
         for s in range(1, blocks)
     ]
     scratch = lambda n: [
-        pltpu.VMEM((count, 48), bf16),
-        pltpu.VMEM((48, n * count), bf16),
+        pltpu.VMEM((48, count), bf16),
+        pltpu.VMEM((n * count, 48), bf16),
         pltpu.VMEM((96, n * count), bf16),
-        pltpu.VMEM((2 * count, width), bf16),
+        pltpu.VMEM((min(8, count // width), 2 * width, width), bf16),
     ]
     params = pltpu.CompilerParams(vmem_limit_bytes=48 * 2**20)
     cost = lambda n: pl.CostEstimate(

time: 45.5 us -> 42 us (0.923)
  Pallas kernels: 28.5 us -> 24.7 us
    pallas_call x1, Pallas kernels: 21.9 us -> 19.7 us  [on_device(): pl.pallas_call(functools.partial(tail_kernel, tiles, owners), out_shape=(...]
    pallas_call x1, Pallas kernels: 6.66 us -> 5.07 us  [on_device(): pl.pallas_call(own_kernel, out_shape=jax.ShapeDtypeStruct((96, count), f3...]
  transfers between devices with their start and end apart: 7 -> 7, of which waited for: 4 -> 5; matrix products, arithmetic and copies ran while one was open for 0% -> 0% of each run, Pallas kernels for 15% -> 12%
where the time goes in v4:
time: 42 us; the launch traced here: 41.8 us
  Pallas kernels  24.7 us (59%)
  starting transfers between devices  9.67 us (23%)
  waiting for transfers between devices  5.12 us (12%)
  other arithmetic  1.49 us (4%)
  between operations  0.74 us (2%)
    pallas_call x1, Pallas kernels, on_device(): pl.pallas_call(functools.partial(tail_kernel, tiles, owners), out_shape=(...  19.7 us
    ppermute x3, starting transfers between devices, on_device(): lax.ppermute(sources, 'blk', [(i, (i + s) % blocks) for i in range(blocks)])  6.11 us
    pallas_call x1, Pallas kernels, on_device(): pl.pallas_call(own_kernel, out_shape=jax.ShapeDtypeStruct((96, count), f3...  5.07 us
    ppermute x4, waiting for transfers between devices, on_device(): lax.ppermute(x, 'dom', [(i, i ^ s) for i in range(owners)])  4.75 us
    ppermute x4, starting transfers between devices, on_device(): lax.ppermute(x, 'dom', [(i, i ^ s) for i in range(owners)])  3.56 us
    concatenate x1, other arithmetic, on_device(): sources = jnp.concatenate([positions, strength, core_radius[None]], axis=0)  0.85 us
  transfers between devices with their start and end apart: 7, of which 5 were waited for; matrix products, arithmetic and copies ran while one was open for 0% of the time, Pallas kernels for 12%

profile of v4, /device:TPU:0, one launch (start us, length us, event | category | flops | bytes accessed | tf_op | source)
XLA Modules:
  0.0 41.8 jit_solution(8309426487684765502)
XLA Ops:
  0.6 0.0 copy-start
  0.6 0.8 %pad_maximum_fusion.src_ref = f32[7,2048]{1,0:T(8,128)S(1)} fusion(f32[1,2048]{1,0:T(1,128)} %bitcast.26, f32[3,2048]{1,0:T(4,128)} %param.9, f32[3,2048]{1,0:T(4,128)} %pos_ref.3), kind=kLoop, calls=%fused_computation | loop fusion | flops 28672 | bytes 114688 | tf_op jit(solution)/shard_map/concatenate | solution.py:250
  1.5 0.0 copy-start.1
  1.5 0.0 copy-start.2
  1.5 0.0 copy-start.3
  1.5 0.0 copy-start.4
  1.5 0.0 copy-start.5
  1.6 5.1 %collective-permute-start.2 = (f32[7,2048]{1,0:T(8,128)S(1)}, f32[7,2048]{1,0:T(8,128)S(1)}, u32[]{:S(2)}, u32[]{:S(2)}) collective-permute-start(f32[7,2048]{1,0:T(8,128)S(1)} %pad_maximum_fusion.src_ref), channel_id=1, source_target_pairs={{0,3},{1,0},{2,1},{3,2},{4,7},{5,4},{6,5},{7,6},{8,11},{9,8},{10,9... | collective-permute-start | bytes 172040 | tf_op jit(solution)/shard_map/ppermute | solution.py:252
  6.7 0.0 collective-permute-start.1
  6.7 1.0 %collective-permute-start = (f32[7,2048]{1,0:T(8,128)S(1)}, f32[7,2048]{1,0:T(8,128)S(1)}, u32[]{:S(2)}, u32[]{:S(2)}) collective-permute-start(f32[7,2048]{1,0:T(8,128)S(1)} %pad_maximum_fusion.src_ref), channel_id=1, source_target_pairs={{0,1},{1,2},{2,3},{3,0},{4,5},{5,6},{6,7},{7,4},{8,9},{9,10},{10,1... | collective-permute-start | bytes 172040 | tf_op jit(solution)/shard_map/ppermute | solution.py:252
  7.7 0.0 copy-done
  7.7 5.1 %own_pairs.1.before_ref = f32[96,2048]{1,0:T(8,128)S(1)} custom-call(f32[3,2048]{1,0:T(4,128)S(1)} %copy-done, f32[7,2048]{1,0:T(8,128)S(1)} %pad_maximum_fusion.src_ref), custom_call_target="tpu_custom_call" | custom-call | flops 6442450944 | bytes 2097152 | tf_op jit(solution)/shard_map/own_pairs/pallas_call | solution.py:267
  12.7 0.0 collective-permute-done.2.refs_2_
  12.8 0.4 collective-permute-done.1.refs_1_
  13.1 0.0 collective-permute-done.refs_0_
  13.1 0.0 copy-done.1
  13.1 0.0 copy-done.2
  13.1 0.0 copy-done.3
  13.1 0.0 copy-done.4
  13.2 0.0 copy-done.5
  13.2 19.7 %other_pairs_and_deposit.1 = (f32[3,2048]{1,0:T(4,128)}, f32[256,128]{1,0:T(8,128)S(1)}, f32[256,128]{1,0:T(8,128)S(1)}) custom-call(f32[3,2048]{1,0:T(4,128)S(1)} %copy-done, f32[7,2048]{1,0:T(8,128)S(1)} %pad_maximum_fusion.src_ref, f32[96,2048]{1,0:T(8,128)S(1)} %own_pairs.1.before_ref, f32[1,2048]{1,0:T(1,128)S(1)} %bitcast.14, f32[3,2048]{1,0:T(4,128)S(1)} %copy-done.1, ...), custom_call_target="tpu_custom_call" | custom-call | flops 19327352832 | bytes 2097152 | tf_op jit(solution)/shard_map/other_pairs_and_deposit/pallas_call | solution.py:278
  32.8 0.0 collective-permute-start.3
  32.8 1.3 %collective-permute-done.3 = f32[256,128]{1,0:T(8,128)S(1)} collective-permute-done((f32[256,128]{1,0:T(8,128)S(1)}, f32[256,128]{1,0:T(8,128)S(1)}, u32[]{:S(2)}, u32[]{:S(2)}) %collective-permute-start.3) | collective-permute-done | bytes 131104 | tf_op jit(solution)/shard_map/ppermute | solution.py:299
  34.2 1.6 %collective-permute-start.6 = (f32[16,4,128]{2,1,0:T(4,128)S(1)}, f32[16,4,128]{2,1,0:T(4,128)S(1)}, u32[]{:S(2)}, u32[]{:S(2)}) collective-permute-start(f32[16,4,128]{2,1,0:T(4,128)S(1)} %bitcast.25), channel_id=1, source_target_pairs={{0,8},{4,12},{8,0},{12,4},{16,24},{20,28},{24,16},{28,20},{1,9},{5... | collective-permute-start | bytes 98312 | tf_op jit(solution)/shard_map/ppermute | solution.py:299
  35.8 1.5 %collective-permute-start.4 = (f32[16,4,128]{2,1,0:T(4,128)S(1)}, f32[16,4,128]{2,1,0:T(4,128)S(1)}, u32[]{:S(2)}, u32[]{:S(2)}) collective-permute-start(f32[16,4,128]{2,1,0:T(4,128)S(1)} %bitcast.24), channel_id=1, source_target_pairs={{0,24},{4,28},{8,16},{12,20},{16,8},{20,12},{24,0},{28,4},{1,25},{... | collective-permute-start | bytes 98312 | tf_op jit(solution)/shard_map/ppermute | solution.py:299
  37.3 0.5 %collective-permute-start.5 = (f32[16,4,128]{2,1,0:T(4,128)S(1)}, f32[16,4,128]{2,1,0:T(4,128)S(1)}, u32[]{:S(2)}, u32[]{:S(2)}) collective-permute-start(f32[16,4,128]{2,1,0:T(4,128)S(1)} %bitcast.23), channel_id=1, source_target_pairs={{0,16},{4,20},{8,24},{12,28},{16,0},{20,4},{24,8},{28,12},{1,17},{... | collective-permute-start | bytes 98312 | tf_op jit(solution)/shard_map/ppermute | solution.py:299
  37.8 0.4 %collective-permute-done.6 = f32[16,4,128]{2,1,0:T(4,128)S(1)} collective-permute-done((f32[16,4,128]{2,1,0:T(4,128)S(1)}, f32[16,4,128]{2,1,0:T(4,128)S(1)}, u32[]{:S(2)}, u32[]{:S(2)}) %collective-permute-start.6) | collective-permute-done | bytes 32800 | tf_op jit(solution)/shard_map/ppermute | solution.py:299
  38.2 2.4 %collective-permute-done.4 = f32[16,4,128]{2,1,0:T(4,128)S(1)} collective-permute-done((f32[16,4,128]{2,1,0:T(4,128)S(1)}, f32[16,4,128]{2,1,0:T(4,128)S(1)}, u32[]{:S(2)}, u32[]{:S(2)}) %collective-permute-start.4) | collective-permute-done | bytes 32800 | tf_op jit(solution)/shard_map/ppermute | solution.py:299
  40.6 0.6 %collective-permute-done.5 = f32[16,4,128]{2,1,0:T(4,128)S(1)} collective-permute-done((f32[16,4,128]{2,1,0:T(4,128)S(1)}, f32[16,4,128]{2,1,0:T(4,128)S(1)}, u32[]{:S(2)}, u32[]{:S(2)}) %collective-permute-start.5) | collective-permute-done | bytes 32800 | tf_op jit(solution)/shard_map/ppermute | solution.py:299
  41.2 0.6 %add_add_fusion = f32[8,8,128]{2,1,0:T(8,128)} fusion(f32[8,8,128]{2,1,0:T(8,128)S(1)} %bitcast.19, f32[8,8,128]{2,1,0:T(8,128)S(1)} %bitcast.21, f32[8,8,128]{2,1,0:T(8,128)S(1)} %bitcast.18, f32[8,8,128]{2,1,0:T(8,128)S(1)} %bitcast.20), kind=kLoop, calls=%fused_computation.1 | loop fusion | flops 24576 | bytes 163840 | tf_op jit(solution)/shard_map/add | solution.py:302
  (2 shorter events, 0.0 us)
Async XLA Ops:
  0.6 7.0 %copy-start = (f32[3,2048]{1,0:T(4,128)S(1)}, f32[3,2048]{1,0:T(4,128)}, u32[]{:S(2)}) copy-start(f32[3,2048]{1,0:T(4,128)} %pos_ref.3) | copy-start | bytes 73732
  1.5 11.6 %copy-start.1 = (f32[3,2048]{1,0:T(4,128)S(1)}, f32[3,2048]{1,0:T(4,128)}, u32[]{:S(2)}) copy-start(f32[3,2048]{1,0:T(4,128)} %frac_ref.1) | copy-start | bytes 73732
  1.5 11.6 %copy-start.2 = (f32[2048]{0:T(1024)S(1)}, f32[2048]{0:T(1024)}, u32[]{:S(2)}) copy-start(f32[2048]{0:T(1024)} %param.11) | copy-start | bytes 24580
  1.5 11.6 %copy-start.3 = (s32[2048]{0:T(1024)S(1)}, s32[2048]{0:T(1024)}, u32[]{:S(2)}) copy-start(s32[2048]{0:T(1024)} %param.13) | copy-start | bytes 24580
  1.5 11.6 %copy-start.4 = (s32[2048]{0:T(1024)S(1)}, s32[2048]{0:T(1024)}, u32[]{:S(2)}) copy-start(s32[2048]{0:T(1024)} %param.14) | copy-start | bytes 24580
  1.5 11.6 %copy-start.5 = (s32[2048,1]{0,1:T(1,128)S(1)}, s32[2048,1]{0,1:T(1,128)}, u32[]{:S(2)}) copy-start(s32[2048,1]{0,1:T(1,128)} %param.15) | copy-start | bytes 24580
  1.6 11.2 %collective-permute-start.2 = (f32[7,2048]{1,0:T(8,128)S(1)}, f32[7,2048]{1,0:T(8,128)S(1)}, u32[]{:S(2)}, u32[]{:S(2)}) collective-permute-start(f32[7,2048]{1,0:T(8,128)S(1)} %pad_maximum_fusion.src_ref), channel_id=1, source_target_pairs={{0,3},{1,0},{2,1},{3,2},{4,7},{5,4},{6,5},{7,6},{8,11},{9,8},{10,9... | collective-permute-start | bytes 172040 | tf_op jit(solution)/shard_map/ppermute | solution.py:252
  6.7 6.5 %collective-permute-start.1 = (f32[7,2048]{1,0:T(8,128)S(1)}, f32[7,2048]{1,0:T(8,128)S(1)}, u32[]{:S(2)}, u32[]{:S(2)}) collective-permute-start(f32[7,2048]{1,0:T(8,128)S(1)} %pad_maximum_fusion.src_ref), channel_id=1, source_target_pairs={{0,2},{1,3},{2,0},{3,1},{4,6},{5,7},{6,4},{7,5},{8,10},{9,11},{10,... | collective-permute-start | bytes 172040 | tf_op jit(solution)/shard_map/ppermute | solution.py:252
  6.7 6.5 %collective-permute-start = (f32[7,2048]{1,0:T(8,128)S(1)}, f32[7,2048]{1,0:T(8,128)S(1)}, u32[]{:S(2)}, u32[]{:S(2)}) collective-permute-start(f32[7,2048]{1,0:T(8,128)S(1)} %pad_maximum_fusion.src_ref), channel_id=1, source_target_pairs={{0,1},{1,2},{2,3},{3,0},{4,5},{5,6},{6,7},{7,4},{8,9},{9,10},{10,1... | collective-permute-start | bytes 172040 | tf_op jit(solution)/shard_map/ppermute | solution.py:252
  32.8 1.3 %collective-permute-start.3 = (f32[256,128]{1,0:T(8,128)S(1)}, f32[256,128]{1,0:T(8,128)S(1)}, u32[]{:S(2)}, u32[]{:S(2)}) collective-permute-start(f32[256,128]{1,0:T(8,128)S(1)} %get-tuple-element.7), channel_id=1, source_target_pairs={{0,4},{4,0},{8,12},{12,8},{16,20},{20,16},{24,28},{28,24},{1,5},{5... | collective-permute-start | bytes 393224 | tf_op jit(solution)/shard_map/ppermute | solution.py:299
  34.2 4.0 %collective-permute-start.6 = (f32[16,4,128]{2,1,0:T(4,128)S(1)}, f32[16,4,128]{2,1,0:T(4,128)S(1)}, u32[]{:S(2)}, u32[]{:S(2)}) collective-permute-start(f32[16,4,128]{2,1,0:T(4,128)S(1)} %bitcast.25), channel_id=1, source_target_pairs={{0,8},{4,12},{8,0},{12,4},{16,24},{20,28},{24,16},{28,20},{1,9},{5... | collective-permute-start | bytes 98312 | tf_op jit(solution)/shard_map/ppermute | solution.py:299
  35.8 4.8 %collective-permute-start.4 = (f32[16,4,128]{2,1,0:T(4,128)S(1)}, f32[16,4,128]{2,1,0:T(4,128)S(1)}, u32[]{:S(2)}, u32[]{:S(2)}) collective-permute-start(f32[16,4,128]{2,1,0:T(4,128)S(1)} %bitcast.24), channel_id=1, source_target_pairs={{0,24},{4,28},{8,16},{12,20},{16,8},{20,12},{24,0},{28,4},{1,25},{... | collective-permute-start | bytes 98312 | tf_op jit(solution)/shard_map/ppermute | solution.py:299
  37.3 3.9 %collective-permute-start.5 = (f32[16,4,128]{2,1,0:T(4,128)S(1)}, f32[16,4,128]{2,1,0:T(4,128)S(1)}, u32[]{:S(2)}, u32[]{:S(2)}) collective-permute-start(f32[16,4,128]{2,1,0:T(4,128)S(1)} %bitcast.23), channel_id=1, source_target_pairs={{0,16},{4,20},{8,24},{12,28},{16,0},{20,4},{24,8},{28,12},{1,17},{... | collective-permute-start | bytes 98312 | tf_op jit(solution)/shard_map/ppermute | solution.py:299

commit v5 on v4

--- a/solution.py
+++ b/solution.py
@@ -167,9 +167,9 @@
     owner_ref,
     *refs,
 ):
-    other_refs = refs[:-9]
-    velocity_ref, keep_ref, send_ref, *refs = refs[-9:]
-    target_ref, feature_ref, moment_ref, slope_ref, sum_ref, pick_ref = refs
+    other_refs = refs[:-12]
+    velocity_ref, value_ref, spread_ref, send_ref, *refs = refs[-12:]
+    target_ref, feature_ref, moment_ref, slope_ref, sum_ref, pick_ref, ready_ref, copied = refs
     count = src_ref.shape[1]
     points = rows_of(pos_ref[...], 0, 3)
     target_ref[...] = target_features(points).astype(bf16)
@@ -189,7 +189,9 @@
     sums = sum_ref[0:30, :] + sum_ref[30:60, :] + sum_ref[60:90, :]
     vortex = rows_of(src_ref[...], 3, 3)
     velocity, stretch = combine(points, vortex, sums)
-    velocity_ref[...] = jnp.concatenate(velocity, axis=0)
+    ready_ref[...] = jnp.concatenate(velocity, axis=0)
+    velocity_copy = pltpu.make_async_copy(ready_ref, velocity_ref, copied)
+    velocity_copy.start()
 
     values = [inverse_volume * (a + time_step * d) for a, d in zip(vortex, stretch)]
     values.append(inverse_volume * dye_ref[...])
@@ -212,14 +214,24 @@
     spread_low = (spread - spread_high.astype(f32)).astype(bf16)
     spread_both = jnp.concatenate([spread_high, spread_low], axis=0)
 
-    slot = owner_ref[...] ^ lax.axis_index("dom")
-    slot = (slot & 1) * (owners // 2) + (slot >> 1)
+    value_ref[...] = jnp.concatenate(values, axis=0)
+    spread_ref[...] = spread_both
+    send_ref[...] = deposits(
+        tiles, owners, 1, owner_ref[...], tile_ref[...], value_ref[...], spread_both, pick_ref
+    )
+    velocity_copy.wait()
+
+
+def deposits(tiles, owners, odd, owner, tile, value, spread_both, pick_ref):
+    count = owner.shape[1]
+    slot = owner ^ lax.axis_index("dom")
+    number = jnp.where((slot & 1) == odd, (slot >> 1) * tiles + tile, -8)
     node = lax.broadcasted_iota(jnp.int32, (16, count), 0)
-    mine = slot * tiles + tile_ref[...] - (node >> 2)
-    value = jnp.concatenate(values * 4, axis=0)
+    mine = number - (node >> 2)
+    value = jnp.concatenate([value] * 4, axis=0)
     value_high = value.astype(bf16).astype(f32)
     value_low = value - value_high
-    total = owners * tiles * 4
+    total = owners * tiles * 2
     for group in range(total // 16):
         mask = mine == 4 * group
         first = 16 * group
@@ -230,13 +242,21 @@
         pick_ref[...], spread_both, transposed_rhs, preferred_element_type=f32
     )
     both = both[:, 0:128] + both[:, 128:256]
-    both = both[:total] + both[total:]
-    keep_ref[...] = both[: total // 2]
-    send_ref[...] = both[total // 2 :]
+    return both[:total] + both[total:]
+
+
+def keep_kernel(tiles, owners, value_ref, spread_ref, tile_ref, owner_ref, keep_ref, pick_ref):
+    keep_ref[...] = deposits(
+        tiles, owners, 0, owner_ref[...], tile_ref[...], value_ref[...], spread_ref[...], pick_ref
+    )
 
 
 def vmem_specs(count):
     return [pl.BlockSpec(memory_space=pltpu.VMEM)] * count
+
+
+def partner(i, step, count):
+    return i ^ step if count & (count - 1) == 0 else (i + step) % count
 
 
 def on_device(
@@ -249,7 +269,7 @@
     width = math.gcd(count, 256)
     sources = jnp.concatenate([positions, strength, core_radius[None]], axis=0)
     others = [
-        lax.ppermute(sources, "blk", [(i, (i + s) % blocks) for i in range(blocks)])
+        lax.ppermute(sources, "blk", [(i, partner(i, s, blocks)) for i in range(blocks)])
         for s in range(1, blocks)
     ]
     scratch = lambda n: [
@@ -275,13 +295,26 @@
         name="own_pairs",
     )(positions, sources)
     half = jax.ShapeDtypeStruct((owners * tiles * 2, 128), f32)
-    velocity, keep, send = pl.pallas_call(
+    pick = pltpu.VMEM((owners * tiles * 4, count), bf16)
+    tile_row = tile_local[None]
+    owner_row = owner_dom.reshape(1, count)
+    velocity, value, spread, send = pl.pallas_call(
         functools.partial(tail_kernel, tiles, owners),
-        out_shape=(jax.ShapeDtypeStruct((3, count), f32), half, half),
+        out_shape=(
+            jax.ShapeDtypeStruct((3, count), f32),
+            jax.ShapeDtypeStruct((4, count), f32),
+            jax.ShapeDtypeStruct((256, count), bf16),
+            half,
+        ),
         in_specs=vmem_specs(8 + len(others)),
-        out_specs=tuple(vmem_specs(3)),
+        out_specs=(pl.BlockSpec(memory_space=pl.ANY), *vmem_specs(3)),
         scratch_shapes=scratch(len(others))
-        + [pltpu.VMEM((96, count), f32), pltpu.VMEM((owners * tiles * 8, count), bf16)],
+        + [
+            pltpu.VMEM((96, count), f32),
+            pick,
+            pltpu.VMEM((3, count), f32),
+            pltpu.SemaphoreType.DMA,
+        ],
         compiler_params=params,
         cost_estimate=cost(len(others)),
         name="other_pairs_and_deposit",
@@ -292,10 +325,24 @@
         dye_amount[None],
         cell_fraction,
         cell_index[None],
-        tile_local[None],
-        owner_dom.reshape(1, count),
+        tile_row,
+        owner_row,
         *others,
     )
+    keep = pl.pallas_call(
+        functools.partial(keep_kernel, tiles, owners),
+        out_shape=half,
+        in_specs=vmem_specs(4),
+        out_specs=vmem_specs(1)[0],
+        scratch_shapes=[pick],
+        compiler_params=params,
+        cost_estimate=pl.CostEstimate(
+            flops=owners * tiles * 8 * count * 256 * 2,
+            bytes_accessed=count * 1024,
+            transcendentals=0,
+        ),
+        name="deposit_even_slots",
+    )(value, spread, tile_row, owner_row)
     exchange = lambda x, s: lax.ppermute(x, "dom", [(i, i ^ s) for i in range(owners)])
     grid = (keep + exchange(send, 1)).reshape(owners // 2, tiles, 4, 128)
     got = [exchange(grid[j], 2 * j) for j in range(owners // 2 - 1, 0, -1)]

time: 42 us -> 41 us (0.976)
  waiting for transfers between devices: 5.12 us -> 4.14 us
    pallas_call x0 -> x1, Pallas kernels: none -> 0.75 us  [on_device(): pl.pallas_call(functools.partial(keep_kernel, tiles, owners), out_shape=h...]
    ppermute x4, waiting for transfers between devices: 4.75 us -> 4.13 us  [on_device(): lax.ppermute(x, 'dom', [(i, i ^ s) for i in range(owners)])]
    pallas_call x1, Pallas kernels: 19.7 us -> 19.2 us  [on_device(): pl.pallas_call(functools.partial(tail_kernel, tiles, owners), out_shape=(...]
  transfers between devices with their start and end apart: 7 -> 7, of which waited for: 5 -> 4; matrix products, arithmetic and copies ran while one was open for 0% -> 0% of each run, Pallas kernels for 12% -> 14%
where the time goes in v5:
time: 41 us; the launch traced here: 40.8 us
  Pallas kernels  25 us (61%)
  starting transfers between devices  9.38 us (23%)
  waiting for transfers between devices  4.14 us (10%)
  other arithmetic  1.49 us (4%)
  between operations  0.79 us (2%)
    pallas_call x1, Pallas kernels, on_device(): pl.pallas_call(functools.partial(tail_kernel, tiles, owners), out_shape=(...  19.2 us
    ppermute x3, starting transfers between devices, on_device(): lax.ppermute(sources, 'blk', [(i, partner(i, s, blocks)) for i in range(b...  5.76 us
    pallas_call x1, Pallas kernels, on_device(): pl.pallas_call(own_kernel, out_shape=jax.ShapeDtypeStruct((96, count), f3...  5.07 us
    ppermute x4, waiting for transfers between devices, on_device(): lax.ppermute(x, 'dom', [(i, i ^ s) for i in range(owners)])  4.13 us
    ppermute x4, starting transfers between devices, on_device(): lax.ppermute(x, 'dom', [(i, i ^ s) for i in range(owners)])  3.62 us
    concatenate x1, other arithmetic, on_device(): sources = jnp.concatenate([positions, strength, core_radius[None]], axis=0)  0.85 us
  transfers between devices with their start and end apart: 7, of which 4 were waited for; matrix products, arithmetic and copies ran while one was open for 0% of the time, Pallas kernels for 14%

profile of v5, /device:TPU:0, one launch (start us, length us, event | category | flops | bytes accessed | tf_op | source)
XLA Modules:
  0.0 40.8 jit_solution(16507987242059204493)
XLA Ops:
  0.6 0.0 copy-start
  0.6 0.8 %pad_maximum_fusion.src_ref = f32[7,2048]{1,0:T(8,128)S(1)} fusion(f32[1,2048]{1,0:T(1,128)} %bitcast.28, f32[3,2048]{1,0:T(4,128)} %param.9, f32[3,2048]{1,0:T(4,128)} %pos_ref.3), kind=kLoop, calls=%fused_computation | loop fusion | flops 28672 | bytes 114688 | tf_op jit(solution)/shard_map/concatenate | solution.py:270
  1.5 0.0 copy-start.1
  1.5 0.0 copy-start.2
  1.5 0.0 copy-start.3
  1.5 0.0 copy-start.4
  1.5 0.0 copy-start.5
  1.6 5.1 %collective-permute-start.2 = (f32[7,2048]{1,0:T(8,128)S(1)}, f32[7,2048]{1,0:T(8,128)S(1)}, u32[]{:S(2)}, u32[]{:S(2)}) collective-permute-start(f32[7,2048]{1,0:T(8,128)S(1)} %pad_maximum_fusion.src_ref), channel_id=1, source_target_pairs={{0,3},{1,2},{2,1},{3,0},{4,7},{5,6},{6,5},{7,4},{8,11},{9,10},{10,... | collective-permute-start | bytes 172040 | tf_op jit(solution)/shard_map/ppermute | solution.py:272
  6.7 0.0 collective-permute-start.1
  6.7 0.6 %collective-permute-start = (f32[7,2048]{1,0:T(8,128)S(1)}, f32[7,2048]{1,0:T(8,128)S(1)}, u32[]{:S(2)}, u32[]{:S(2)}) collective-permute-start(f32[7,2048]{1,0:T(8,128)S(1)} %pad_maximum_fusion.src_ref), channel_id=1, source_target_pairs={{0,1},{1,0},{2,3},{3,2},{4,5},{5,4},{6,7},{7,6},{8,9},{9,8},{10,11... | collective-permute-start | bytes 172040 | tf_op jit(solution)/shard_map/ppermute | solution.py:272
  7.3 0.0 copy-done
  7.3 5.1 %own_pairs.1.before_ref = f32[96,2048]{1,0:T(8,128)S(1)} custom-call(f32[3,2048]{1,0:T(4,128)S(1)} %copy-done, f32[7,2048]{1,0:T(8,128)S(1)} %pad_maximum_fusion.src_ref), custom_call_target="tpu_custom_call" | custom-call | flops 6442450944 | bytes 2097152 | tf_op jit(solution)/shard_map/own_pairs/pallas_call | solution.py:287
  12.4 0.0 collective-permute-done.2.refs_2_
  12.4 0.0 collective-permute-done.1.refs_1_
  12.4 0.0 collective-permute-done.refs_0_
  12.4 0.0 copy-done.1
  12.4 0.0 copy-done.2
  12.4 0.0 copy-done.3
  12.4 0.0 copy-done.4
  12.5 0.0 copy-done.5
  12.5 19.2 %other_pairs_and_deposit.1 = (f32[3,2048]{1,0:T(4,128)}, f32[4,2048]{1,0:T(4,128)S(1)}, bf16[256,2048]{1,0:T(8,128)(2,1)S(1)}, f32[256,128]{1,0:T(8,128)S(1)}) custom-call(f32[3,2048]{1,0:T(4,128)S(1)} %copy-done, f32[7,2048]{1,0:T(8,128)S(1)} %pad_maximum_fusion.src_ref, f32[96,2048]{1,0:T(8,128)S(1)} %own_pairs.1.before_ref, f32[1,2048]{1,0:T(1,128)S(1)} %bitcast.14, ...), custom_call_target="tpu_custom_call" | custom-call | flops 19327352832 | bytes 2097152 | tf_op jit(solution)/shard_map/other_pairs_and_deposit/pallas_call | solution.py:301
  31.6 0.1 collective-permute-start.3
  31.7 0.7 %deposit_even_slots.1 = f32[256,128]{1,0:T(8,128)S(1)} custom-call(f32[4,2048]{1,0:T(4,128)S(1)} %get-tuple-element.7.value_ref, bf16[256,2048]{1,0:T(8,128)(2,1)S(1)} %get-tuple-element.8.spread_ref, s32[1,2048]{1,0:T(1,128)S(1)} %bitcast.17, s32[1,2048]{1,0:T(1,128)S(1)} %bitcast.19), custom_call_target="tpu_custom_call" | custom-call | flops 1073741824 | bytes 2097152 | tf_op jit(solution)/shard_map/deposit_even_slots/pallas_call | solution.py:332
  32.5 0.6 %collective-permute-done.3 = f32[256,128]{1,0:T(8,128)S(1)} collective-permute-done((f32[256,128]{1,0:T(8,128)S(1)}, f32[256,128]{1,0:T(8,128)S(1)}, u32[]{:S(2)}, u32[]{:S(2)}) %collective-permute-start.3) | collective-permute-done | bytes 131104 | tf_op jit(solution)/shard_map/ppermute | solution.py:346
  33.1 1.7 %collective-permute-start.6 = (f32[16,4,128]{2,1,0:T(4,128)S(1)}, f32[16,4,128]{2,1,0:T(4,128)S(1)}, u32[]{:S(2)}, u32[]{:S(2)}) collective-permute-start(f32[16,4,128]{2,1,0:T(4,128)S(1)} %bitcast.27), channel_id=1, source_target_pairs={{0,8},{4,12},{8,0},{12,4},{16,24},{20,28},{24,16},{28,20},{1,9},{5... | collective-permute-start | bytes 98312 | tf_op jit(solution)/shard_map/ppermute | solution.py:346
  34.8 1.5 %collective-permute-start.4 = (f32[16,4,128]{2,1,0:T(4,128)S(1)}, f32[16,4,128]{2,1,0:T(4,128)S(1)}, u32[]{:S(2)}, u32[]{:S(2)}) collective-permute-start(f32[16,4,128]{2,1,0:T(4,128)S(1)} %bitcast.26), channel_id=1, source_target_pairs={{0,24},{4,28},{8,16},{12,20},{16,8},{20,12},{24,0},{28,4},{1,25},{... | collective-permute-start | bytes 98312 | tf_op jit(solution)/shard_map/ppermute | solution.py:346
  36.3 0.4 collective-permute-start.5
  36.6 0.4 %collective-permute-done.6 = f32[16,4,128]{2,1,0:T(4,128)S(1)} collective-permute-done((f32[16,4,128]{2,1,0:T(4,128)S(1)}, f32[16,4,128]{2,1,0:T(4,128)S(1)}, u32[]{:S(2)}, u32[]{:S(2)}) %collective-permute-start.6) | collective-permute-done | bytes 32800 | tf_op jit(solution)/shard_map/ppermute | solution.py:346
  37.1 2.5 %collective-permute-done.4 = f32[16,4,128]{2,1,0:T(4,128)S(1)} collective-permute-done((f32[16,4,128]{2,1,0:T(4,128)S(1)}, f32[16,4,128]{2,1,0:T(4,128)S(1)}, u32[]{:S(2)}, u32[]{:S(2)}) %collective-permute-start.4) | collective-permute-done | bytes 32800 | tf_op jit(solution)/shard_map/ppermute | solution.py:346
  39.6 0.6 %collective-permute-done.5 = f32[16,4,128]{2,1,0:T(4,128)S(1)} collective-permute-done((f32[16,4,128]{2,1,0:T(4,128)S(1)}, f32[16,4,128]{2,1,0:T(4,128)S(1)}, u32[]{:S(2)}, u32[]{:S(2)}) %collective-permute-start.5) | collective-permute-done | bytes 32800 | tf_op jit(solution)/shard_map/ppermute | solution.py:346
  40.2 0.6 %add_add_fusion = f32[8,8,128]{2,1,0:T(8,128)} fusion(f32[8,8,128]{2,1,0:T(8,128)S(1)} %bitcast.21, f32[8,8,128]{2,1,0:T(8,128)S(1)} %bitcast.23, f32[8,8,128]{2,1,0:T(8,128)S(1)} %bitcast.20, f32[8,8,128]{2,1,0:T(8,128)S(1)} %bitcast.22), kind=kLoop, calls=%fused_computation.1 | loop fusion | flops 24576 | bytes 163840 | tf_op jit(solution)/shard_map/add | solution.py:349
  (2 shorter events, 0.0 us)
Async XLA Ops:
  0.6 6.7 %copy-start = (f32[3,2048]{1,0:T(4,128)S(1)}, f32[3,2048]{1,0:T(4,128)}, u32[]{:S(2)}) copy-start(f32[3,2048]{1,0:T(4,128)} %pos_ref.3) | copy-start | bytes 73732
  1.5 10.9 %copy-start.1 = (f32[3,2048]{1,0:T(4,128)S(1)}, f32[3,2048]{1,0:T(4,128)}, u32[]{:S(2)}) copy-start(f32[3,2048]{1,0:T(4,128)} %frac_ref.1) | copy-start | bytes 73732
  1.5 10.9 %copy-start.2 = (f32[2048]{0:T(1024)S(1)}, f32[2048]{0:T(1024)}, u32[]{:S(2)}) copy-start(f32[2048]{0:T(1024)} %param.11) | copy-start | bytes 24580
  1.5 10.9 %copy-start.3 = (s32[2048]{0:T(1024)S(1)}, s32[2048]{0:T(1024)}, u32[]{:S(2)}) copy-start(s32[2048]{0:T(1024)} %param.13) | copy-start | bytes 24580
  1.5 10.9 %copy-start.4 = (s32[2048]{0:T(1024)S(1)}, s32[2048]{0:T(1024)}, u32[]{:S(2)}) copy-start(s32[2048]{0:T(1024)} %param.14) | copy-start | bytes 24580
  1.5 10.9 %copy-start.5 = (s32[2048,1]{0,1:T(1,128)S(1)}, s32[2048,1]{0,1:T(1,128)}, u32[]{:S(2)}) copy-start(s32[2048,1]{0,1:T(1,128)} %param.15) | copy-start | bytes 24580
  1.6 10.8 %collective-permute-start.2 = (f32[7,2048]{1,0:T(8,128)S(1)}, f32[7,2048]{1,0:T(8,128)S(1)}, u32[]{:S(2)}, u32[]{:S(2)}) collective-permute-start(f32[7,2048]{1,0:T(8,128)S(1)} %pad_maximum_fusion.src_ref), channel_id=1, source_target_pairs={{0,3},{1,2},{2,1},{3,0},{4,7},{5,6},{6,5},{7,4},{8,11},{9,10},{10,... | collective-permute-start | bytes 172040 | tf_op jit(solution)/shard_map/ppermute | solution.py:272
  6.7 5.7 %collective-permute-start.1 = (f32[7,2048]{1,0:T(8,128)S(1)}, f32[7,2048]{1,0:T(8,128)S(1)}, u32[]{:S(2)}, u32[]{:S(2)}) collective-permute-start(f32[7,2048]{1,0:T(8,128)S(1)} %pad_maximum_fusion.src_ref), channel_id=1, source_target_pairs={{0,2},{1,3},{2,0},{3,1},{4,6},{5,7},{6,4},{7,5},{8,10},{9,11},{10,... | collective-permute-start | bytes 172040 | tf_op jit(solution)/shard_map/ppermute | solution.py:272
  6.7 5.7 %collective-permute-start = (f32[7,2048]{1,0:T(8,128)S(1)}, f32[7,2048]{1,0:T(8,128)S(1)}, u32[]{:S(2)}, u32[]{:S(2)}) collective-permute-start(f32[7,2048]{1,0:T(8,128)S(1)} %pad_maximum_fusion.src_ref), channel_id=1, source_target_pairs={{0,1},{1,0},{2,3},{3,2},{4,5},{5,4},{6,7},{7,6},{8,9},{9,8},{10,11... | collective-permute-start | bytes 172040 | tf_op jit(solution)/shard_map/ppermute | solution.py:272
  31.6 1.4 %collective-permute-start.3 = (f32[256,128]{1,0:T(8,128)S(1)}, f32[256,128]{1,0:T(8,128)S(1)}, u32[]{:S(2)}, u32[]{:S(2)}) collective-permute-start(f32[256,128]{1,0:T(8,128)S(1)} %get-tuple-element.9), channel_id=1, source_target_pairs={{0,4},{4,0},{8,12},{12,8},{16,20},{20,16},{24,28},{28,24},{1,5},{5... | collective-permute-start | bytes 393224 | tf_op jit(solution)/shard_map/ppermute | solution.py:346
  33.1 4.0 %collective-permute-start.6 = (f32[16,4,128]{2,1,0:T(4,128)S(1)}, f32[16,4,128]{2,1,0:T(4,128)S(1)}, u32[]{:S(2)}, u32[]{:S(2)}) collective-permute-start(f32[16,4,128]{2,1,0:T(4,128)S(1)} %bitcast.27), channel_id=1, source_target_pairs={{0,8},{4,12},{8,0},{12,4},{16,24},{20,28},{24,16},{28,20},{1,9},{5... | collective-permute-start | bytes 98312 | tf_op jit(solution)/shard_map/ppermute | solution.py:346
  34.8 4.8 %collective-permute-start.4 = (f32[16,4,128]{2,1,0:T(4,128)S(1)}, f32[16,4,128]{2,1,0:T(4,128)S(1)}, u32[]{:S(2)}, u32[]{:S(2)}) collective-permute-start(f32[16,4,128]{2,1,0:T(4,128)S(1)} %bitcast.26), channel_id=1, source_target_pairs={{0,24},{4,28},{8,16},{12,20},{16,8},{20,12},{24,0},{28,4},{1,25},{... | collective-permute-start | bytes 98312 | tf_op jit(solution)/shard_map/ppermute | solution.py:346
  36.3 3.9 %collective-permute-start.5 = (f32[16,4,128]{2,1,0:T(4,128)S(1)}, f32[16,4,128]{2,1,0:T(4,128)S(1)}, u32[]{:S(2)}, u32[]{:S(2)}) collective-permute-start(f32[16,4,128]{2,1,0:T(4,128)S(1)} %bitcast.25), channel_id=1, source_target_pairs={{0,16},{4,20},{8,24},{12,28},{16,0},{20,4},{24,8},{28,12},{1,17},{... | collective-permute-start | bytes 98312 | tf_op jit(solution)/shard_map/ppermute | solution.py:346

commit v6 on v5

--- a/solution.py
+++ b/solution.py
@@ -18,10 +18,10 @@
 
 
 def split3(x):
-    high = x.astype(bf16).astype(f32)
-    rest = x - high
-    middle = rest.astype(bf16).astype(f32)
-    return high, middle, rest - middle
+    high = x.astype(bf16)
+    rest = x - high.astype(f32)
+    middle = rest.astype(bf16)
+    return high, middle, (rest - middle.astype(f32)).astype(bf16)
 
 
 def rows_of(array, first, count):
@@ -44,8 +44,8 @@
     one = jnp.ones_like(points[0])
     zero = jnp.zeros_like(one)
     stack = jnp.concatenate(points + [one, square_sum(points), zero, zero, zero], axis=0)
-    high, middle, low = split3(stack)
-    return jnp.concatenate([high, middle, high, low, high, middle], axis=0)
+    high, middle, low = [part.astype(f32) for part in split3(stack)]
+    return jnp.concatenate([high, middle, high, low, high, middle], axis=0).astype(bf16)
 
 
 def source_features(src):
@@ -56,12 +56,13 @@
     one = jnp.ones_like(radius)
     zero = jnp.zeros_like(radius)
     stack = jnp.concatenate([-2.0 * p for p in points] + [offset, one, zero, zero, zero], axis=0)
-    high, middle, low = split3(stack)
+    high, middle, low = [part.astype(f32) for part in split3(stack)]
     features = jnp.concatenate([high, high, middle, high, low, middle], axis=0)
     base = jnp.concatenate(vortex + cross_rows(vortex, points), axis=0)
-    groups = jnp.concatenate([base] + [base * p for p in points] + [base * offset], axis=0)
-    moments = jnp.concatenate(list(split3(groups)) + [jnp.zeros_like(base)], axis=0)
-    return features.T.astype(bf16), moments.astype(bf16)
+    groups = jnp.concatenate(
+        [base] + [base * p for p in points] + [base * offset, zero, zero], axis=0
+    )
+    return features.T.astype(bf16), jnp.concatenate(split3(groups), axis=0)
 
 
 def add_pair_sums(lag, unroll, target_ref, feature_ref, moment_ref, sum_ref, slope_ref):
@@ -114,7 +115,7 @@
 def own_kernel(
     pos_ref, src_ref, sum_ref, target_ref, feature_ref, moment_ref, slope_ref
 ):
-    target_ref[...] = target_features(rows_of(pos_ref[...], 0, 3)).astype(bf16)
+    target_ref[...] = target_features(rows_of(pos_ref[...], 0, 3))
     feature_ref[...], moment_ref[...] = source_features(src_ref[...])
     sum_ref[...] = jnp.zeros_like(sum_ref)
     tiles = sum_ref.shape[1] // slope_ref.shape[2]
@@ -172,7 +173,7 @@
     target_ref, feature_ref, moment_ref, slope_ref, sum_ref, pick_ref, ready_ref, copied = refs
     count = src_ref.shape[1]
     points = rows_of(pos_ref[...], 0, 3)
-    target_ref[...] = target_features(points).astype(bf16)
+    target_ref[...] = target_features(points)
     for k, other_ref in enumerate(other_refs):
         place = slice(k * count, (k + 1) * count)
         feature_ref[place], moment_ref[:, place] = source_features(other_ref[...])
@@ -186,7 +187,7 @@
         sum_ref,
         slope_ref,
     )
-    sums = sum_ref[0:30, :] + sum_ref[30:60, :] + sum_ref[60:90, :]
+    sums = sum_ref[0:32, :] + sum_ref[32:64, :] + sum_ref[64:96, :]
     vortex = rows_of(src_ref[...], 3, 3)
     velocity, stretch = combine(points, vortex, sums)
     ready_ref[...] = jnp.concatenate(velocity, axis=0)
@@ -222,10 +223,22 @@
     velocity_copy.wait()
 
 
+def slots_of(owners):
+    if owners == 8:
+        return (0, 6, 2, 3), (1, 7, 5, 4)
+    return range(0, owners, 2), range(1, owners, 2)
+
+
 def deposits(tiles, owners, odd, owner, tile, value, spread_both, pick_ref):
     count = owner.shape[1]
-    slot = owner ^ lax.axis_index("dom")
-    number = jnp.where((slot & 1) == odd, (slot >> 1) * tiles + tile, -8)
+    me = lax.axis_index("dom")
+    slot = owner ^ me
+    if owners == 8:
+        traded = (slot & 1) | ((slot & 2) << 1) | ((slot & 4) >> 1)
+        slot = jnp.where((me & 1) == 1, traded, slot)
+    number = jnp.full(slot.shape, -8, jnp.int32)
+    for place, s in enumerate(slots_of(owners)[odd]):
+        number = jnp.where(slot == s, place * tiles + tile, number)
     node = lax.broadcasted_iota(jnp.int32, (16, count), 0)
     mine = number - (node >> 2)
     value = jnp.concatenate([value] * 4, axis=0)
@@ -345,6 +358,10 @@
     )(value, spread, tile_row, owner_row)
     exchange = lambda x, s: lax.ppermute(x, "dom", [(i, i ^ s) for i in range(owners)])
     grid = (keep + exchange(send, 1)).reshape(owners // 2, tiles, 4, 128)
+    if owners == 8:
+        near = lax.ppermute(grid[2:], "dom", [(i, i ^ (4 if i & 1 else 2)) for i in range(owners)])
+        far = exchange(grid[1], 6)
+        return velocity, grid[0] + near[0] + far + exchange(near[1], 1)
     got = [exchange(grid[j], 2 * j) for j in range(owners // 2 - 1, 0, -1)]
     return velocity, sum(got, grid[0])
 

time: 41 us -> 40.2 us (0.980)
    ppermute x4 -> x3, starting transfers between devices: 3.62 us -> 1.55 us  [on_device(): lax.ppermute(x, 'dom', [(i, i ^ s) for i in range(owners)])]
    ppermute x4 -> x3, waiting for transfers between devices: 4.13 us -> 2.39 us  [on_device(): lax.ppermute(x, 'dom', [(i, i ^ s) for i in range(owners)])]
    ppermute x0 -> x1, starting transfers between devices: none -> 1.67 us  [on_device(): lax.ppermute(grid[2:], 'dom', [(i, i ^ (4 if i & 1 else 2)) for i in rang...]
    ppermute x0 -> x1, waiting for transfers between devices: none -> 1.53 us  [on_device(): lax.ppermute(grid[2:], 'dom', [(i, i ^ (4 if i & 1 else 2)) for i in rang...]
  transfers between devices with their start and end apart: 7 -> 7, of which waited for: 4 -> 3; matrix products, arithmetic and copies ran while one was open for 0% -> 0% of each run, Pallas kernels for 14% -> 14%
where the time goes in v6:
time: 40.2 us; the launch traced here: 40 us
  Pallas kernels  24.7 us (61%)
  starting transfers between devices  8.98 us (22%)
  waiting for transfers between devices  3.93 us (10%)
  other arithmetic  1.5 us (4%)
  between operations  0.79 us (2%)
    pallas_call x1, Pallas kernels, on_device(): pl.pallas_call(functools.partial(tail_kernel, tiles, owners), out_shape=(...  19 us
    ppermute x3, starting transfers between devices, on_device(): lax.ppermute(sources, 'blk', [(i, partner(i, s, blocks)) for i in range(b...  5.76 us
    pallas_call x1, Pallas kernels, on_device(): pl.pallas_call(own_kernel, out_shape=jax.ShapeDtypeStruct((96, count), f3...  4.99 us
    ppermute x3, waiting for transfers between devices, on_device(): lax.ppermute(x, 'dom', [(i, i ^ s) for i in range(owners)])  2.39 us
    ppermute x1, starting transfers between devices, on_device(): lax.ppermute(grid[2:], 'dom', [(i, i ^ (4 if i & 1 else 2)) for i in rang...  1.67 us
    ppermute x3, starting transfers between devices, on_device(): lax.ppermute(x, 'dom', [(i, i ^ s) for i in range(owners)])  1.55 us
    ppermute x1, waiting for transfers between devices, on_device(): lax.ppermute(grid[2:], 'dom', [(i, i ^ (4 if i & 1 else 2)) for i in rang...  1.53 us
    concatenate x1, other arithmetic, on_device(): sources = jnp.concatenate([positions, strength, core_radius[None]], axis=0)  0.85 us
  transfers between devices with their start and end apart: 7, of which 3 were waited for; matrix products, arithmetic and copies ran while one was open for 0% of the time, Pallas kernels for 14%

profile of v6, /device:TPU:0, one launch (start us, length us, event | category | flops | bytes accessed | tf_op | source)
XLA Modules:
  0.0 40.0 jit_solution(16904817013540704629)
XLA Ops:
  0.6 0.0 copy-start
  0.6 0.8 %pad_maximum_fusion.src_ref = f32[7,2048]{1,0:T(8,128)S(1)} fusion(f32[1,2048]{1,0:T(1,128)} %bitcast.27, f32[3,2048]{1,0:T(4,128)} %param.9, f32[3,2048]{1,0:T(4,128)} %pos_ref.3), kind=kLoop, calls=%fused_computation | loop fusion | flops 28672 | bytes 114688 | tf_op jit(solution)/shard_map/concatenate | solution.py:283
  1.5 0.0 copy-start.1
  1.5 0.0 copy-start.2
  1.5 0.0 copy-start.3
  1.5 0.0 copy-start.4
  1.5 0.0 copy-start.5
  1.6 5.1 %collective-permute-start.2 = (f32[7,2048]{1,0:T(8,128)S(1)}, f32[7,2048]{1,0:T(8,128)S(1)}, u32[]{:S(2)}, u32[]{:S(2)}) collective-permute-start(f32[7,2048]{1,0:T(8,128)S(1)} %pad_maximum_fusion.src_ref), channel_id=1, source_target_pairs={{0,3},{1,2},{2,1},{3,0},{4,7},{5,6},{6,5},{7,4},{8,11},{9,10},{10,... | collective-permute-start | bytes 172040 | tf_op jit(solution)/shard_map/ppermute | solution.py:285
  6.7 0.0 collective-permute-start.1
  6.7 0.6 %collective-permute-start = (f32[7,2048]{1,0:T(8,128)S(1)}, f32[7,2048]{1,0:T(8,128)S(1)}, u32[]{:S(2)}, u32[]{:S(2)}) collective-permute-start(f32[7,2048]{1,0:T(8,128)S(1)} %pad_maximum_fusion.src_ref), channel_id=1, source_target_pairs={{0,1},{1,0},{2,3},{3,2},{4,5},{5,4},{6,7},{7,6},{8,9},{9,8},{10,11... | collective-permute-start | bytes 172040 | tf_op jit(solution)/shard_map/ppermute | solution.py:285
  7.3 0.0 copy-done
  7.3 5.0 %own_pairs.1.before_ref = f32[96,2048]{1,0:T(8,128)S(1)} custom-call(f32[3,2048]{1,0:T(4,128)S(1)} %copy-done, f32[7,2048]{1,0:T(8,128)S(1)} %pad_maximum_fusion.src_ref), custom_call_target="tpu_custom_call" | custom-call | flops 6442450944 | bytes 2097152 | tf_op jit(solution)/shard_map/own_pairs/pallas_call | solution.py:300
  12.3 0.0 collective-permute-done.2.refs_2_
  12.3 0.0 collective-permute-done.1.refs_1_
  12.3 0.0 collective-permute-done.refs_0_
  12.3 0.0 copy-done.1
  12.4 0.0 copy-done.2
  12.4 0.0 copy-done.3
  12.4 0.0 copy-done.4
  12.4 0.0 copy-done.5
  12.4 19.0 %other_pairs_and_deposit.1 = (f32[3,2048]{1,0:T(4,128)}, f32[4,2048]{1,0:T(4,128)S(1)}, bf16[256,2048]{1,0:T(8,128)(2,1)S(1)}, f32[256,128]{1,0:T(8,128)S(1)}) custom-call(f32[3,2048]{1,0:T(4,128)S(1)} %copy-done, f32[7,2048]{1,0:T(8,128)S(1)} %pad_maximum_fusion.src_ref, f32[96,2048]{1,0:T(8,128)S(1)} %own_pairs.1.before_ref, f32[1,2048]{1,0:T(1,128)S(1)} %bitcast.18, ...), custom_call_target="tpu_custom_call" | custom-call | flops 19327352832 | bytes 2097152 | tf_op jit(solution)/shard_map/other_pairs_and_deposit/pallas_call | solution.py:314
  31.4 0.1 collective-permute-start.3
  31.5 0.7 %deposit_even_slots.1 = f32[256,128]{1,0:T(8,128)S(1)} custom-call(f32[4,2048]{1,0:T(4,128)S(1)} %get-tuple-element.7.value_ref, bf16[256,2048]{1,0:T(8,128)(2,1)S(1)} %get-tuple-element.8.spread_ref, s32[1,2048]{1,0:T(1,128)S(1)} %bitcast.21, s32[1,2048]{1,0:T(1,128)S(1)} %bitcast.23), custom_call_target="tpu_custom_call" | custom-call | flops 1073741824 | bytes 2097152 | tf_op jit(solution)/shard_map/deposit_even_slots/pallas_call | solution.py:345
  32.2 0.6 %collective-permute-done.3 = f32[256,128]{1,0:T(8,128)S(1)} collective-permute-done((f32[256,128]{1,0:T(8,128)S(1)}, f32[256,128]{1,0:T(8,128)S(1)}, u32[]{:S(2)}, u32[]{:S(2)}) %collective-permute-start.3) | collective-permute-done | bytes 131104 | tf_op jit(solution)/shard_map/ppermute | solution.py:359
  32.8 1.7 %collective-permute-start.4 = (f32[2,16,4,128]{3,2,1,0:T(4,128)S(1)}, f32[2,16,4,128]{3,2,1,0:T(4,128)S(1)}, u32[]{:S(2)}, u32[]{:S(2)}) collective-permute-start(f32[2,16,4,128]{3,2,1,0:T(4,128)S(1)} %bitcast.25), channel_id=1, source_target_pairs={{0,8},{4,20},{8,0},{12,28},{16,24},{20,4},{24,16},{28,12},{1,9},{5... | collective-permute-start | bytes 196616 | tf_op jit(solution)/shard_map/ppermute | solution.py:362
  34.5 1.5 %collective-permute-start.5 = (f32[16,4,128]{2,1,0:T(4,128)S(1)}, f32[16,4,128]{2,1,0:T(4,128)S(1)}, u32[]{:S(2)}, u32[]{:S(2)}) collective-permute-start(f32[16,4,128]{2,1,0:T(4,128)S(1)} %bitcast.26), channel_id=1, source_target_pairs={{0,24},{4,28},{8,16},{12,20},{16,8},{20,12},{24,0},{28,4},{1,25},{... | collective-permute-start | bytes 98312 | tf_op jit(solution)/shard_map/ppermute | solution.py:359
  36.0 1.5 %collective-permute-done.4 = f32[2,16,4,128]{3,2,1,0:T(4,128)S(1)} collective-permute-done((f32[2,16,4,128]{3,2,1,0:T(4,128)S(1)}, f32[2,16,4,128]{3,2,1,0:T(4,128)S(1)}, u32[]{:S(2)}, u32[]{:S(2)}) %collective-permute-start.4) | collective-permute-done | bytes 65568 | tf_op jit(solution)/shard_map/ppermute | solution.py:362
  37.5 0.0 collective-permute-start.6
  37.5 1.8 %collective-permute-done.5 = f32[16,4,128]{2,1,0:T(4,128)S(1)} collective-permute-done((f32[16,4,128]{2,1,0:T(4,128)S(1)}, f32[16,4,128]{2,1,0:T(4,128)S(1)}, u32[]{:S(2)}, u32[]{:S(2)}) %collective-permute-start.5) | collective-permute-done | bytes 32800 | tf_op jit(solution)/shard_map/ppermute | solution.py:359
  39.3 0.0 collective-permute-done.6
  39.3 0.6 %fusion.2 = f32[16,4,128]{2,1,0:T(4,128)} fusion(f32[16,4,128]{2,1,0:T(4,128)S(1)} %collective-permute-done.6, f32[16,4,128]{2,1,0:T(4,128)S(1)} %collective-permute-done.5, f32[16,4,128]{2,1,0:T(4,128)S(1)} %bitcast.24, f32[2,16,4,128]{3,2,1,0:T(4,128)S(1)} %collective-permute-done.4), kind=kLoop, calls=%fused_computation.5 | loop fusion | flops 24576 | bytes 163840 | tf_op jit(solution)/shard_map/add | solution.py:364
  (4 shorter events, 0.0 us)
Async XLA Ops:
  0.6 6.7 %copy-start = (f32[3,2048]{1,0:T(4,128)S(1)}, f32[3,2048]{1,0:T(4,128)}, u32[]{:S(2)}) copy-start(f32[3,2048]{1,0:T(4,128)} %pos_ref.3) | copy-start | bytes 73732
  1.5 10.9 %copy-start.1 = (f32[3,2048]{1,0:T(4,128)S(1)}, f32[3,2048]{1,0:T(4,128)}, u32[]{:S(2)}) copy-start(f32[3,2048]{1,0:T(4,128)} %frac_ref.1) | copy-start | bytes 73732
  1.5 10.9 %copy-start.2 = (f32[2048]{0:T(1024)S(1)}, f32[2048]{0:T(1024)}, u32[]{:S(2)}) copy-start(f32[2048]{0:T(1024)} %param.11) | copy-start | bytes 24580
  1.5 10.9 %copy-start.3 = (s32[2048]{0:T(1024)S(1)}, s32[2048]{0:T(1024)}, u32[]{:S(2)}) copy-start(s32[2048]{0:T(1024)} %param.13) | copy-start | bytes 24580
  1.5 10.8 %copy-start.4 = (s32[2048]{0:T(1024)S(1)}, s32[2048]{0:T(1024)}, u32[]{:S(2)}) copy-start(s32[2048]{0:T(1024)} %param.14) | copy-start | bytes 24580
  1.5 10.8 %copy-start.5 = (s32[2048,1]{0,1:T(1,128)S(1)}, s32[2048,1]{0,1:T(1,128)}, u32[]{:S(2)}) copy-start(s32[2048,1]{0,1:T(1,128)} %param.15) | copy-start | bytes 24580
  1.6 10.8 %collective-permute-start.2 = (f32[7,2048]{1,0:T(8,128)S(1)}, f32[7,2048]{1,0:T(8,128)S(1)}, u32[]{:S(2)}, u32[]{:S(2)}) collective-permute-start(f32[7,2048]{1,0:T(8,128)S(1)} %pad_maximum_fusion.src_ref), channel_id=1, source_target_pairs={{0,3},{1,2},{2,1},{3,0},{4,7},{5,6},{6,5},{7,4},{8,11},{9,10},{10,... | collective-permute-start | bytes 172040 | tf_op jit(solution)/shard_map/ppermute | solution.py:285
  6.7 5.7 %collective-permute-start.1 = (f32[7,2048]{1,0:T(8,128)S(1)}, f32[7,2048]{1,0:T(8,128)S(1)}, u32[]{:S(2)}, u32[]{:S(2)}) collective-permute-start(f32[7,2048]{1,0:T(8,128)S(1)} %pad_maximum_fusion.src_ref), channel_id=1, source_target_pairs={{0,2},{1,3},{2,0},{3,1},{4,6},{5,7},{6,4},{7,5},{8,10},{9,11},{10,... | collective-permute-start | bytes 172040 | tf_op jit(solution)/shard_map/ppermute | solution.py:285
  6.7 5.7 %collective-permute-start = (f32[7,2048]{1,0:T(8,128)S(1)}, f32[7,2048]{1,0:T(8,128)S(1)}, u32[]{:S(2)}, u32[]{:S(2)}) collective-permute-start(f32[7,2048]{1,0:T(8,128)S(1)} %pad_maximum_fusion.src_ref), channel_id=1, source_target_pairs={{0,1},{1,0},{2,3},{3,2},{4,5},{5,4},{6,7},{7,6},{8,9},{9,8},{10,11... | collective-permute-start | bytes 172040 | tf_op jit(solution)/shard_map/ppermute | solution.py:285
  31.4 1.4 %collective-permute-start.3 = (f32[256,128]{1,0:T(8,128)S(1)}, f32[256,128]{1,0:T(8,128)S(1)}, u32[]{:S(2)}, u32[]{:S(2)}) collective-permute-start(f32[256,128]{1,0:T(8,128)S(1)} %get-tuple-element.9), channel_id=1, source_target_pairs={{0,4},{4,0},{8,12},{12,8},{16,20},{20,16},{24,28},{28,24},{1,5},{5... | collective-permute-start | bytes 393224 | tf_op jit(solution)/shard_map/ppermute | solution.py:359
  32.8 4.7 %collective-permute-start.4 = (f32[2,16,4,128]{3,2,1,0:T(4,128)S(1)}, f32[2,16,4,128]{3,2,1,0:T(4,128)S(1)}, u32[]{:S(2)}, u32[]{:S(2)}) collective-permute-start(f32[2,16,4,128]{3,2,1,0:T(4,128)S(1)} %bitcast.25), channel_id=1, source_target_pairs={{0,8},{4,20},{8,0},{12,28},{16,24},{20,4},{24,16},{28,12},{1,9},{5... | collective-permute-start | bytes 196616 | tf_op jit(solution)/shard_map/ppermute | solution.py:362
  34.5 4.8 %collective-permute-start.5 = (f32[16,4,128]{2,1,0:T(4,128)S(1)}, f32[16,4,128]{2,1,0:T(4,128)S(1)}, u32[]{:S(2)}, u32[]{:S(2)}) collective-permute-start(f32[16,4,128]{2,1,0:T(4,128)S(1)} %bitcast.26), channel_id=1, source_target_pairs={{0,24},{4,28},{8,16},{12,20},{16,8},{20,12},{24,0},{28,4},{1,25},{... | collective-permute-start | bytes 98312 | tf_op jit(solution)/shard_map/ppermute | solution.py:359
  37.5 1.8 %collective-permute-start.6 = (f32[16,4,128]{2,1,0:T(4,128)S(1)}, f32[16,4,128]{2,1,0:T(4,128)S(1)}, u32[]{:S(2)}, u32[]{:S(2)}) collective-permute-start(f32[16,4,128]{2,1,0:T(4,128)S(1)} %slice_bitcast_fusion), channel_id=1, source_target_pairs={{0,4},{4,0},{8,12},{12,8},{16,20},{20,16},{24,28},{28,24},{1,5},{5... | collective-permute-start | bytes 98312 | tf_op jit(solution)/shard_map/ppermute | solution.py:359

commit v7 on v6

--- a/solution.py
+++ b/solution.py
@@ -92,8 +92,9 @@
             moments, slope_ref[number % slots, :chunk], preferred_element_type=f32
         ) + jnp.dot(moments, slope_ref[number % slots, chunk:], preferred_element_type=f32)
 
-    for number in range(chunks - lag, chunks):
-        slope_ref[number % slots] = jnp.zeros(slope_ref.shape[1:], bf16)
+    if tiles > unroll:
+        for number in range(chunks - lag, chunks):
+            slope_ref[number % slots] = jnp.zeros(slope_ref.shape[1:], bf16)
 
     def step(k, carry):
         for u in range(unroll):
@@ -102,12 +103,15 @@
             for number in range(chunks):
                 if number >= lag:
                     consume(start, number - lag)
-                else:
+                elif u > 0 or tiles > unroll:
                     consume(before, number - lag + chunks)
                 produce(start, number)
         return carry
 
-    lax.fori_loop(0, tiles // unroll, step, 0)
+    if tiles > unroll:
+        lax.fori_loop(0, tiles // unroll, step, 0)
+    else:
+        step(0, 0)
     for number in range(chunks - lag, chunks):
         consume((tiles - 1) * width, number)
 
@@ -120,7 +124,7 @@
     sum_ref[...] = jnp.zeros_like(sum_ref)
     tiles = sum_ref.shape[1] // slope_ref.shape[2]
     add_pair_sums(
-        4, math.gcd(tiles, 8), target_ref, feature_ref, moment_ref, sum_ref, slope_ref
+        8, math.gcd(tiles, 8), target_ref, feature_ref, moment_ref, sum_ref, slope_ref
     )
 
 
@@ -218,18 +222,25 @@
     value_ref[...] = jnp.concatenate(values, axis=0)
     spread_ref[...] = spread_both
     send_ref[...] = deposits(
-        tiles, owners, 1, owner_ref[...], tile_ref[...], value_ref[...], spread_both, pick_ref
+        tiles,
+        owners,
+        slots_of(owners)[0],
+        owner_ref[...],
+        tile_ref[...],
+        value_ref[...],
+        spread_both,
+        pick_ref,
     )
     velocity_copy.wait()
 
 
 def slots_of(owners):
     if owners == 8:
-        return (0, 6, 2, 3), (1, 7, 5, 4)
-    return range(0, owners, 2), range(1, owners, 2)
-
-
-def deposits(tiles, owners, odd, owner, tile, value, spread_both, pick_ref):
+        return (7, 5, 4), (6, 2, 3), (0, 1)
+    return tuple(range(1, owners, 2)), tuple(range(0, owners, 2)), ()
+
+
+def deposits(tiles, owners, slots, owner, tile, value, spread_both, pick_ref):
     count = owner.shape[1]
     me = lax.axis_index("dom")
     slot = owner ^ me
@@ -237,14 +248,14 @@
         traded = (slot & 1) | ((slot & 2) << 1) | ((slot & 4) >> 1)
         slot = jnp.where((me & 1) == 1, traded, slot)
     number = jnp.full(slot.shape, -8, jnp.int32)
-    for place, s in enumerate(slots_of(owners)[odd]):
+    for place, s in enumerate(slots):
         number = jnp.where(slot == s, place * tiles + tile, number)
     node = lax.broadcasted_iota(jnp.int32, (16, count), 0)
     mine = number - (node >> 2)
     value = jnp.concatenate([value] * 4, axis=0)
     value_high = value.astype(bf16).astype(f32)
     value_low = value - value_high
-    total = owners * tiles * 2
+    total = len(slots) * tiles * 4
     for group in range(total // 16):
         mask = mine == 4 * group
         first = 16 * group
@@ -258,9 +269,18 @@
     return both[:total] + both[total:]
 
 
-def keep_kernel(tiles, owners, value_ref, spread_ref, tile_ref, owner_ref, keep_ref, pick_ref):
-    keep_ref[...] = deposits(
-        tiles, owners, 0, owner_ref[...], tile_ref[...], value_ref[...], spread_ref[...], pick_ref
+def deposit_kernel(
+    tiles, owners, slots, value_ref, spread_ref, tile_ref, owner_ref, out_ref, pick_ref
+):
+    out_ref[...] = deposits(
+        tiles,
+        owners,
+        slots,
+        owner_ref[...],
+        tile_ref[...],
+        value_ref[...],
+        spread_ref[...],
+        pick_ref,
     )
 
 
@@ -307,8 +327,9 @@
         cost_estimate=cost(1),
         name="own_pairs",
     )(positions, sources)
-    half = jax.ShapeDtypeStruct((owners * tiles * 2, 128), f32)
-    pick = pltpu.VMEM((owners * tiles * 4, count), bf16)
+    sent, kept, apart = slots_of(owners)
+    rows_for = lambda slots: jax.ShapeDtypeStruct((len(slots) * tiles * 4, 128), f32)
+    pick_for = lambda slots: pltpu.VMEM((len(slots) * tiles * 8, count), bf16)
     tile_row = tile_local[None]
     owner_row = owner_dom.reshape(1, count)
     velocity, value, spread, send = pl.pallas_call(
@@ -317,14 +338,14 @@
             jax.ShapeDtypeStruct((3, count), f32),
             jax.ShapeDtypeStruct((4, count), f32),
             jax.ShapeDtypeStruct((256, count), bf16),
-            half,
+            rows_for(sent),
         ),
         in_specs=vmem_specs(8 + len(others)),
         out_specs=(pl.BlockSpec(memory_space=pl.ANY), *vmem_specs(3)),
         scratch_shapes=scratch(len(others))
         + [
             pltpu.VMEM((96, count), f32),
-            pick,
+            pick_for(sent),
             pltpu.VMEM((3, count), f32),
             pltpu.SemaphoreType.DMA,
         ],
@@ -342,26 +363,29 @@
         owner_row,
         *others,
     )
-    keep = pl.pallas_call(
-        functools.partial(keep_kernel, tiles, owners),
-        out_shape=half,
+    deposit = lambda slots, name: pl.pallas_call(
+        functools.partial(deposit_kernel, tiles, owners, slots),
+        out_shape=rows_for(slots),
         in_specs=vmem_specs(4),
         out_specs=vmem_specs(1)[0],
-        scratch_shapes=[pick],
+        scratch_shapes=[pick_for(slots)],
         compiler_params=params,
         cost_estimate=pl.CostEstimate(
-            flops=owners * tiles * 8 * count * 256 * 2,
+            flops=len(slots) * tiles * 8 * count * 256 * 2,
             bytes_accessed=count * 1024,
             transcendentals=0,
         ),
-        name="deposit_even_slots",
-    )(value, spread, tile_row, owner_row)
+        name=name,
+    )(value, spread, tile_row, owner_row).reshape(len(slots), tiles, 4, 128)
     exchange = lambda x, s: lax.ppermute(x, "dom", [(i, i ^ s) for i in range(owners)])
-    grid = (keep + exchange(send, 1)).reshape(owners // 2, tiles, 4, 128)
+    arrived = exchange(send.reshape(len(sent), tiles, 4, 128), 1)
+    grid = deposit(kept, "deposit_kept_slots") + arrived
     if owners == 8:
-        near = lax.ppermute(grid[2:], "dom", [(i, i ^ (4 if i & 1 else 2)) for i in range(owners)])
-        far = exchange(grid[1], 6)
-        return velocity, grid[0] + near[0] + far + exchange(near[1], 1)
+        far = exchange(grid[0], 6)
+        near = lax.ppermute(grid[1:], "dom", [(i, i ^ (4 if i & 1 else 2)) for i in range(owners)])
+        own = deposit(apart, "deposit_chip_slots")
+        over = exchange(own[1] + near[1], 1)
+        return velocity, own[0] + near[0] + far + over
     got = [exchange(grid[j], 2 * j) for j in range(owners // 2 - 1, 0, -1)]
     return velocity, sum(got, grid[0])
 

time: 40.2 us -> 39.8 us (0.990)
  waiting for transfers between devices: 3.93 us -> 3.47 us
    pallas_call x1 -> x2, Pallas kernels: 0.74 us -> 1.07 us  [on_device(): pl.pallas_call(functools.partial(deposit_kernel, tiles, owners, slots), o...]
  transfers between devices with their start and end apart: 7 -> 7, of which waited for: 3 -> 3; matrix products, arithmetic and copies ran while one was open for 0% -> 0% of each run, Pallas kernels for 14% -> 15%
where the time goes in v7:
time: 39.8 us; the launch traced here: 39.7 us
  Pallas kernels  24.7 us (62%)
  starting transfers between devices  9.08 us (23%)
  waiting for transfers between devices  3.47 us (9%)
  other arithmetic  1.52 us (4%)
  between operations  0.79 us (2%)
    pallas_call x1, Pallas kernels, on_device(): pl.pallas_call(functools.partial(tail_kernel, tiles, owners), out_shape=(...  18.8 us
    ppermute x3, starting transfers between devices, on_device(): lax.ppermute(sources, 'blk', [(i, partner(i, s, blocks)) for i in range(b...  5.76 us
    pallas_call x1, Pallas kernels, on_device(): pl.pallas_call(own_kernel, out_shape=jax.ShapeDtypeStruct((96, count), f3...  4.89 us
    ppermute x3, waiting for transfers between devices, on_device(): lax.ppermute(x, 'dom', [(i, i ^ s) for i in range(owners)])  2.05 us
    ppermute x1, starting transfers between devices, on_device(): lax.ppermute(grid[1:], 'dom', [(i, i ^ (4 if i & 1 else 2)) for i in rang...  1.69 us
    ppermute x3, starting transfers between devices, on_device(): lax.ppermute(x, 'dom', [(i, i ^ s) for i in range(owners)])  1.63 us
    ppermute x1, waiting for transfers between devices, on_device(): lax.ppermute(grid[1:], 'dom', [(i, i ^ (4 if i & 1 else 2)) for i in rang...  1.37 us
    pallas_call x2, Pallas kernels, on_device(): pl.pallas_call(functools.partial(deposit_kernel, tiles, owners, slots), o...  1.07 us
  transfers between devices with their start and end apart: 7, of which 3 were waited for; matrix products, arithmetic and copies ran while one was open for 0% of the time, Pallas kernels for 15%

profile of v7, /device:TPU:0, one launch (start us, length us, event | category | flops | bytes accessed | tf_op | source)
XLA Modules:
  0.0 39.7 jit_solution(11454733584605273613)
XLA Ops:
  0.6 0.0 copy-start
  0.6 0.8 %pad_maximum_fusion.src_ref = f32[7,2048]{1,0:T(8,128)S(1)} fusion(f32[1,2048]{1,0:T(1,128)} %bitcast.35, f32[3,2048]{1,0:T(4,128)} %param.9, f32[3,2048]{1,0:T(4,128)} %pos_ref.3), kind=kLoop, calls=%fused_computation | loop fusion | flops 28672 | bytes 114688 | tf_op jit(solution)/shard_map/concatenate | solution.py:303
  1.5 0.0 copy-start.1
  1.5 0.0 copy-start.2
  1.5 0.0 copy-start.3
  1.5 0.0 copy-start.4
  1.5 0.0 copy-start.5
  1.6 5.1 %collective-permute-start.2 = (f32[7,2048]{1,0:T(8,128)S(1)}, f32[7,2048]{1,0:T(8,128)S(1)}, u32[]{:S(2)}, u32[]{:S(2)}) collective-permute-start(f32[7,2048]{1,0:T(8,128)S(1)} %pad_maximum_fusion.src_ref), channel_id=1, source_target_pairs={{0,3},{1,2},{2,1},{3,0},{4,7},{5,6},{6,5},{7,4},{8,11},{9,10},{10,... | collective-permute-start | bytes 172040 | tf_op jit(solution)/shard_map/ppermute | solution.py:305
  6.7 0.0 collective-permute-start.1
  6.7 0.6 %collective-permute-start = (f32[7,2048]{1,0:T(8,128)S(1)}, f32[7,2048]{1,0:T(8,128)S(1)}, u32[]{:S(2)}, u32[]{:S(2)}) collective-permute-start(f32[7,2048]{1,0:T(8,128)S(1)} %pad_maximum_fusion.src_ref), channel_id=1, source_target_pairs={{0,1},{1,0},{2,3},{3,2},{4,5},{5,4},{6,7},{7,6},{8,9},{9,8},{10,11... | collective-permute-start | bytes 172040 | tf_op jit(solution)/shard_map/ppermute | solution.py:305
  7.3 0.0 copy-done
  7.3 4.9 %own_pairs.1.before_ref = f32[96,2048]{1,0:T(8,128)S(1)} custom-call(f32[3,2048]{1,0:T(4,128)S(1)} %copy-done, f32[7,2048]{1,0:T(8,128)S(1)} %pad_maximum_fusion.src_ref), custom_call_target="tpu_custom_call" | custom-call | flops 6442450944 | bytes 2097152 | tf_op jit(solution)/shard_map/own_pairs/pallas_call | solution.py:320
  12.2 0.0 collective-permute-done.2.refs_2_
  12.2 0.0 collective-permute-done.1.refs_1_
  12.3 0.0 collective-permute-done.refs_0_
  12.3 0.0 copy-done.1
  12.3 0.0 copy-done.2
  12.3 0.0 copy-done.3
  12.3 0.0 copy-done.4
  12.3 0.0 copy-done.5
  12.3 18.8 %other_pairs_and_deposit.1 = (f32[3,2048]{1,0:T(4,128)}, f32[4,2048]{1,0:T(4,128)S(1)}, bf16[256,2048]{1,0:T(8,128)(2,1)S(1)}, f32[192,128]{1,0:T(8,128)S(1)}) custom-call(f32[3,2048]{1,0:T(4,128)S(1)} %copy-done, f32[7,2048]{1,0:T(8,128)S(1)} %pad_maximum_fusion.src_ref, f32[96,2048]{1,0:T(8,128)S(1)} %own_pairs.1.before_ref, f32[1,2048]{1,0:T(1,128)S(1)} %bitcast.31, ...), custom_call_target="tpu_custom_call" | custom-call | flops 19327352832 | bytes 2097152 | tf_op jit(solution)/shard_map/other_pairs_and_deposit/pallas_call | solution.py:335
  31.1 0.1 collective-permute-start.3
  31.2 0.5 %deposit_chip_slots.1 = f32[128,128]{1,0:T(8,128)S(1)} custom-call(f32[4,2048]{1,0:T(4,128)S(1)} %get-tuple-element.7.value_ref, bf16[256,2048]{1,0:T(8,128)(2,1)S(1)} %get-tuple-element.8.spread_ref, s32[1,2048]{1,0:T(1,128)S(1)} %bitcast.25, s32[1,2048]{1,0:T(1,128)S(1)} %bitcast.28), custom_call_target="tpu_custom_call" | custom-call | flops 268435456 | bytes 2097152 | tf_op jit(solution)/shard_map/deposit_chip_slots/pallas_call | solution.py:366
  31.7 0.6 %deposit_kept_slots.1 = f32[192,128]{1,0:T(8,128)S(1)} custom-call(f32[4,2048]{1,0:T(4,128)S(1)} %get-tuple-element.7.value_ref, bf16[256,2048]{1,0:T(8,128)(2,1)S(1)} %get-tuple-element.8.spread_ref, s32[1,2048]{1,0:T(1,128)S(1)} %bitcast.26, s32[1,2048]{1,0:T(1,128)S(1)} %bitcast.29), custom_call_target="tpu_custom_call" | custom-call | flops 402653184 | bytes 2097152 | tf_op jit(solution)/shard_map/deposit_kept_slots/pallas_call | solution.py:366
  32.3 0.2 collective-permute-done.3
  32.5 1.7 %collective-permute-start.4 = (f32[2,16,4,128]{3,2,1,0:T(4,128)S(1)}, f32[2,16,4,128]{3,2,1,0:T(4,128)S(1)}, u32[]{:S(2)}, u32[]{:S(2)}) collective-permute-start(f32[2,16,4,128]{3,2,1,0:T(4,128)S(1)} %slice.27), channel_id=1, source_target_pairs={{0,8},{4,20},{8,0},{12,28},{16,24},{20,4},{24,16},{28,12},{1,9},{5... | collective-permute-start | bytes 196616 | tf_op jit(solution)/shard_map/ppermute | solution.py:385
  34.2 1.5 %collective-permute-start.5 = (f32[16,4,128]{2,1,0:T(4,128)S(1)}, f32[16,4,128]{2,1,0:T(4,128)S(1)}, u32[]{:S(2)}, u32[]{:S(2)}) collective-permute-start(f32[16,4,128]{2,1,0:T(4,128)S(1)} %slice_bitcast_fusion.1), channel_id=1, source_target_pairs={{0,24},{4,28},{8,16},{12,20},{16,8},{20,12},{24,0},{28,4},{1,25},{... | collective-permute-start | bytes 98312 | tf_op jit(solution)/shard_map/ppermute | solution.py:380
  35.7 1.4 %collective-permute-done.4 = f32[2,16,4,128]{3,2,1,0:T(4,128)S(1)} collective-permute-done((f32[2,16,4,128]{3,2,1,0:T(4,128)S(1)}, f32[2,16,4,128]{3,2,1,0:T(4,128)S(1)}, u32[]{:S(2)}, u32[]{:S(2)}) %collective-permute-start.4) | collective-permute-done | bytes 65568 | tf_op jit(solution)/shard_map/ppermute | solution.py:385
  37.1 0.1 collective-permute-start.6
  37.2 1.9 %collective-permute-done.5 = f32[16,4,128]{2,1,0:T(4,128)S(1)} collective-permute-done((f32[16,4,128]{2,1,0:T(4,128)S(1)}, f32[16,4,128]{2,1,0:T(4,128)S(1)}, u32[]{:S(2)}, u32[]{:S(2)}) %collective-permute-start.5) | collective-permute-done | bytes 32800 | tf_op jit(solution)/shard_map/ppermute | solution.py:380
  39.0 0.0 collective-permute-done.6
  39.0 0.6 %fusion.3 = f32[16,4,128]{2,1,0:T(4,128)} fusion(f32[16,4,128]{2,1,0:T(4,128)S(1)} %collective-permute-done.6, f32[16,4,128]{2,1,0:T(4,128)S(1)} %collective-permute-done.5, f32[16,4,128]{2,1,0:T(4,128)S(1)} %bitcast.33, f32[2,16,4,128]{3,2,1,0:T(4,128)S(1)} %collective-permute-done.4), kind=kLoop, calls=%fused_computation.7 | loop fusion | flops 24576 | bytes 163840 | tf_op jit(solution)/shard_map/add | solution.py:388
  (5 shorter events, 0.1 us)
Async XLA Ops:
  0.6 6.7 %copy-start = (f32[3,2048]{1,0:T(4,128)S(1)}, f32[3,2048]{1,0:T(4,128)}, u32[]{:S(2)}) copy-start(f32[3,2048]{1,0:T(4,128)} %pos_ref.3) | copy-start | bytes 73732
  1.5 10.8 %copy-start.1 = (s32[2048]{0:T(1024)S(1)}, s32[2048]{0:T(1024)}, u32[]{:S(2)}) copy-start(s32[2048]{0:T(1024)} %param.14) | copy-start | bytes 24580
  1.5 10.8 %copy-start.2 = (s32[2048,1]{0,1:T(1,128)S(1)}, s32[2048,1]{0,1:T(1,128)}, u32[]{:S(2)}) copy-start(s32[2048,1]{0,1:T(1,128)} %param.15) | copy-start | bytes 24580
  1.5 10.8 %copy-start.3 = (f32[3,2048]{1,0:T(4,128)S(1)}, f32[3,2048]{1,0:T(4,128)}, u32[]{:S(2)}) copy-start(f32[3,2048]{1,0:T(4,128)} %frac_ref.1) | copy-start | bytes 73732
  1.5 10.8 %copy-start.4 = (f32[2048]{0:T(1024)S(1)}, f32[2048]{0:T(1024)}, u32[]{:S(2)}) copy-start(f32[2048]{0:T(1024)} %param.11) | copy-start | bytes 24580
  1.5 10.8 %copy-start.5 = (s32[2048]{0:T(1024)S(1)}, s32[2048]{0:T(1024)}, u32[]{:S(2)}) copy-start(s32[2048]{0:T(1024)} %param.13) | copy-start | bytes 24580
  1.6 10.7 %collective-permute-start.2 = (f32[7,2048]{1,0:T(8,128)S(1)}, f32[7,2048]{1,0:T(8,128)S(1)}, u32[]{:S(2)}, u32[]{:S(2)}) collective-permute-start(f32[7,2048]{1,0:T(8,128)S(1)} %pad_maximum_fusion.src_ref), channel_id=1, source_target_pairs={{0,3},{1,2},{2,1},{3,0},{4,7},{5,6},{6,5},{7,4},{8,11},{9,10},{10,... | collective-permute-start | bytes 172040 | tf_op jit(solution)/shard_map/ppermute | solution.py:305
  6.7 5.6 %collective-permute-start.1 = (f32[7,2048]{1,0:T(8,128)S(1)}, f32[7,2048]{1,0:T(8,128)S(1)}, u32[]{:S(2)}, u32[]{:S(2)}) collective-permute-start(f32[7,2048]{1,0:T(8,128)S(1)} %pad_maximum_fusion.src_ref), channel_id=1, source_target_pairs={{0,2},{1,3},{2,0},{3,1},{4,6},{5,7},{6,4},{7,5},{8,10},{9,11},{10,... | collective-permute-start | bytes 172040 | tf_op jit(solution)/shard_map/ppermute | solution.py:305
  6.7 5.6 %collective-permute-start = (f32[7,2048]{1,0:T(8,128)S(1)}, f32[7,2048]{1,0:T(8,128)S(1)}, u32[]{:S(2)}, u32[]{:S(2)}) collective-permute-start(f32[7,2048]{1,0:T(8,128)S(1)} %pad_maximum_fusion.src_ref), channel_id=1, source_target_pairs={{0,1},{1,0},{2,3},{3,2},{4,5},{5,4},{6,7},{7,6},{8,9},{9,8},{10,11... | collective-permute-start | bytes 172040 | tf_op jit(solution)/shard_map/ppermute | solution.py:305
  31.1 1.4 %collective-permute-start.3 = (f32[3,16,4,128]{3,2,1,0:T(4,128)S(1)}, f32[3,16,4,128]{3,2,1,0:T(4,128)S(1)}, u32[]{:S(2)}, u32[]{:S(2)}) collective-permute-start(f32[3,16,4,128]{3,2,1,0:T(4,128)S(1)} %bitcast.30), channel_id=1, source_target_pairs={{0,4},{4,0},{8,12},{12,8},{16,20},{20,16},{24,28},{28,24},{1,5},{5... | collective-permute-start | bytes 294920 | tf_op jit(solution)/shard_map/ppermute | solution.py:380
  32.5 4.6 %collective-permute-start.4 = (f32[2,16,4,128]{3,2,1,0:T(4,128)S(1)}, f32[2,16,4,128]{3,2,1,0:T(4,128)S(1)}, u32[]{:S(2)}, u32[]{:S(2)}) collective-permute-start(f32[2,16,4,128]{3,2,1,0:T(4,128)S(1)} %slice.27), channel_id=1, source_target_pairs={{0,8},{4,20},{8,0},{12,28},{16,24},{20,4},{24,16},{28,12},{1,9},{5... | collective-permute-start | bytes 196616 | tf_op jit(solution)/shard_map/ppermute | solution.py:385
  34.2 4.8 %collective-permute-start.5 = (f32[16,4,128]{2,1,0:T(4,128)S(1)}, f32[16,4,128]{2,1,0:T(4,128)S(1)}, u32[]{:S(2)}, u32[]{:S(2)}) collective-permute-start(f32[16,4,128]{2,1,0:T(4,128)S(1)} %slice_bitcast_fusion.1), channel_id=1, source_target_pairs={{0,24},{4,28},{8,16},{12,20},{16,8},{20,12},{24,0},{28,4},{1,25},{... | collective-permute-start | bytes 98312 | tf_op jit(solution)/shard_map/ppermute | solution.py:380
  37.1 1.9 %collective-permute-start.6 = (f32[16,4,128]{2,1,0:T(4,128)S(1)}, f32[16,4,128]{2,1,0:T(4,128)S(1)}, u32[]{:S(2)}, u32[]{:S(2)}) collective-permute-start(f32[16,4,128]{2,1,0:T(4,128)S(1)} %fusion), channel_id=1, source_target_pairs={{0,4},{4,0},{8,12},{12,8},{16,20},{20,16},{24,28},{28,24},{1,5},{5... | collective-permute-start | bytes 98312 | tf_op jit(solution)/shard_map/ppermute | solution.py:380

commit v8 on v7

--- a/solution.py
+++ b/solution.py
@@ -48,8 +48,16 @@
     return jnp.concatenate([high, middle, high, low, high, middle], axis=0).astype(bf16)
 
 
-def source_features(src):
-    points = rows_of(src, 0, 3)
+def centered(pos, center):
+    return rows_of(pos - center, 0, 3)
+
+
+def center_of(pos):
+    return jnp.mean(pos, axis=1, keepdims=True)
+
+
+def source_features(src, center):
+    points = centered(src[0:3], center)
     vortex = rows_of(src, 3, 3)
     radius = src[6:7]
     offset = square_sum(points) + radius * radius
@@ -119,8 +127,9 @@
 def own_kernel(
     pos_ref, src_ref, sum_ref, target_ref, feature_ref, moment_ref, slope_ref
 ):
-    target_ref[...] = target_features(rows_of(pos_ref[...], 0, 3))
-    feature_ref[...], moment_ref[...] = source_features(src_ref[...])
+    center = center_of(pos_ref[...])
+    target_ref[...] = target_features(centered(pos_ref[...], center))
+    feature_ref[...], moment_ref[...] = source_features(src_ref[...], center)
     sum_ref[...] = jnp.zeros_like(sum_ref)
     tiles = sum_ref.shape[1] // slope_ref.shape[2]
     add_pair_sums(
@@ -176,11 +185,12 @@
     velocity_ref, value_ref, spread_ref, send_ref, *refs = refs[-12:]
     target_ref, feature_ref, moment_ref, slope_ref, sum_ref, pick_ref, ready_ref, copied = refs
     count = src_ref.shape[1]
-    points = rows_of(pos_ref[...], 0, 3)
+    center = center_of(pos_ref[...])
+    points = centered(pos_ref[...], center)
     target_ref[...] = target_features(points)
     for k, other_ref in enumerate(other_refs):
         place = slice(k * count, (k + 1) * count)
-        feature_ref[place], moment_ref[:, place] = source_features(other_ref[...])
+        feature_ref[place], moment_ref[:, place] = source_features(other_ref[...], center)
     sum_ref[...] = before_ref[...]
     add_pair_sums(
         8,

time: 39.8 us -> 40.3 us (1.013)
  Pallas kernels: 24.7 us -> 25.2 us
  transfers between devices with their start and end apart: 7 -> 7, of which waited for: 3 -> 3; matrix products, arithmetic and copies ran while one was open for 0% -> 0% of each run, Pallas kernels for 15% -> 16%
where the time goes in v8:
time: 40.3 us; the launch traced here: 40.1 us
  Pallas kernels  25.2 us (63%)
  starting transfers between devices  9.07 us (23%)
  waiting for transfers between devices  3.44 us (9%)
  other arithmetic  1.52 us (4%)
  between operations  0.82 us (2%)
    pallas_call x1, Pallas kernels, on_device(): pl.pallas_call(functools.partial(tail_kernel, tiles, owners), out_shape=(...  18.9 us
    ppermute x3, starting transfers between devices, on_device(): lax.ppermute(sources, 'blk', [(i, partner(i, s, blocks)) for i in range(b...  5.76 us
    pallas_call x1, Pallas kernels, on_device(): pl.pallas_call(own_kernel, out_shape=jax.ShapeDtypeStruct((96, count), f3...  5.2 us
    ppermute x3, waiting for transfers between devices, on_device(): lax.ppermute(x, 'dom', [(i, i ^ s) for i in range(owners)])  2.05 us
    ppermute x1, starting transfers between devices, on_device(): lax.ppermute(grid[1:], 'dom', [(i, i ^ (4 if i & 1 else 2)) for i in rang...  1.7 us
    ppermute x3, starting transfers between devices, on_device(): lax.ppermute(x, 'dom', [(i, i ^ s) for i in range(owners)])  1.62 us
    ppermute x1, waiting for transfers between devices, on_device(): lax.ppermute(grid[1:], 'dom', [(i, i ^ (4 if i & 1 else 2)) for i in rang...  1.38 us
    pallas_call x2, Pallas kernels, on_device(): pl.pallas_call(functools.partial(deposit_kernel, tiles, owners, slots), o...  1.08 us
  transfers between devices with their start and end apart: 7, of which 3 were waited for; matrix products, arithmetic and copies ran while one was open for 0% of the time, Pallas kernels for 16%

profile of v8, /device:TPU:0, one launch (start us, length us, event | category | flops | bytes accessed | tf_op | source)
XLA Modules:
  0.0 40.1 jit_solution(13575441028683148229)
XLA Ops:
  0.6 0.0 copy-start
  0.6 0.8 %pad_maximum_fusion.src_ref = f32[7,2048]{1,0:T(8,128)S(1)} fusion(f32[1,2048]{1,0:T(1,128)} %bitcast.35, f32[3,2048]{1,0:T(4,128)} %param.9, f32[3,2048]{1,0:T(4,128)} %pos_ref.3), kind=kLoop, calls=%fused_computation | loop fusion | flops 28672 | bytes 114688 | tf_op jit(solution)/shard_map/concatenate | solution.py:313
  1.5 0.0 copy-start.1
  1.5 0.0 copy-start.2
  1.5 0.0 copy-start.3
  1.5 0.0 copy-start.4
  1.5 0.0 copy-start.5
  1.6 5.1 %collective-permute-start.2 = (f32[7,2048]{1,0:T(8,128)S(1)}, f32[7,2048]{1,0:T(8,128)S(1)}, u32[]{:S(2)}, u32[]{:S(2)}) collective-permute-start(f32[7,2048]{1,0:T(8,128)S(1)} %pad_maximum_fusion.src_ref), channel_id=1, source_target_pairs={{0,3},{1,2},{2,1},{3,0},{4,7},{5,6},{6,5},{7,4},{8,11},{9,10},{10,... | collective-permute-start | bytes 172040 | tf_op jit(solution)/shard_map/ppermute | solution.py:315
  6.7 0.0 collective-permute-start.1
  6.7 0.6 %collective-permute-start = (f32[7,2048]{1,0:T(8,128)S(1)}, f32[7,2048]{1,0:T(8,128)S(1)}, u32[]{:S(2)}, u32[]{:S(2)}) collective-permute-start(f32[7,2048]{1,0:T(8,128)S(1)} %pad_maximum_fusion.src_ref), channel_id=1, source_target_pairs={{0,1},{1,0},{2,3},{3,2},{4,5},{5,4},{6,7},{7,6},{8,9},{9,8},{10,11... | collective-permute-start | bytes 172040 | tf_op jit(solution)/shard_map/ppermute | solution.py:315
  7.3 0.0 copy-done
  7.3 5.2 %own_pairs.1.before_ref = f32[96,2048]{1,0:T(8,128)S(1)} custom-call(f32[3,2048]{1,0:T(4,128)S(1)} %copy-done, f32[7,2048]{1,0:T(8,128)S(1)} %pad_maximum_fusion.src_ref), custom_call_target="tpu_custom_call" | custom-call | flops 6442450944 | bytes 2097152 | tf_op jit(solution)/shard_map/own_pairs/pallas_call | solution.py:330
  12.5 0.0 collective-permute-done.2.refs_2_
  12.5 0.0 collective-permute-done.1.refs_1_
  12.5 0.0 collective-permute-done.refs_0_
  12.6 0.0 copy-done.1
  12.6 0.0 copy-done.2
  12.6 0.0 copy-done.3
  12.6 0.0 copy-done.4
  12.6 0.0 copy-done.5
  12.6 18.9 %other_pairs_and_deposit.1 = (f32[3,2048]{1,0:T(4,128)}, f32[4,2048]{1,0:T(4,128)S(1)}, bf16[256,2048]{1,0:T(8,128)(2,1)S(1)}, f32[192,128]{1,0:T(8,128)S(1)}) custom-call(f32[3,2048]{1,0:T(4,128)S(1)} %copy-done, f32[7,2048]{1,0:T(8,128)S(1)} %pad_maximum_fusion.src_ref, f32[96,2048]{1,0:T(8,128)S(1)} %own_pairs.1.before_ref, f32[1,2048]{1,0:T(1,128)S(1)} %bitcast.31, ...), custom_call_target="tpu_custom_call" | custom-call | flops 19327352832 | bytes 2097152 | tf_op jit(solution)/shard_map/other_pairs_and_deposit/pallas_call | solution.py:345
  31.6 0.1 collective-permute-start.3
  31.6 0.5 %deposit_chip_slots.1 = f32[128,128]{1,0:T(8,128)S(1)} custom-call(f32[4,2048]{1,0:T(4,128)S(1)} %get-tuple-element.7.value_ref, bf16[256,2048]{1,0:T(8,128)(2,1)S(1)} %get-tuple-element.8.spread_ref, s32[1,2048]{1,0:T(1,128)S(1)} %bitcast.25, s32[1,2048]{1,0:T(1,128)S(1)} %bitcast.28), custom_call_target="tpu_custom_call" | custom-call | flops 268435456 | bytes 2097152 | tf_op jit(solution)/shard_map/deposit_chip_slots/pallas_call | solution.py:376
  32.1 0.6 %deposit_kept_slots.1 = f32[192,128]{1,0:T(8,128)S(1)} custom-call(f32[4,2048]{1,0:T(4,128)S(1)} %get-tuple-element.7.value_ref, bf16[256,2048]{1,0:T(8,128)(2,1)S(1)} %get-tuple-element.8.spread_ref, s32[1,2048]{1,0:T(1,128)S(1)} %bitcast.26, s32[1,2048]{1,0:T(1,128)S(1)} %bitcast.29), custom_call_target="tpu_custom_call" | custom-call | flops 402653184 | bytes 2097152 | tf_op jit(solution)/shard_map/deposit_kept_slots/pallas_call | solution.py:376
  32.7 0.2 collective-permute-done.3
  33.0 1.7 %collective-permute-start.4 = (f32[2,16,4,128]{3,2,1,0:T(4,128)S(1)}, f32[2,16,4,128]{3,2,1,0:T(4,128)S(1)}, u32[]{:S(2)}, u32[]{:S(2)}) collective-permute-start(f32[2,16,4,128]{3,2,1,0:T(4,128)S(1)} %slice.27), channel_id=1, source_target_pairs={{0,8},{4,20},{8,0},{12,28},{16,24},{20,4},{24,16},{28,12},{1,9},{5... | collective-permute-start | bytes 196616 | tf_op jit(solution)/shard_map/ppermute | solution.py:395
  34.7 1.5 %collective-permute-start.5 = (f32[16,4,128]{2,1,0:T(4,128)S(1)}, f32[16,4,128]{2,1,0:T(4,128)S(1)}, u32[]{:S(2)}, u32[]{:S(2)}) collective-permute-start(f32[16,4,128]{2,1,0:T(4,128)S(1)} %slice_bitcast_fusion.1), channel_id=1, source_target_pairs={{0,24},{4,28},{8,16},{12,20},{16,8},{20,12},{24,0},{28,4},{1,25},{... | collective-permute-start | bytes 98312 | tf_op jit(solution)/shard_map/ppermute | solution.py:390
  36.1 1.4 %collective-permute-done.4 = f32[2,16,4,128]{3,2,1,0:T(4,128)S(1)} collective-permute-done((f32[2,16,4,128]{3,2,1,0:T(4,128)S(1)}, f32[2,16,4,128]{3,2,1,0:T(4,128)S(1)}, u32[]{:S(2)}, u32[]{:S(2)}) %collective-permute-start.4) | collective-permute-done | bytes 65568 | tf_op jit(solution)/shard_map/ppermute | solution.py:395
  37.5 0.1 collective-permute-start.6
  37.6 1.9 %collective-permute-done.5 = f32[16,4,128]{2,1,0:T(4,128)S(1)} collective-permute-done((f32[16,4,128]{2,1,0:T(4,128)S(1)}, f32[16,4,128]{2,1,0:T(4,128)S(1)}, u32[]{:S(2)}, u32[]{:S(2)}) %collective-permute-start.5) | collective-permute-done | bytes 32800 | tf_op jit(solution)/shard_map/ppermute | solution.py:390
  39.5 0.0 collective-permute-done.6
  39.5 0.6 %fusion.3 = f32[16,4,128]{2,1,0:T(4,128)} fusion(f32[16,4,128]{2,1,0:T(4,128)S(1)} %collective-permute-done.6, f32[16,4,128]{2,1,0:T(4,128)S(1)} %collective-permute-done.5, f32[16,4,128]{2,1,0:T(4,128)S(1)} %bitcast.33, f32[2,16,4,128]{3,2,1,0:T(4,128)S(1)} %collective-permute-done.4), kind=kLoop, calls=%fused_computation.7 | loop fusion | flops 24576 | bytes 163840 | tf_op jit(solution)/shard_map/add | solution.py:398
  (5 shorter events, 0.1 us)
Async XLA Ops:
  0.6 6.7 %copy-start = (f32[3,2048]{1,0:T(4,128)S(1)}, f32[3,2048]{1,0:T(4,128)}, u32[]{:S(2)}) copy-start(f32[3,2048]{1,0:T(4,128)} %pos_ref.3) | copy-start | bytes 73732
  1.5 11.1 %copy-start.1 = (s32[2048]{0:T(1024)S(1)}, s32[2048]{0:T(1024)}, u32[]{:S(2)}) copy-start(s32[2048]{0:T(1024)} %param.14) | copy-start | bytes 24580
  1.5 11.1 %copy-start.2 = (s32[2048,1]{0,1:T(1,128)S(1)}, s32[2048,1]{0,1:T(1,128)}, u32[]{:S(2)}) copy-start(s32[2048,1]{0,1:T(1,128)} %param.15) | copy-start | bytes 24580
  1.5 11.1 %copy-start.3 = (f32[3,2048]{1,0:T(4,128)S(1)}, f32[3,2048]{1,0:T(4,128)}, u32[]{:S(2)}) copy-start(f32[3,2048]{1,0:T(4,128)} %frac_ref.1) | copy-start | bytes 73732
  1.5 11.1 %copy-start.4 = (f32[2048]{0:T(1024)S(1)}, f32[2048]{0:T(1024)}, u32[]{:S(2)}) copy-start(f32[2048]{0:T(1024)} %param.11) | copy-start | bytes 24580
  1.5 11.1 %copy-start.5 = (s32[2048]{0:T(1024)S(1)}, s32[2048]{0:T(1024)}, u32[]{:S(2)}) copy-start(s32[2048]{0:T(1024)} %param.13) | copy-start | bytes 24580
  1.6 11.0 %collective-permute-start.2 = (f32[7,2048]{1,0:T(8,128)S(1)}, f32[7,2048]{1,0:T(8,128)S(1)}, u32[]{:S(2)}, u32[]{:S(2)}) collective-permute-start(f32[7,2048]{1,0:T(8,128)S(1)} %pad_maximum_fusion.src_ref), channel_id=1, source_target_pairs={{0,3},{1,2},{2,1},{3,0},{4,7},{5,6},{6,5},{7,4},{8,11},{9,10},{10,... | collective-permute-start | bytes 172040 | tf_op jit(solution)/shard_map/ppermute | solution.py:315
  6.7 5.9 %collective-permute-start.1 = (f32[7,2048]{1,0:T(8,128)S(1)}, f32[7,2048]{1,0:T(8,128)S(1)}, u32[]{:S(2)}, u32[]{:S(2)}) collective-permute-start(f32[7,2048]{1,0:T(8,128)S(1)} %pad_maximum_fusion.src_ref), channel_id=1, source_target_pairs={{0,2},{1,3},{2,0},{3,1},{4,6},{5,7},{6,4},{7,5},{8,10},{9,11},{10,... | collective-permute-start | bytes 172040 | tf_op jit(solution)/shard_map/ppermute | solution.py:315
  6.7 5.9 %collective-permute-start = (f32[7,2048]{1,0:T(8,128)S(1)}, f32[7,2048]{1,0:T(8,128)S(1)}, u32[]{:S(2)}, u32[]{:S(2)}) collective-permute-start(f32[7,2048]{1,0:T(8,128)S(1)} %pad_maximum_fusion.src_ref), channel_id=1, source_target_pairs={{0,1},{1,0},{2,3},{3,2},{4,5},{5,4},{6,7},{7,6},{8,9},{9,8},{10,11... | collective-permute-start | bytes 172040 | tf_op jit(solution)/shard_map/ppermute | solution.py:315
  31.6 1.4 %collective-permute-start.3 = (f32[3,16,4,128]{3,2,1,0:T(4,128)S(1)}, f32[3,16,4,128]{3,2,1,0:T(4,128)S(1)}, u32[]{:S(2)}, u32[]{:S(2)}) collective-permute-start(f32[3,16,4,128]{3,2,1,0:T(4,128)S(1)} %bitcast.30), channel_id=1, source_target_pairs={{0,4},{4,0},{8,12},{12,8},{16,20},{20,16},{24,28},{28,24},{1,5},{5... | collective-permute-start | bytes 294920 | tf_op jit(solution)/shard_map/ppermute | solution.py:390
  33.0 4.6 %collective-permute-start.4 = (f32[2,16,4,128]{3,2,1,0:T(4,128)S(1)}, f32[2,16,4,128]{3,2,1,0:T(4,128)S(1)}, u32[]{:S(2)}, u32[]{:S(2)}) collective-permute-start(f32[2,16,4,128]{3,2,1,0:T(4,128)S(1)} %slice.27), channel_id=1, source_target_pairs={{0,8},{4,20},{8,0},{12,28},{16,24},{20,4},{24,16},{28,12},{1,9},{5... | collective-permute-start | bytes 196616 | tf_op jit(solution)/shard_map/ppermute | solution.py:395
  34.7 4.8 %collective-permute-start.5 = (f32[16,4,128]{2,1,0:T(4,128)S(1)}, f32[16,4,128]{2,1,0:T(4,128)S(1)}, u32[]{:S(2)}, u32[]{:S(2)}) collective-permute-start(f32[16,4,128]{2,1,0:T(4,128)S(1)} %slice_bitcast_fusion.1), channel_id=1, source_target_pairs={{0,24},{4,28},{8,16},{12,20},{16,8},{20,12},{24,0},{28,4},{1,25},{... | collective-permute-start | bytes 98312 | tf_op jit(solution)/shard_map/ppermute | solution.py:390
  37.5 1.9 %collective-permute-start.6 = (f32[16,4,128]{2,1,0:T(4,128)S(1)}, f32[16,4,128]{2,1,0:T(4,128)S(1)}, u32[]{:S(2)}, u32[]{:S(2)}) collective-permute-start(f32[16,4,128]{2,1,0:T(4,128)S(1)} %fusion), channel_id=1, source_target_pairs={{0,4},{4,0},{8,12},{12,8},{16,20},{20,16},{24,28},{28,24},{1,5},{5... | collective-permute-start | bytes 98312 | tf_op jit(solution)/shard_map/ppermute | solution.py:390
